TPU v7x, 1024 devices: a whole 4x8x16 slice. The times are simulated.
1024 devices in a mesh: row: 64 (over z, y_lo, core), col: 16 (over x, y_hi).
Axes of the slice: x: 4, y: 8 (y_hi: 4, y_lo: 2; y = y_hi * 2 + y_lo), z: 16, core: 2. Of those that a mesh axis runs over, the one named last changes fastest.
Arguments:
- adjacency: bfloat16 [32768, 16384], P('row', 'col'), may hold values from -0.0625 to 0.0625
- block_mask: int32 [128, 64], P('row', 'col'), may hold values 0 or 1
- features: bfloat16 [16384, 512], P(('col', 'row')), may hold values from -6 to 6
- weight: bfloat16 [512, 512], replicated, may hold values from -0.25 to 0.25
- upstream: bfloat16 [32768, 512], P(('row', 'col')), may hold values from -18 to 18
Outputs:
- output: bfloat16 [32768, 512], P(('row', 'col'))
- feature_grad: float32 [16384, 512], P(('col', 'row'))
- weight_grad: float32 [512, 512], replicated
All inputs are finite; a program needn't handle non-finite values. No bound on the sum of `block_mask` on one device may be relied on, other than what follows from the above.
Results may differ from a plain program's by a relative error of at most 0.011.
Values may be sent and summed in bfloat16 or wider, within the bound.
No kernel may reach another device: no remote copies, remote signals or barrier semaphores. Data moves between devices by JAX's collectives and lax.ppermute only.
A program may use at most 32 MiB of HBM per device.

v0:
```python
import jax
import jax.numpy as jnp
from jax import lax
from jax.sharding import PartitionSpec as P

TILE = 256


def shards(adjacency, block_mask, features, weight, upstream):
    masked = adjacency * jnp.repeat(jnp.repeat(block_mask, TILE, 0), TILE, 1).astype(jnp.bfloat16)
    panel_rows = adjacency.shape[0]
    columns = masked
    partial_agg = jnp.dot(
        columns,
        lax.all_gather(features, "row", axis=0, tiled=True),
        preferred_element_type=jnp.float32,
    )
    aggregate = lax.psum_scatter(partial_agg, "col", scatter_dimension=0, tiled=True).astype(
        jnp.bfloat16
    )
    pre = jnp.dot(aggregate, weight, preferred_element_type=jnp.float32)
    output = jax.nn.silu(pre).astype(jnp.bfloat16)
    sigma = jax.nn.sigmoid(pre)
    dpre = (upstream.astype(jnp.float32) * sigma * (1.0 + pre * (1.0 - sigma))).astype(jnp.bfloat16)
    grad_in = jnp.dot(dpre, weight.T, preferred_element_type=jnp.float32).astype(jnp.bfloat16)
    grad_whole = lax.all_gather(grad_in, "col", axis=0, tiled=True)
    columns = masked
    feature_grad = lax.psum_scatter(
        jnp.dot(columns.T, grad_whole, preferred_element_type=jnp.float32),
        "row",
        scatter_dimension=0,
        tiled=True,
    )
    local_terms = jnp.dot(aggregate.T, dpre, preferred_element_type=jnp.float32)
    summed = lax.psum(local_terms, ("row", "col"))
    weight_grad = summed * (panel_rows * lax.axis_size("row")) ** (-0.5)
    return (output, feature_grad, weight_grad)


def solution(mesh):
    return jax.shard_map(
        shards,
        mesh=mesh,
        in_specs=(
            P("row", "col"),
            P("row", "col"),
            P(("col", "row"), None),
            P(),
            P(("row", "col"), None),
        ),
        out_specs=(P(("row", "col"), None), P(("col", "row"), None), P()),
        check_vma=False,
    )
```

profile of v0, /device:TPU:1, one launch (start us, length us, event | category | flops | bytes accessed | tf_op | source)
XLA Modules:
  0.0 973.5 jit_solution(9885739958293524273)
XLA Ops:
  7.2 0.0 copy-start
  7.2 0.0 all-gather.2.cloned.1.call-start
  7.2 0.7 all-gather.2.cloned.1.call-update
  7.9 0.0 reduce-scatter.3.cloned.1.call-start
  8.0 0.7 convert_element_type.26
  8.7 0.7 broadcast_in_dim.7
  9.4 0.2 copy.8
  9.6 0.4 mul.22
  10.0 134.0 %all-gather.2.cloned.1.call-done = bf16[1024,512]{1,0:T(8,128)(2,1)} async-done(((bf16[16,512]{1,0:T(8,128)(2,1)}), bf16[1024,512]{1,0:T(8,128)(2,1)}) %all-gather.2.cloned.1.call-update) | async-done | bytes 1048592 | tf_op jit(solution)/shard_map/all_gather | solution.py:15
  144.1 2.9 fusion.4
  147.0 0.0 reduce-scatter.3.cloned.1.call-update
  147.0 0.0 all-reduce.2.cloned.1.call-start
  147.0 99.2 %reduce-scatter.3.cloned.1.call-done = f32[32,512]{1,0:T(8,128)} async-done(((f32[512,512]{1,0:T(8,128)}), f32[32,512]{1,0:T(8,128)}) %reduce-scatter.3.cloned.1.call-update) | async-done | bytes 65552 | tf_op jit(solution)/shard_map/reduce_scatter | solution.py:18
  246.3 1.7 multiply_convert_fusion.1
  247.9 0.2 convolution_convert_fusion
  248.2 2.2 fusion
  250.3 0.0 all-reduce.2.cloned.1.call-update
  250.4 0.0 reduce-scatter.5.cloned.1.call-start
  250.4 38.7 %all_gather.7 = bf16[512,512]{1,0:T(8,128)(2,1)S(1)} all-gather(bf16[32,512]{1,0:T(8,128)(2,1)S(1)} %convolution_convert_fusion), channel_id=1, replica_groups=mesh['row'=64,'col'=16] {'col'}, dimensions={0}, use_global_device_ids=true | all-gather | bytes 557056 | tf_op jit(solution)/shard_map/all_gather | solution.py:26
  289.1 2.1 fusion.5
  291.2 0.0 reduce-scatter.5.cloned.1.call-update
  291.2 445.5 %all-reduce.2.cloned.1.call-done = f32[512,512]{1,0:T(8,128)} async-done(((f32[512,512]{1,0:T(8,128)}), f32[512,512]{1,0:T(8,128)}) %all-reduce.2.cloned.1.call-update) | async-done | bytes 1048592 | tf_op jit(solution)/shard_map/psum | solution.py:35
  736.7 2.3 broadcast_multiply_fusion
  739.0 227.9 %reduce-scatter.5.cloned.1.call-done = f32[16,512]{1,0:T(8,128)} async-done(((f32[1024,512]{1,0:T(8,128)}), f32[16,512]{1,0:T(8,128)}) %reduce-scatter.5.cloned.1.call-update) | async-done | bytes 32784 | tf_op jit(solution)/shard_map/reduce_scatter | solution.py:28
  (6 shorter events, 0.0 us)
Async XLA Ops:
  7.2 239.1 %copy-start = (bf16[512,512]{1,0:T(8,128)(2,1)S(1)}, bf16[512,512]{1,0:T(8,128)(2,1)}, u32[]{:S(2)}) copy-start(bf16[512,512]{1,0:T(8,128)(2,1)} %param.8) | copy-start | bytes 1572868
  7.2 2.4 copy-start.1
  7.2 136.9 %all-gather.2.cloned.1.call-start = ((), (), s32[]{:S(2)}) async-start(), calls=%async_computation.2 | async-start | bytes 1064960 | tf_op jit(solution)/shard_map/all_gather | solution.py:15
  7.9 238.3 %reduce-scatter.3.cloned.1.call-start = ((), (), s32[]{:S(2)}) async-start(), calls=%async_computation.3 | async-start | bytes 1114112 | tf_op jit(solution)/shard_map/reduce_scatter | solution.py:18
  10.0 237.9 %copy-start.2 = (bf16[32,512]{1,0:T(8,128)(2,1)S(1)}, bf16[32,512]{1,0:T(8,128)(2,1)}, u32[]{:S(2)}) copy-start(bf16[32,512]{1,0:T(8,128)(2,1)} %param.9) | copy-start | bytes 98308
  147.0 589.7 %all-reduce.2.cloned.1.call-start = ((), (), s32[]{:S(2)}) async-start(), calls=%async_computation.5 | async-start | bytes 2097152 | tf_op jit(solution)/shard_map/psum | solution.py:35
  250.4 716.6 %reduce-scatter.5.cloned.1.call-start = ((), (), s32[]{:S(2)}) async-start(), calls=%async_computation.4 | async-start | bytes 2129920 | tf_op jit(solution)/shard_map/reduce_scatter | solution.py:28
Sparse Core Ops, SparseCore 0:
  10.8 133.2 all-gather.1
  149.9 96.3 reduce-scatter.2
  253.2 483.4 all-reduce.1
  740.9 226.0 reduce-scatter.4
where the time goes:
time: 977 us; the launch traced here: 973 us
  waiting for transfers between devices  907 us (93%)
  blocking collectives  38.7 us (4%)
  between operations  13.8 us (1%)
    psum x1, waiting for transfers between devices, shards(): summed = lax.psum(local_terms, ('row', 'col'))  446 us
    reduce_scatter x1, waiting for transfers between devices, shards(): lax.psum_scatter(jnp.dot(columns.T, grad_whole, preferred_element_type=jn...  228 us
    all_gather x1, waiting for transfers between devices, shards(): lax.all_gather(features, 'row', axis=0, tiled=True)  134 us
    reduce_scatter x1, waiting for transfers between devices, shards(): lax.psum_scatter(partial_agg, 'col', scatter_dimension=0, tiled=True)  99.2 us
    all_gather x1, blocking collectives, shards(): grad_whole = lax.all_gather(grad_in, 'col', axis=0, tiled=True)  38.7 us
  transfers between devices with their start and end apart: 4, of which 4 were waited for; matrix products, arithmetic and copies ran while one was open for 1% of the time, Pallas kernels for 0%

commit v1 on v0

v1 whole, which is shorter than its diff:
```python
import jax
import jax.numpy as jnp
from jax import lax
from jax.sharding import Mesh, PartitionSpec as P

TILE = 256
F32 = jnp.float32
BF16 = jnp.bfloat16


def exchange(chunks, axis):
    return lax.all_to_all(chunks, axis, split_axis=0, concat_axis=0, tiled=True)


def gather(block, axis):
    n = lax.axis_size(axis)
    return exchange(jnp.broadcast_to(block[None], (n,) + block.shape), axis)


def shards(adjacency, block_mask, features, weight, upstream):
    rows, cols = adjacency.shape
    width = features.shape[1]
    nz, nyl, ncore, nx, nyh = (lax.axis_size(a) for a in ("z", "yl", "core", "x", "yh"))
    n_row, n_col = nz * nyl * ncore, nx * nyh
    masked = adjacency * jnp.repeat(jnp.repeat(block_mask, TILE, 0), TILE, 1).astype(BF16)

    own = features.shape[0]
    by_z = gather(features, "z")
    by_yl = gather(by_z, "yl")
    by_core = gather(by_yl, "core")
    panel = by_core.transpose(2, 1, 0, 3, 4).reshape(cols, width)

    partial = jnp.dot(masked, panel, preferred_element_type=F32).astype(BF16)
    over_x = exchange(partial.reshape(nx, rows // nx, width), "x")
    summed_x = over_x.astype(F32).sum(0).astype(BF16)
    over_yh = exchange(summed_x.reshape(nyh, rows // n_col, width), "yh")
    aggregate = over_yh.astype(F32).sum(0).astype(BF16)

    pre = jnp.dot(aggregate, weight, preferred_element_type=F32)
    sigma = jax.nn.sigmoid(pre)
    output = (pre * sigma).astype(BF16)
    dpre = (upstream.astype(F32) * sigma * (1.0 + pre * (1.0 - sigma))).astype(BF16)

    both = jnp.concatenate([aggregate, dpre], axis=1)
    both = gather(gather(both, "yh").reshape(rows // nx, 2 * width), "x").reshape(rows, 2 * width)
    agg_all, dpre_all = both[:, :width], both[:, width:]
    grad_in = lax.dot_general(
        dpre_all, weight, (((1,), (1,)), ((), ())), preferred_element_type=F32
    ).astype(BF16)
    partial_fg = lax.dot_general(masked, grad_in, (((0,), (0,)), ((), ())), preferred_element_type=F32)
    slab = width // nx
    agg_slab = lax.dynamic_slice_in_dim(agg_all, lax.axis_index("x") * slab, slab, axis=1)
    partial_w = lax.dot_general(agg_slab, dpre_all, (((0,), (0,)), ((), ())), preferred_element_type=F32)

    chunk = cols // n_row
    fg = partial_fg.astype(BF16).reshape(nz, nyl, ncore, chunk, width).transpose(2, 1, 0, 3, 4)
    w = partial_w.astype(BF16)

    def fold(fg, w, axis, n):
        feet = fg.reshape(n, -1, width)
        send = jnp.concatenate([feet, jnp.broadcast_to(w[None], (n,) + w.shape)], axis=1)
        got = exchange(send, axis).astype(F32).sum(0).astype(BF16)
        return got[: feet.shape[1]], got[feet.shape[1] :]

    fg, w = fold(fg, w, "core", ncore)
    fg, w = fold(fg, w, "yl", nyl)
    send = jnp.concatenate([fg.reshape(nz, chunk, width), w.reshape(nz, slab // nz, width)], axis=1)
    got = exchange(send, "z").astype(F32).sum(0)
    feature_grad = got[:chunk]
    w_own = (got[chunk:] * (rows * n_row) ** (-0.5)).astype(BF16)
    weight_grad = gather(gather(w_own, "z").reshape(slab, width), "x").reshape(width, width).astype(F32)
    return (output, feature_grad, weight_grad)


def solution(mesh):
    fine = Mesh(mesh.devices.reshape(16, 2, 2, 4, 4), ("z", "yl", "core", "x", "yh"))
    row, col = ("z", "yl", "core"), ("x", "yh")
    return jax.shard_map(
        shards,
        mesh=fine,
        in_specs=(P(row, col), P(row, col), P(col + row, None), P(), P(row + col, None)),
        out_specs=(P(row + col, None), P(col + row, None), P()),
        check_vma=False,
    )
```

time: 977 us -> 201 us (0.21)
  waiting for transfers between devices: 907 us -> 19.4 us
  blocking collectives: 38.7 us -> 153 us
  between operations: 13.8 us -> 0.92 us
  starting transfers between devices: 0.16 us -> 10.5 us
    psum x1 -> x0, waiting for transfers between devices: 446 us -> none  [shards(): summed = lax.psum(local_terms, ('row', 'col'))]
    reduce_scatter x2 -> x0, waiting for transfers between devices: 327 us -> none  [the longest x1 228 us: shards(): lax.psum_scatter(jnp.dot(columns.T, grad_whole, preferred_element_type=jn...]
    all_to_all x0 -> x9, blocking collectives: none -> 153 us  [exchange(): return lax.all_to_all(chunks, axis, split_axis=0, concat_axis=0, tiled=True)]
    all_gather x1 -> x0, waiting for transfers between devices: 134 us -> none  [shards(): lax.all_gather(features, 'row', axis=0, tiled=True)]
    all_gather x1 -> x0, blocking collectives: 38.7 us -> none  [shards(): grad_whole = lax.all_gather(grad_in, 'col', axis=0, tiled=True)]
    all_to_all x0 -> x3, waiting for transfers between devices: none -> 19.4 us  [exchange(): return lax.all_to_all(chunks, axis, split_axis=0, concat_axis=0, tiled=True)]
    all_to_all x0 -> x3, starting transfers between devices: none -> 10.5 us  [exchange(): return lax.all_to_all(chunks, axis, split_axis=0, concat_axis=0, tiled=True)]
  transfers between devices with their start and end apart: 4 -> 3, of which waited for: 4 -> 3; matrix products, arithmetic and copies ran while one was open for 1% -> 1% of each run, Pallas kernels for 0% -> 0%
where the time goes in v1:
time: 201 us; the launch traced here: 198 us
  blocking collectives  153 us (76%)
  waiting for transfers between devices  19.4 us (10%)
  starting transfers between devices  10.5 us (5%)
  local copies, waits for them, and re-layouts  7.86 us (4%)
  matrix products  3.88 us (2%)
  other arithmetic  2.68 us (1%)
    all_to_all x9, blocking collectives, exchange(): return lax.all_to_all(chunks, axis, split_axis=0, concat_axis=0, tiled=True)  153 us
    all_to_all x3, waiting for transfers between devices, exchange(): return lax.all_to_all(chunks, axis, split_axis=0, concat_axis=0, tiled=True)  19.4 us
    all_to_all x3, starting transfers between devices, exchange(): return lax.all_to_all(chunks, axis, split_axis=0, concat_axis=0, tiled=True)  10.5 us
  transfers between devices with their start and end apart: 3, of which 3 were waited for; matrix products, arithmetic and copies ran while one was open for 1% of the time, Pallas kernels for 0%

profile of v1, /device:TPU:1, one launch (start us, length us, event | category | flops | bytes accessed | tf_op | source)
XLA Modules:
  0.0 197.7 jit_solution(344324389822800722)
XLA Ops:
  0.7 0.8 broadcast_in_dim.28
  1.5 32.4 %all_to_all.60 = bf16[16,16,512]{2,1,0:T(8,128)(2,1)S(1)} all-to-all(bf16[16,16,512]{2,1,0:T(8,128)(2,1)S(1)} %broadcast_in_dim.28), channel_id=1, replica_groups=mesh['z'=16,'yl'=2,'core'=2,'x'=4,'yh'=4] {'z'}, dimensions={0} | all-to-all | bytes 524288 | tf_op jit(solution)/shard_map/all_to_all | solution.py:12
  33.8 0.9 broadcast_in_dim.29
  34.7 3.5 %all-to-all-start.1 = ((bf16[2,16,16,512]{3,2,1,0:T(8,128)(2,1)}), bf16[2,16,16,512]{3,2,1,0:T(8,128)(2,1)S(1)}, u32[]{:S(2)}, u32[]{:S(2)}) async-start(bf16[2,16,16,512]{3,2,1,0:T(8,128)(2,1)} %broadcast_in_dim.29), calls=%async_computation.1 | async-start | bytes 1048576 | tf_op jit(solution)/shard_map/all_to_all | solution.py:12
  39.2 1.0 copy-done.1
  40.6 3.0 %all-to-all-done.1 = bf16[2,16,16,512]{3,2,1,0:T(8,128)(2,1)S(1)} async-done(((bf16[2,16,16,512]{3,2,1,0:T(8,128)(2,1)}), bf16[2,16,16,512]{3,2,1,0:T(8,128)(2,1)S(1)}, u32[]{:S(2)}, u32[]{:S(2)}) %all-to-all-start.1) | async-done | bytes 524320 | tf_op jit(solution)/shard_map/all_to_all | solution.py:12
  43.8 11.5 %all_to_all.61 = bf16[2,2,16,16,512]{4,3,1,2,0:T(8,128)(2,1)S(1)} all-to-all(bf16[2,2,16,16,512]{4,3,1,2,0:T(8,128)(2,1)S(1)} %broadcast_in_dim.30), channel_id=1, replica_groups=mesh['z'=16,'yl'=2,'core'=2,'x'=4,'yh'=4] {'core'}, dimensions={0} | all-to-all | bytes 2097152 | tf_op jit(solution)/shard_map/all_to_all | solution.py:12
  56.1 12.4 %all_to_all.62 = bf16[4,128,512]{2,1,0:T(8,128)(2,1)S(1)} all-to-all(bf16[4,128,512]{2,1,0:T(8,128)(2,1)S(1)} %bitcast.41), channel_id=1, replica_groups=mesh['z'=16,'yl'=2,'core'=2,'x'=4,'yh'=4] {'x'}, dimensions={0} | all-to-all | bytes 1048576 | tf_op jit(solution)/shard_map/all_to_all | solution.py:12
  68.6 13.9 %all_to_all.63 = bf16[4,32,512]{2,1,0:T(8,128)(2,1)S(1)} all-to-all(bf16[4,32,512]{2,1,0:T(8,128)(2,1)S(1)} %bitcast.42), channel_id=1, replica_groups=mesh['z'=16,'yl'=2,'core'=2,'x'=4,'yh'=4] {'yh'}, dimensions={0} | all-to-all | bytes 262144 | tf_op jit(solution)/shard_map/all_to_all | solution.py:12
  82.5 0.8 multiply_convert_fusion
  83.4 10.7 %all_to_all.64 = bf16[4,32,1024]{2,1,0:T(8,128)(2,1)S(1)} all-to-all(bf16[4,32,1024]{2,1,0:T(8,128)(2,1)S(1)} %broadcast_in_dim.31), channel_id=1, replica_groups=mesh['z'=16,'yl'=2,'core'=2,'x'=4,'yh'=4] {'yh'}, dimensions={0} | all-to-all | bytes 524288 | tf_op jit(solution)/shard_map/all_to_all | solution.py:12
  94.1 1.1 broadcast_in_dim.33
  95.2 3.5 %all-to-all-start.6 = ((bf16[4,128,1024]{2,1,0:T(8,128)(2,1)}), bf16[4,128,1024]{2,1,0:T(8,128)(2,1)S(1)}, u32[]{:S(2)}, u32[]{:S(2)}) async-start(bf16[4,128,1024]{2,1,0:T(8,128)(2,1)} %broadcast_in_dim.33), calls=%async_computation.6 | async-start | bytes 2097152 | tf_op jit(solution)/shard_map/all_to_all | solution.py:12
  98.7 10.1 %all-to-all-done.6 = bf16[4,128,1024]{2,1,0:T(8,128)(2,1)S(1)} async-done(((bf16[4,128,1024]{2,1,0:T(8,128)(2,1)}), bf16[4,128,1024]{2,1,0:T(8,128)(2,1)S(1)}, u32[]{:S(2)}, u32[]{:S(2)}) %all-to-all-start.6) | async-done | bytes 1048608 | tf_op jit(solution)/shard_map/all_to_all | solution.py:12
  108.8 2.1 %convolution_convert_fusion = bf16[1024,512]{1,0:T(8,128)(2,1)} fusion(bf16[512,1024]{1,0:T(8,128)(2,1)S(1)} %mul.24, bf16[512,512]{1,0:T(8,128)(2,1)S(1)} %copy-done, bf16[512,1024]{1,0:T(8,128)(2,1)S(1)} %bitcast.29), kind=kOutput, calls=%fused_computation | convolution fusion | flops 806092800 | bytes 3145728 | tf_op jit(solution)/shard_map/dot_general | solution.py:50
  110.9 1.2 copy-done.2
  112.5 10.4 %all_to_all.65 = bf16[2,640,512]{2,1,0:T(8,128)(2,1)S(1)} all-to-all(bf16[2,640,512]{2,1,0:T(8,128)(2,1)S(1)} %pad_maximum_fusion), channel_id=1, replica_groups=mesh['z'=16,'yl'=2,'core'=2,'x'=4,'yh'=4] {'core'}, dimensions={0} | all-to-all | bytes 2621440 | tf_op jit(solution)/shard_map/all_to_all | solution.py:12
  123.7 13.0 %all_to_all.66 = bf16[2,384,512]{2,1,0:T(8,128)(2,1)S(1)} all-to-all(bf16[2,384,512]{2,1,0:T(8,128)(2,1)S(1)} %pad_maximum_fusion.1), channel_id=1, replica_groups=mesh['z'=16,'yl'=2,'core'=2,'x'=4,'yh'=4] {'yl'}, dimensions={0} | all-to-all | bytes 1572864 | tf_op jit(solution)/shard_map/all_to_all | solution.py:12
  136.9 24.5 %all_to_all.67 = bf16[16,24,512]{2,1,0:T(8,128)(2,1)S(1)} all-to-all(bf16[16,24,512]{2,1,0:T(8,128)(2,1)S(1)} %pad_maximum_fusion.2), channel_id=1, replica_groups=mesh['z'=16,'yl'=2,'core'=2,'x'=4,'yh'=4] {'z'}, dimensions={0} | all-to-all | bytes 786432 | tf_op jit(solution)/shard_map/all_to_all | solution.py:12
  161.5 23.8 %all_to_all.68 = bf16[16,8,512]{2,1,0:T(8,128)(2,1)S(1)} all-to-all(bf16[16,8,512]{2,1,0:T(8,128)(2,1)S(1)} %broadcast_in_dim.72), channel_id=1, replica_groups=mesh['z'=16,'yl'=2,'core'=2,'x'=4,'yh'=4] {'z'}, dimensions={0} | all-to-all | bytes 262144 | tf_op jit(solution)/shard_map/all_to_all | solution.py:12
  185.3 0.8 broadcast_in_dim.74
  186.2 3.5 %all-to-all-start.11 = ((bf16[4,128,512]{2,1,0:T(8,128)(2,1)}), bf16[4,128,512]{2,1,0:T(8,128)(2,1)S(1)}, u32[]{:S(2)}, u32[]{:S(2)}) async-start(bf16[4,128,512]{2,1,0:T(8,128)(2,1)} %broadcast_in_dim.74), calls=%async_computation.11 | async-start | bytes 1048576 | tf_op jit(solution)/shard_map/all_to_all | solution.py:12
  190.3 6.3 %all-to-all-done.11 = bf16[4,128,512]{2,1,0:T(8,128)(2,1)S(1)} async-done(((bf16[4,128,512]{2,1,0:T(8,128)(2,1)}), bf16[4,128,512]{2,1,0:T(8,128)(2,1)S(1)}, u32[]{:S(2)}, u32[]{:S(2)}) %all-to-all-start.11) | async-done | bytes 524320 | tf_op jit(solution)/shard_map/all_to_all | solution.py:12
  196.6 1.1 bitcast_convert_fusion
  (39 shorter events, 4.6 us)
Async XLA Ops:
  0.6 81.9 %copy-start = (bf16[512,512]{1,0:T(8,128)(2,1)S(1)}, bf16[512,512]{1,0:T(8,128)(2,1)}, u32[]{:S(2)}) copy-start(bf16[512,512]{1,0:T(8,128)(2,1)} %param.8) | copy-start | bytes 1572868
  0.6 37.5 %copy-start.4 = (s32[2,4]{1,0:T(2,128)S(1)}, s32[2,4]{1,0:T(2,128)}, u32[]{:S(2)}) copy-start(s32[2,4]{1,0:T(2,128)} %param.6) | copy-start | bytes 100
  34.7 8.9 %all-to-all-start.1 = ((bf16[2,16,16,512]{3,2,1,0:T(8,128)(2,1)}), bf16[2,16,16,512]{3,2,1,0:T(8,128)(2,1)S(1)}, u32[]{:S(2)}, u32[]{:S(2)}) async-start(bf16[2,16,16,512]{3,2,1,0:T(8,128)(2,1)} %broadcast_in_dim.29), calls=%async_computation.1 | async-start | bytes 1048576 | tf_op jit(solution)/shard_map/all_to_all | solution.py:12
  38.9 1.2 copy-start.1
  56.1 26.4 %copy-start.3 = (bf16[32,512]{1,0:T(8,128)(2,1)S(1)}, bf16[32,512]{1,0:T(8,128)(2,1)}, u32[]{:S(2)}) copy-start(bf16[32,512]{1,0:T(8,128)(2,1)} %param.9) | copy-start | bytes 98308
  95.2 13.6 %all-to-all-start.6 = ((bf16[4,128,1024]{2,1,0:T(8,128)(2,1)}), bf16[4,128,1024]{2,1,0:T(8,128)(2,1)S(1)}, u32[]{:S(2)}, u32[]{:S(2)}) async-start(bf16[4,128,1024]{2,1,0:T(8,128)(2,1)} %broadcast_in_dim.33), calls=%async_computation.6 | async-start | bytes 2097152 | tf_op jit(solution)/shard_map/all_to_all | solution.py:12
  110.8 1.2 copy-start.2
  186.2 10.4 %all-to-all-start.11 = ((bf16[4,128,512]{2,1,0:T(8,128)(2,1)}), bf16[4,128,512]{2,1,0:T(8,128)(2,1)S(1)}, u32[]{:S(2)}, u32[]{:S(2)}) async-start(bf16[4,128,512]{2,1,0:T(8,128)(2,1)} %broadcast_in_dim.74), calls=%async_computation.11 | async-start | bytes 1048576 | tf_op jit(solution)/shard_map/all_to_all | solution.py:12

commit v2 on v1

v2 whole, which is shorter than its diff:
```python
import jax
import jax.numpy as jnp
from jax import lax
from jax.sharding import Mesh, PartitionSpec as P

TILE = 256
F32 = jnp.float32
BF16 = jnp.bfloat16


def exchange(chunks, axis):
    return lax.all_to_all(chunks, axis, split_axis=0, concat_axis=0, tiled=True)


def gather(block, axis):
    n = lax.axis_size(axis)
    return exchange(jnp.broadcast_to(block[None], (n,) + block.shape), axis)


def shards(adjacency, block_mask, features, weight, upstream):
    rows, cols = adjacency.shape
    width = features.shape[1]
    nz, nyl, ncore, nx, nyh = (lax.axis_size(a) for a in ("z", "yl", "core", "x", "yh"))
    n_row, n_col = nz * nyl * ncore, nx * nyh
    masked = adjacency * jnp.repeat(jnp.repeat(block_mask, TILE, 0), TILE, 1).astype(BF16)

    n = lax.axis_index
    up_all = lax.all_gather(upstream.astype(F32), ("x", "yh"), axis=0, tiled=True)
    panel = gather(gather(gather(features, "z"), "yl"), "core")
    panel = panel.transpose(2, 1, 0, 3, 4).reshape(cols, width)

    partial = jnp.dot(masked, panel, preferred_element_type=F32).astype(BF16)
    over_x = exchange(partial.reshape(nx, rows // nx, width), "x")
    aggregate = gather(over_x.astype(F32).sum(0).astype(BF16), "yh").astype(F32).sum(0).astype(BF16)
    own = lax.dynamic_slice_in_dim(aggregate, n("yh") * (rows // n_col), rows // n_col, axis=0)
    pre = jnp.dot(own, weight, preferred_element_type=F32)
    output = (pre * jax.nn.sigmoid(pre)).astype(BF16)

    agg_all = gather(aggregate, "x").reshape(rows, width)
    pre = jnp.dot(agg_all, weight, preferred_element_type=F32)
    sigma = jax.nn.sigmoid(pre)
    dpre_all = (up_all * sigma * (1.0 + pre * (1.0 - sigma))).astype(BF16)
    grad_in = lax.dot_general(
        dpre_all, weight, (((1,), (1,)), ((), ())), preferred_element_type=F32
    ).astype(BF16)
    partial_fg = lax.dot_general(masked, grad_in, (((0,), (0,)), ((), ())), preferred_element_type=F32)
    slab = width // n_col
    agg_slab = lax.dynamic_slice_in_dim(agg_all, n(("yh", "x")) * slab, slab, axis=1)
    w = lax.dot_general(agg_slab, dpre_all, (((0,), (0,)), ((), ())), preferred_element_type=F32)

    chunk, piece = cols // n_row, slab // (ncore * nyl)
    fg = partial_fg.astype(BF16).reshape(nz, nyl, ncore, chunk, width).transpose(2, 1, 0, 3, 4)
    fg = fg.reshape(ncore, nyl * nz * chunk, width)
    w = w.astype(BF16).reshape(ncore, nyl * piece, width)
    both = exchange(jnp.concatenate([fg, w], axis=1), "core").astype(F32).sum(0).astype(BF16)
    fg = both[: nyl * nz * chunk].reshape(nyl, nz * chunk, width)
    w = both[nyl * nz * chunk :].reshape(nyl, piece, width)
    both = exchange(jnp.concatenate([fg, w], axis=1), "yl").astype(F32).sum(0).astype(BF16)
    fg = both[: nz * chunk].reshape(nz, chunk, width)
    w = jnp.broadcast_to(both[nz * chunk :][None], (nz, piece, width))
    both = exchange(jnp.concatenate([fg, w], axis=1), "z").astype(F32).sum(0)
    feature_grad = both[:chunk]
    w = (both[chunk:] * (rows * n_row) ** (-0.5)).astype(BF16)
    w = gather(w, ("yl", "yh"))
    w = gather(w, ("x", "core"))
    w = w.reshape(nx, ncore, nyl, nyh, piece, width).transpose(3, 0, 1, 2, 4, 5)
    weight_grad = w.astype(F32).reshape(width, width)
    return (output, feature_grad, weight_grad)


def solution(mesh):
    fine = Mesh(mesh.devices.reshape(16, 2, 2, 4, 4), ("z", "yl", "core", "x", "yh"))
    row, col = ("z", "yl", "core"), ("x", "yh")
    return jax.shard_map(
        shards,
        mesh=fine,
        in_specs=(P(row, col), P(row, col), P(col + row, None), P(), P(row + col, None)),
        out_specs=(P(row + col, None), P(col + row, None), P()),
        check_vma=False,
    )
```

time: 201 us -> 221 us (1.100)
  blocking collectives: 153 us -> 134 us
  waiting for transfers between devices: 19.4 us -> 35.7 us
  between operations: 0.92 us -> 14.3 us
  starting transfers between devices: 10.5 us -> 18.5 us
  matrix products: 3.88 us -> 7.73 us
    all_gather x0 -> x1, waiting for transfers between devices: none -> 25.4 us  [shards(): lax.all_gather(upstream.astype(F32), ('x', 'yh'), axis=0, tiled=True)]
    all_to_all x9 -> x8, blocking collectives: 153 us -> 134 us  [exchange(): return lax.all_to_all(chunks, axis, split_axis=0, concat_axis=0, tiled=True)]
    all_to_all x3, waiting for transfers between devices: 19.4 us -> 10.3 us  [exchange(): return lax.all_to_all(chunks, axis, split_axis=0, concat_axis=0, tiled=True)]
    all_to_all x3, starting transfers between devices: 10.5 us -> 18.5 us  [exchange(): return lax.all_to_all(chunks, axis, split_axis=0, concat_axis=0, tiled=True)]
    dot_general x1 -> x2, matrix products: 0.85 us -> 3.57 us  [the longest x1 2.74 us: shards(): pre = jnp.dot(agg_all, weight, preferred_element_type=F32)]
  transfers between devices with their start and end apart: 3 -> 4, of which waited for: 3 -> 3; matrix products, arithmetic and copies ran while one was open for 1% -> 2% of each run, Pallas kernels for 0% -> 0%
where the time goes in v2:
time: 221 us; the launch traced here: 220 us
  blocking collectives  134 us (61%)
  waiting for transfers between devices  35.7 us (16%)
  starting transfers between devices  18.5 us (8%)
  between operations  14.3 us (6%)
  matrix products  7.73 us (3%)
  local copies, waits for them, and re-layouts  7.41 us (3%)
    all_to_all x8, blocking collectives, exchange(): return lax.all_to_all(chunks, axis, split_axis=0, concat_axis=0, tiled=True)  134 us
    all_gather x1, waiting for transfers between devices, shards(): lax.all_gather(upstream.astype(F32), ('x', 'yh'), axis=0, tiled=True)  25.4 us
    all_to_all x3, starting transfers between devices, exchange(): return lax.all_to_all(chunks, axis, split_axis=0, concat_axis=0, tiled=True)  18.5 us
    all_to_all x3, waiting for transfers between devices, exchange(): return lax.all_to_all(chunks, axis, split_axis=0, concat_axis=0, tiled=True)  10.3 us
  transfers between devices with their start and end apart: 4, of which 3 were waited for; matrix products, arithmetic and copies ran while one was open for 2% of the time, Pallas kernels for 0%

profile of v2, /device:TPU:1, one launch (start us, length us, event | category | flops | bytes accessed | tf_op | source)
XLA Modules:
  0.0 219.9 jit_solution(8298420782574349753)
XLA Ops:
  7.2 0.8 broadcast_in_dim.22
  8.0 32.4 %all_to_all.55 = bf16[16,16,512]{2,1,0:T(8,128)(2,1)S(1)} all-to-all(bf16[16,16,512]{2,1,0:T(8,128)(2,1)S(1)} %broadcast_in_dim.22), channel_id=1, replica_groups=mesh['z'=16,'yl'=2,'core'=2,'x'=4,'yh'=4] {'z'}, dimensions={0} | all-to-all | bytes 524288 | tf_op jit(solution)/shard_map/all_to_all | solution.py:12
  40.3 0.9 broadcast_in_dim.23
  41.2 3.5 %all-to-all-start.1 = ((bf16[2,16,16,512]{3,2,1,0:T(8,128)(2,1)}), bf16[2,16,16,512]{3,2,1,0:T(8,128)(2,1)S(1)}, u32[]{:S(2)}, u32[]{:S(2)}) async-start(bf16[2,16,16,512]{3,2,1,0:T(8,128)(2,1)} %broadcast_in_dim.23), calls=%async_computation.1 | async-start | bytes 1048576 | tf_op jit(solution)/shard_map/all_to_all | solution.py:12
  46.4 1.0 copy-done.1
  47.8 2.3 %all-to-all-done.1 = bf16[2,16,16,512]{3,2,1,0:T(8,128)(2,1)S(1)} async-done(((bf16[2,16,16,512]{3,2,1,0:T(8,128)(2,1)}), bf16[2,16,16,512]{3,2,1,0:T(8,128)(2,1)S(1)}, u32[]{:S(2)}, u32[]{:S(2)}) %all-to-all-start.1) | async-done | bytes 524320 | tf_op jit(solution)/shard_map/all_to_all | solution.py:12
  50.3 11.5 %all_to_all.56 = bf16[2,2,16,16,512]{4,3,1,2,0:T(8,128)(2,1)S(1)} all-to-all(bf16[2,2,16,16,512]{4,3,1,2,0:T(8,128)(2,1)S(1)} %broadcast_in_dim.24), channel_id=1, replica_groups=mesh['z'=16,'yl'=2,'core'=2,'x'=4,'yh'=4] {'core'}, dimensions={0} | all-to-all | bytes 2097152 | tf_op jit(solution)/shard_map/all_to_all | solution.py:12
  62.6 12.4 %all_to_all.57 = bf16[4,128,512]{2,1,0:T(8,128)(2,1)S(1)} all-to-all(bf16[4,128,512]{2,1,0:T(8,128)(2,1)S(1)} %bitcast.43), channel_id=1, replica_groups=mesh['z'=16,'yl'=2,'core'=2,'x'=4,'yh'=4] {'x'}, dimensions={0} | all-to-all | bytes 1048576 | tf_op jit(solution)/shard_map/all_to_all | solution.py:12
  75.2 21.1 %all_to_all.58 = bf16[4,128,512]{2,1,0:T(8,128)(2,1)S(1)} all-to-all(bf16[4,128,512]{2,1,0:T(8,128)(2,1)S(1)} %broadcast_in_dim.25), channel_id=1, replica_groups=mesh['z'=16,'yl'=2,'core'=2,'x'=4,'yh'=4] {'yh'}, dimensions={0} | all-to-all | bytes 1048576 | tf_op jit(solution)/shard_map/all_to_all | solution.py:12
  96.4 0.8 broadcast_in_dim.26
  97.2 3.5 %all-to-all-start.5 = ((bf16[4,128,512]{2,1,0:T(8,128)(2,1)}), bf16[4,128,512]{2,1,0:T(8,128)(2,1)S(1)}, u32[]{:S(2)}, u32[]{:S(2)}) async-start(bf16[4,128,512]{2,1,0:T(8,128)(2,1)} %broadcast_in_dim.26), calls=%async_computation.5 | async-start | bytes 1048576 | tf_op jit(solution)/shard_map/all_to_all | solution.py:12
  100.7 25.4 %all-gather.2.cloned.1.call-done = f32[512,512]{1,0:T(8,128)} async-done(((f32[32,512]{1,0:T(8,128)}), f32[512,512]{1,0:T(8,128)}) %all-gather.2.cloned.1.call-update) | async-done | bytes 1048592 | tf_op jit(solution)/shard_map/all_gather | solution.py:28
  126.1 2.7 %multiply_convert_fusion = bf16[512,512]{1,0:T(8,128)(2,1)} fusion(f32[512,512]{1,0:T(8,128)} %all-gather.2.cloned.1.call-done, bf16[512,512]{1,0:T(8,128)(2,1)S(1)} %bitcast.40, bf16[512,512]{1,0:T(8,128)(2,1)S(1)} %copy-done), kind=kOutput, calls=%fused_computation.6 | convolution fusion | flops 270794752 | bytes 2621440 | tf_op jit(solution)/shard_map/dot_general | solution.py:40
  128.8 2.1 convolution_convert_fusion
  130.9 1.3 convolution_convert_fusion.3
  132.4 5.9 %all_to_all.59 = bf16[2,528,512]{2,1,0:T(8,128)(2,1)S(1)} all-to-all(bf16[2,528,512]{2,1,0:T(8,128)(2,1)S(1)} %pad_maximum_fusion), channel_id=1, replica_groups=mesh['z'=16,'yl'=2,'core'=2,'x'=4,'yh'=4] {'core'}, dimensions={0} | all-to-all | bytes 2162688 | tf_op jit(solution)/shard_map/all_to_all | solution.py:12
  139.0 10.3 %all_to_all.60 = bf16[2,264,512]{2,1,0:T(8,128)(2,1)S(1)} all-to-all(bf16[2,264,512]{2,1,0:T(8,128)(2,1)S(1)} %pad_maximum_fusion.1), channel_id=1, replica_groups=mesh['z'=16,'yl'=2,'core'=2,'x'=4,'yh'=4] {'yl'}, dimensions={0} | all-to-all | bytes 1081344 | tf_op jit(solution)/shard_map/all_to_all | solution.py:12
  149.5 30.0 %all_to_all.61 = bf16[16,24,512]{2,1,0:T(8,128)(2,1)S(1)} all-to-all(bf16[16,24,512]{2,1,0:T(8,128)(2,1)S(1)} %pad_maximum_fusion.2), channel_id=1, replica_groups=mesh['z'=16,'yl'=2,'core'=2,'x'=4,'yh'=4] {'z'}, dimensions={0} | all-to-all | bytes 786432 | tf_op jit(solution)/shard_map/all_to_all | solution.py:12
  179.6 10.4 %all_to_all.62 = bf16[8,8,512]{2,1,0:T(8,128)(2,1)S(1)} all-to-all(bf16[8,8,512]{2,1,0:T(8,128)(2,1)S(1)} %broadcast_in_dim.28), channel_id=1, replica_groups=mesh['z'=16,'yl'=2,'core'=2,'x'=4,'yh'=4] {'yl','yh'}, dimensions={0} | all-to-all | bytes 131072 | tf_op jit(solution)/shard_map/all_to_all | solution.py:12
  190.0 0.8 broadcast_in_dim.29
  190.8 11.5 %all-to-all-start.10 = ((bf16[8,8,8,512]{3,2,1,0:T(8,128)(2,1)}), bf16[8,8,8,512]{3,2,1,0:T(8,128)(2,1)S(1)}, u32[]{:S(2)}, u32[]{:S(2)}) async-start(bf16[8,8,8,512]{3,2,1,0:T(8,128)(2,1)} %broadcast_in_dim.29), calls=%async_computation.10 | async-start | bytes 1048576 | tf_op jit(solution)/shard_map/all_to_all | solution.py:12
  202.3 0.8 multiply_convert_fusion.1
  203.8 8.0 %all-to-all-done.10 = bf16[8,8,8,512]{3,2,1,0:T(8,128)(2,1)S(1)} async-done(((bf16[8,8,8,512]{3,2,1,0:T(8,128)(2,1)}), bf16[8,8,8,512]{3,2,1,0:T(8,128)(2,1)S(1)}, u32[]{:S(2)}, u32[]{:S(2)}) %all-to-all-start.10) | async-done | bytes 524320 | tf_op jit(solution)/shard_map/all_to_all | solution.py:12
  212.0 1.1 copy.18
  (39 shorter events, 4.9 us)
Async XLA Ops:
  7.2 118.9 %copy-start = (bf16[512,512]{1,0:T(8,128)(2,1)S(1)}, bf16[512,512]{1,0:T(8,128)(2,1)}, u32[]{:S(2)}) copy-start(bf16[512,512]{1,0:T(8,128)(2,1)} %param.8) | copy-start | bytes 1572868
  8.0 36.8 %copy-start.2 = (bf16[32,512]{1,0:T(8,128)(2,1)S(1)}, bf16[32,512]{1,0:T(8,128)(2,1)}, u32[]{:S(2)}) copy-start(bf16[32,512]{1,0:T(8,128)(2,1)} %param.9) | copy-start | bytes 98308
  40.3 5.1 %copy-start.3 = (s32[2,4]{1,0:T(2,128)S(1)}, s32[2,4]{1,0:T(2,128)}, u32[]{:S(2)}) copy-start(s32[2,4]{1,0:T(2,128)} %param.6) | copy-start | bytes 100
  41.2 8.9 %all-to-all-start.1 = ((bf16[2,16,16,512]{3,2,1,0:T(8,128)(2,1)}), bf16[2,16,16,512]{3,2,1,0:T(8,128)(2,1)S(1)}, u32[]{:S(2)}, u32[]{:S(2)}) async-start(bf16[2,16,16,512]{3,2,1,0:T(8,128)(2,1)} %broadcast_in_dim.23), calls=%async_computation.1 | async-start | bytes 1048576 | tf_op jit(solution)/shard_map/all_to_all | solution.py:12
  44.7 81.4 %all-gather.2.cloned.1.call-start = ((), (), s32[]{:S(2)}) async-start(), calls=%async_computation.11 | async-start | bytes 1114112 | tf_op jit(solution)/shard_map/all_gather | solution.py:28
  46.2 1.2 copy-start.1
  97.2 28.8 %all-to-all-start.5 = ((bf16[4,128,512]{2,1,0:T(8,128)(2,1)}), bf16[4,128,512]{2,1,0:T(8,128)(2,1)S(1)}, u32[]{:S(2)}, u32[]{:S(2)}) async-start(bf16[4,128,512]{2,1,0:T(8,128)(2,1)} %broadcast_in_dim.26), calls=%async_computation.5 | async-start | bytes 1048576 | tf_op jit(solution)/shard_map/all_to_all | solution.py:12
  190.8 21.0 %all-to-all-start.10 = ((bf16[8,8,8,512]{3,2,1,0:T(8,128)(2,1)}), bf16[8,8,8,512]{3,2,1,0:T(8,128)(2,1)S(1)}, u32[]{:S(2)}, u32[]{:S(2)}) async-start(bf16[8,8,8,512]{3,2,1,0:T(8,128)(2,1)} %broadcast_in_dim.29), calls=%async_computation.10 | async-start | bytes 1048576 | tf_op jit(solution)/shard_map/all_to_all | solution.py:12
Sparse Core Ops, SparseCore 0:
  49.7 76.2 all-gather.1

commit v3 on v2

--- a/solution.py
+++ b/solution.py
@@ -25,28 +25,32 @@
     masked = adjacency * jnp.repeat(jnp.repeat(block_mask, TILE, 0), TILE, 1).astype(BF16)
 
     n = lax.axis_index
-    up_all = lax.all_gather(upstream.astype(F32), ("x", "yh"), axis=0, tiled=True)
     panel = gather(gather(gather(features, "z"), "yl"), "core")
     panel = panel.transpose(2, 1, 0, 3, 4).reshape(cols, width)
 
     partial = jnp.dot(masked, panel, preferred_element_type=F32).astype(BF16)
-    over_x = exchange(partial.reshape(nx, rows // nx, width), "x")
-    aggregate = gather(over_x.astype(F32).sum(0).astype(BF16), "yh").astype(F32).sum(0).astype(BF16)
-    own = lax.dynamic_slice_in_dim(aggregate, n("yh") * (rows // n_col), rows // n_col, axis=0)
-    pre = jnp.dot(own, weight, preferred_element_type=F32)
-    output = (pre * jax.nn.sigmoid(pre)).astype(BF16)
+    over_col = exchange(partial.reshape(n_col, rows // n_col, width), ("x", "yh"))
+    aggregate = over_col.astype(F32).sum(0).astype(BF16)
+    pre = jnp.dot(aggregate, weight, preferred_element_type=F32)
+    sigma = jax.nn.sigmoid(pre)
+    output = (pre * sigma).astype(BF16)
+    dpre = (upstream.astype(F32) * sigma * (1.0 + pre * (1.0 - sigma))).astype(BF16)
 
-    agg_all = gather(aggregate, "x").reshape(rows, width)
-    pre = jnp.dot(agg_all, weight, preferred_element_type=F32)
-    sigma = jax.nn.sigmoid(pre)
-    dpre_all = (up_all * sigma * (1.0 + pre * (1.0 - sigma))).astype(BF16)
+    both = gather(jnp.concatenate([aggregate, dpre], axis=1), "yh").reshape(rows // nx, 2 * width)
+    slab = width // nyh
+    agg_slab = lax.dynamic_slice_in_dim(both, n("yh") * slab, slab, axis=1)
+    dpre_x = both[:, width:]
+    w = lax.dot_general(agg_slab, dpre_x, (((0,), (0,)), ((), ())), preferred_element_type=F32)
+    w = w.astype(BF16).reshape(nx, slab // nx, width)
+    dpre_x = jnp.broadcast_to(dpre_x[None], (nx,) + dpre_x.shape)
+    both = exchange(jnp.concatenate([dpre_x, w], axis=1), "x")
+    dpre_all = both[:, : rows // nx].reshape(rows, width)
+    w = both[:, rows // nx :].astype(F32).sum(0)
+    slab = width // n_col
     grad_in = lax.dot_general(
         dpre_all, weight, (((1,), (1,)), ((), ())), preferred_element_type=F32
     ).astype(BF16)
     partial_fg = lax.dot_general(masked, grad_in, (((0,), (0,)), ((), ())), preferred_element_type=F32)
-    slab = width // n_col
-    agg_slab = lax.dynamic_slice_in_dim(agg_all, n(("yh", "x")) * slab, slab, axis=1)
-    w = lax.dot_general(agg_slab, dpre_all, (((0,), (0,)), ((), ())), preferred_element_type=F32)
 
     chunk, piece = cols // n_row, slab // (ncore * nyl)
     fg = partial_fg.astype(BF16).reshape(nz, nyl, ncore, chunk, width).transpose(2, 1, 0, 3, 4)

time: 221 us -> 188 us (0.85)
  waiting for transfers between devices: 35.7 us -> 20.4 us
  between operations: 14.3 us -> 0.92 us
  matrix products: 7.73 us -> 3.9 us
    all_gather x1 -> x0, waiting for transfers between devices: 25.4 us -> none  [shards(): lax.all_gather(upstream.astype(F32), ('x', 'yh'), axis=0, tiled=True)]
    all_to_all x3, waiting for transfers between devices: 10.3 us -> 20.4 us  [exchange(): return lax.all_to_all(chunks, axis, split_axis=0, concat_axis=0, tiled=True)]
    dot_general x3 -> x2, matrix products: 4.9 us -> 1.07 us  [the longest x1 0.85 us: shards(): pre = jnp.dot(aggregate, weight, preferred_element_type=F32)]
  transfers between devices with their start and end apart: 4 -> 3, of which waited for: 3 -> 3; matrix products, arithmetic and copies ran while one was open for 2% -> 1% of each run, Pallas kernels for 0% -> 0%
where the time goes in v3:
time: 188 us; the launch traced here: 187 us
  blocking collectives  133 us (71%)
  waiting for transfers between devices  20.4 us (11%)
  starting transfers between devices  18.8 us (10%)
  local copies, waits for them, and re-layouts  8.13 us (4%)
  matrix products  3.9 us (2%)
    all_to_all x8, blocking collectives, exchange(): return lax.all_to_all(chunks, axis, split_axis=0, concat_axis=0, tiled=True)  133 us
    all_to_all x3, waiting for transfers between devices, exchange(): return lax.all_to_all(chunks, axis, split_axis=0, concat_axis=0, tiled=True)  20.4 us
    all_to_all x3, starting transfers between devices, exchange(): return lax.all_to_all(chunks, axis, split_axis=0, concat_axis=0, tiled=True)  18.8 us
  transfers between devices with their start and end apart: 3, of which 3 were waited for; matrix products, arithmetic and copies ran while one was open for 1% of the time, Pallas kernels for 0%

profile of v3, /device:TPU:1, one launch (start us, length us, event | category | flops | bytes accessed | tf_op | source)
XLA Modules:
  0.0 186.8 jit_solution(10908825541851145479)
XLA Ops:
  0.6 0.8 broadcast_in_dim.22
  1.5 32.4 %all_to_all.55 = bf16[16,16,512]{2,1,0:T(8,128)(2,1)S(1)} all-to-all(bf16[16,16,512]{2,1,0:T(8,128)(2,1)S(1)} %broadcast_in_dim.22), channel_id=1, replica_groups=mesh['z'=16,'yl'=2,'core'=2,'x'=4,'yh'=4] {'z'}, dimensions={0} | all-to-all | bytes 524288 | tf_op jit(solution)/shard_map/all_to_all | solution.py:12
  33.8 0.9 broadcast_in_dim.23
  34.7 3.5 %all-to-all-start.1 = ((bf16[2,16,16,512]{3,2,1,0:T(8,128)(2,1)}), bf16[2,16,16,512]{3,2,1,0:T(8,128)(2,1)S(1)}, u32[]{:S(2)}, u32[]{:S(2)}) async-start(bf16[2,16,16,512]{3,2,1,0:T(8,128)(2,1)} %broadcast_in_dim.23), calls=%async_computation.1 | async-start | bytes 1048576 | tf_op jit(solution)/shard_map/all_to_all | solution.py:12
  38.2 0.7 broadcast_in_dim.21
  39.2 1.0 copy-done.1
  40.6 3.0 %all-to-all-done.1 = bf16[2,16,16,512]{3,2,1,0:T(8,128)(2,1)S(1)} async-done(((bf16[2,16,16,512]{3,2,1,0:T(8,128)(2,1)}), bf16[2,16,16,512]{3,2,1,0:T(8,128)(2,1)S(1)}, u32[]{:S(2)}, u32[]{:S(2)}) %all-to-all-start.1) | async-done | bytes 524320 | tf_op jit(solution)/shard_map/all_to_all | solution.py:12
  43.8 11.5 %all_to_all.56 = bf16[2,2,16,16,512]{4,3,1,2,0:T(8,128)(2,1)S(1)} all-to-all(bf16[2,2,16,16,512]{4,3,1,2,0:T(8,128)(2,1)S(1)} %broadcast_in_dim.24), channel_id=1, replica_groups=mesh['z'=16,'yl'=2,'core'=2,'x'=4,'yh'=4] {'core'}, dimensions={0} | all-to-all | bytes 2097152 | tf_op jit(solution)/shard_map/all_to_all | solution.py:12
  56.1 25.9 %all_to_all.57 = bf16[16,32,512]{2,1,0:T(8,128)(2,1)S(1)} all-to-all(bf16[16,32,512]{2,1,0:T(8,128)(2,1)S(1)} %bitcast.44), channel_id=1, replica_groups=mesh['z'=16,'yl'=2,'core'=2,'x'=4,'yh'=4] {'x','yh'}, dimensions={0} | all-to-all | bytes 1048576 | tf_op jit(solution)/shard_map/all_to_all | solution.py:12
  82.1 0.8 multiply_convert_fusion
  83.0 0.7 broadcast_in_dim.25
  83.7 3.8 %all-to-all-start.4 = ((bf16[4,32,1024]{2,1,0:T(8,128)(2,1)}), bf16[4,32,1024]{2,1,0:T(8,128)(2,1)S(1)}, u32[]{:S(2)}, u32[]{:S(2)}) async-start(bf16[4,32,1024]{2,1,0:T(8,128)(2,1)} %broadcast_in_dim.25), calls=%async_computation.4 | async-start | bytes 524288 | tf_op jit(solution)/shard_map/all_to_all | solution.py:12
  87.5 8.5 %all-to-all-done.4 = bf16[4,32,1024]{2,1,0:T(8,128)(2,1)S(1)} async-done(((bf16[4,32,1024]{2,1,0:T(8,128)(2,1)}), bf16[4,32,1024]{2,1,0:T(8,128)(2,1)S(1)}, u32[]{:S(2)}, u32[]{:S(2)}) %all-to-all-start.4) | async-done | bytes 262176 | tf_op jit(solution)/shard_map/all_to_all | solution.py:12
  96.3 10.2 %all_to_all.58 = bf16[4,160,512]{2,1,0:T(8,128)(2,1)S(1)} all-to-all(bf16[4,160,512]{2,1,0:T(8,128)(2,1)S(1)} %pad_maximum_fusion.1), channel_id=1, replica_groups=mesh['z'=16,'yl'=2,'core'=2,'x'=4,'yh'=4] {'x'}, dimensions={0} | all-to-all | bytes 1310720 | tf_op jit(solution)/shard_map/all_to_all | solution.py:12
  106.5 0.8 slice.37
  107.3 2.1 %convolution_convert_fusion = bf16[1024,512]{1,0:T(8,128)(2,1)S(1)} fusion(bf16[512,1024]{1,0:T(8,128)(2,1)S(1)} %mul.24, bf16[512,512]{1,0:T(8,128)(2,1)} %bitcast.45, bf16[512,512]{1,0:T(8,128)(2,1)S(1)} %copy-done), kind=kOutput, calls=%fused_computation | convolution fusion | flops 806092800 | bytes 3145728 | tf_op jit(solution)/shard_map/dot_general | solution.py:53
  109.7 8.3 %all_to_all.59 = bf16[2,528,512]{2,1,0:T(8,128)(2,1)S(1)} all-to-all(bf16[2,528,512]{2,1,0:T(8,128)(2,1)S(1)} %pad_maximum_fusion), channel_id=1, replica_groups=mesh['z'=16,'yl'=2,'core'=2,'x'=4,'yh'=4] {'core'}, dimensions={0} | all-to-all | bytes 2162688 | tf_op jit(solution)/shard_map/all_to_all | solution.py:12
  118.6 10.3 %all_to_all.60 = bf16[2,264,512]{2,1,0:T(8,128)(2,1)S(1)} all-to-all(bf16[2,264,512]{2,1,0:T(8,128)(2,1)S(1)} %pad_maximum_fusion.2), channel_id=1, replica_groups=mesh['z'=16,'yl'=2,'core'=2,'x'=4,'yh'=4] {'yl'}, dimensions={0} | all-to-all | bytes 1081344 | tf_op jit(solution)/shard_map/all_to_all | solution.py:12
  129.0 24.3 %all_to_all.61 = bf16[16,24,512]{2,1,0:T(8,128)(2,1)S(1)} all-to-all(bf16[16,24,512]{2,1,0:T(8,128)(2,1)S(1)} %pad_maximum_fusion.3), channel_id=1, replica_groups=mesh['z'=16,'yl'=2,'core'=2,'x'=4,'yh'=4] {'z'}, dimensions={0} | all-to-all | bytes 786432 | tf_op jit(solution)/shard_map/all_to_all | solution.py:12
  153.5 10.3 %all_to_all.62 = bf16[8,8,512]{2,1,0:T(8,128)(2,1)S(1)} all-to-all(bf16[8,8,512]{2,1,0:T(8,128)(2,1)S(1)} %broadcast_in_dim.28), channel_id=1, replica_groups=mesh['z'=16,'yl'=2,'core'=2,'x'=4,'yh'=4] {'yl','yh'}, dimensions={0} | all-to-all | bytes 131072 | tf_op jit(solution)/shard_map/all_to_all | solution.py:12
  163.8 0.8 broadcast_in_dim.29
  164.6 11.5 %all-to-all-start.10 = ((bf16[8,8,8,512]{3,2,1,0:T(8,128)(2,1)}), bf16[8,8,8,512]{3,2,1,0:T(8,128)(2,1)S(1)}, u32[]{:S(2)}, u32[]{:S(2)}) async-start(bf16[8,8,8,512]{3,2,1,0:T(8,128)(2,1)} %broadcast_in_dim.29), calls=%async_computation.10 | async-start | bytes 1048576 | tf_op jit(solution)/shard_map/all_to_all | solution.py:12
  176.7 8.9 %all-to-all-done.10 = bf16[8,8,8,512]{3,2,1,0:T(8,128)(2,1)S(1)} async-done(((bf16[8,8,8,512]{3,2,1,0:T(8,128)(2,1)}), bf16[8,8,8,512]{3,2,1,0:T(8,128)(2,1)S(1)}, u32[]{:S(2)}, u32[]{:S(2)}) %all-to-all-start.10) | async-done | bytes 524320 | tf_op jit(solution)/shard_map/all_to_all | solution.py:12
  185.7 1.1 copy.18
  (38 shorter events, 3.7 us)
Async XLA Ops:
  0.6 81.5 %copy-start = (bf16[512,512]{1,0:T(8,128)(2,1)S(1)}, bf16[512,512]{1,0:T(8,128)(2,1)}, u32[]{:S(2)}) copy-start(bf16[512,512]{1,0:T(8,128)(2,1)} %param.8) | copy-start | bytes 1572868
  1.4 36.7 %copy-start.3 = (s32[2,4]{1,0:T(2,128)S(1)}, s32[2,4]{1,0:T(2,128)}, u32[]{:S(2)}) copy-start(s32[2,4]{1,0:T(2,128)} %param.6) | copy-start | bytes 100
  34.7 8.9 %all-to-all-start.1 = ((bf16[2,16,16,512]{3,2,1,0:T(8,128)(2,1)}), bf16[2,16,16,512]{3,2,1,0:T(8,128)(2,1)S(1)}, u32[]{:S(2)}, u32[]{:S(2)}) async-start(bf16[2,16,16,512]{3,2,1,0:T(8,128)(2,1)} %broadcast_in_dim.23), calls=%async_computation.1 | async-start | bytes 1048576 | tf_op jit(solution)/shard_map/all_to_all | solution.py:12
  38.9 1.2 copy-start.1
  56.1 26.0 %copy-start.2 = (bf16[32,512]{1,0:T(8,128)(2,1)S(1)}, bf16[32,512]{1,0:T(8,128)(2,1)}, u32[]{:S(2)}) copy-start(bf16[32,512]{1,0:T(8,128)(2,1)} %param.9) | copy-start | bytes 98308
  83.7 12.3 %all-to-all-start.4 = ((bf16[4,32,1024]{2,1,0:T(8,128)(2,1)}), bf16[4,32,1024]{2,1,0:T(8,128)(2,1)S(1)}, u32[]{:S(2)}, u32[]{:S(2)}) async-start(bf16[4,32,1024]{2,1,0:T(8,128)(2,1)} %broadcast_in_dim.25), calls=%async_computation.4 | async-start | bytes 524288 | tf_op jit(solution)/shard_map/all_to_all | solution.py:12
  164.6 21.0 %all-to-all-start.10 = ((bf16[8,8,8,512]{3,2,1,0:T(8,128)(2,1)}), bf16[8,8,8,512]{3,2,1,0:T(8,128)(2,1)S(1)}, u32[]{:S(2)}, u32[]{:S(2)}) async-start(bf16[8,8,8,512]{3,2,1,0:T(8,128)(2,1)} %broadcast_in_dim.29), calls=%async_computation.10 | async-start | bytes 1048576 | tf_op jit(solution)/shard_map/all_to_all | solution.py:12

commit v4 on v3

v4 whole, which is shorter than its diff:
```python
import jax
import jax.numpy as jnp
from jax import lax
from jax.sharding import Mesh, PartitionSpec as P

TILE = 256
F32 = jnp.float32
BF16 = jnp.bfloat16


def exchange(chunks, axis):
    return lax.all_to_all(chunks, axis, split_axis=0, concat_axis=0, tiled=True)


def gather(block, axis):
    n = lax.axis_size(axis)
    return exchange(jnp.broadcast_to(block[None], (n,) + block.shape), axis)


def halve(pair, axis):
    me = lax.axis_index(axis)
    theirs = lax.dynamic_index_in_dim(pair, 1 - me, 0, keepdims=False)
    mine = lax.dynamic_index_in_dim(pair, me, 0, keepdims=False)
    got = lax.ppermute(theirs, axis, [(0, 1), (1, 0)])
    return (mine.astype(F32) + got.astype(F32)).astype(BF16)


def pass_round(block, axis):
    n, me = lax.axis_size(axis), lax.axis_index(axis)
    got = [block]
    for k in range(1, n):
        got.append(lax.ppermute(block, axis, [((i + k) % n, i) for i in range(n)]))
    both = jnp.stack(got + got[:-1])
    return lax.dynamic_slice_in_dim(both, (n - me) % n, n, axis=0)


def shards(adjacency, block_mask, features, weight, upstream):
    rows, cols = adjacency.shape
    width = features.shape[1]
    nz, nyl, ncore, nx, nyh = (lax.axis_size(a) for a in ("z", "yl", "core", "x", "yh"))
    n_row, n_col = nz * nyl * ncore, nx * nyh
    masked = adjacency * jnp.repeat(jnp.repeat(block_mask, TILE, 0), TILE, 1).astype(BF16)

    n = lax.axis_index
    panel = gather(gather(gather(features, "z"), "yl"), "core")
    panel = panel.transpose(2, 1, 0, 3, 4).reshape(cols, width)

    partial = jnp.dot(masked, panel, preferred_element_type=F32).astype(BF16)
    over_col = exchange(partial.reshape(n_col, rows // n_col, width), ("x", "yh"))
    aggregate = over_col.astype(F32).sum(0).astype(BF16)
    pre = jnp.dot(aggregate, weight, preferred_element_type=F32)
    sigma = jax.nn.sigmoid(pre)
    output = (pre * sigma).astype(BF16)
    dpre = (upstream.astype(F32) * sigma * (1.0 + pre * (1.0 - sigma))).astype(BF16)

    both = gather(jnp.concatenate([aggregate, dpre], axis=1), "yh").reshape(rows // nx, 2 * width)
    agg_x, dpre_x = both[:, :width], both[:, width:]
    w = lax.dot_general(agg_x, dpre_x, (((0,), (0,)), ((), ())), preferred_element_type=F32)
    slab = width // n_col
    w = lax.dynamic_index_in_dim(w.reshape(nx, nyh, slab, width), n("yh"), axis=1, keepdims=False)
    dpre_x = jnp.broadcast_to(dpre_x[None], (nx,) + dpre_x.shape)
    both = exchange(jnp.concatenate([dpre_x, w.astype(BF16)], axis=1), "x")
    dpre_all = both[:, : rows // nx].reshape(rows, width)
    w = both[:, rows // nx :].astype(F32).sum(0).astype(BF16)

    chunk, piece = cols // n_row, slab // (ncore * nyl)
    w = exchange(w.reshape(nyl * ncore, piece, width), ("yl", "core")).astype(F32).sum(0).astype(BF16)
    w = gather(w, "z").astype(F32).sum(0) * (rows * n_row) ** (-0.5)
    w = w.astype(BF16)

    grad_in = lax.dot_general(
        dpre_all, weight, (((1,), (1,)), ((), ())), preferred_element_type=F32
    ).astype(BF16)
    partial_fg = lax.dot_general(masked, grad_in, (((0,), (0,)), ((), ())), preferred_element_type=F32)
    fg = partial_fg.astype(BF16).reshape(nz, nyl, ncore, chunk, width).transpose(2, 1, 0, 3, 4)
    fg = halve(fg, "core")
    fg = halve(fg, "yl")
    fg, w = lax.optimization_barrier((fg, w))
    feature_grad = exchange(fg, "z").astype(F32).sum(0)

    w = pass_round(w, ("yl", "core"))
    w = pass_round(w.reshape(slab, width), "yh")
    w, feature_grad = lax.optimization_barrier((w, feature_grad))
    w = gather(w.reshape(slab * nyh, width), "x")
    return (output, feature_grad, w.astype(F32).reshape(width, width))


def solution(mesh):
    fine = Mesh(mesh.devices.reshape(16, 2, 2, 4, 4), ("z", "yl", "core", "x", "yh"))
    row, col = ("z", "yl", "core"), ("x", "yh")
    return jax.shard_map(
        shards,
        mesh=fine,
        in_specs=(P(row, col), P(row, col), P(col + row, None), P(), P(row + col, None)),
        out_specs=(P(row + col, None), P(col + row, None), P()),
        check_vma=False,
    )
```

time: 188 us -> 192 us (1.021)
  the two profiles are of different devices: /device:TPU:1 before, /device:TPU:64 now
where the time goes in v4:
time: 192 us; the launch traced here: 191 us
  blocking collectives  86.6 us (45%)
  starting transfers between devices  47.6 us (25%)
  waiting for transfers between devices  41.6 us (22%)
  local copies, waits for them, and re-layouts  6.34 us (3%)
  other arithmetic  4.21 us (2%)
  matrix products  3.99 us (2%)
    all_to_all x5, blocking collectives, exchange(): return lax.all_to_all(chunks, axis, split_axis=0, concat_axis=0, tiled=True)  86.6 us
    all_to_all x5, waiting for transfers between devices, exchange(): return lax.all_to_all(chunks, axis, split_axis=0, concat_axis=0, tiled=True)  37.8 us
    all_to_all x5, starting transfers between devices, exchange(): return lax.all_to_all(chunks, axis, split_axis=0, concat_axis=0, tiled=True)  25 us
    ppermute x6, starting transfers between devices, pass_round(): got.append(lax.ppermute(block, axis, [((i + k) % n, i) for i in range(n)]))  18.7 us
    ppermute x2, starting transfers between devices, halve(): got = lax.ppermute(theirs, axis, [(0, 1), (1, 0)])  3.86 us
  transfers between devices with their start and end apart: 13, of which 6 were waited for; matrix products, arithmetic and copies ran while one was open for 1% of the time, Pallas kernels for 0%

profile of v4, /device:TPU:64, one launch (start us, length us, event | category | flops | bytes accessed | tf_op | source)
XLA Modules:
  0.0 191.4 jit_solution(10081969319208659717)
XLA Ops:
  1.4 36.1 %all_to_all.50 = bf16[16,16,512]{2,1,0:T(8,128)(2,1)S(1)} all-to-all(bf16[16,16,512]{2,1,0:T(8,128)(2,1)S(1)} %broadcast_in_dim.22), channel_id=1, replica_groups=mesh['z'=16,'yl'=2,'core'=2,'x'=4,'yh'=4] {'z'}, dimensions={0} | all-to-all | bytes 524288 | tf_op jit(solution)/shard_map/all_to_all | solution.py:12
  38.4 3.5 %all-to-all-start.1 = ((bf16[2,16,16,512]{3,2,1,0:T(8,128)(2,1)}), bf16[2,16,16,512]{3,2,1,0:T(8,128)(2,1)S(1)}, u32[]{:S(2)}, u32[]{:S(2)}) async-start(bf16[2,16,16,512]{3,2,1,0:T(8,128)(2,1)} %broadcast_in_dim.23), calls=%async_computation.1 | async-start | bytes 1048576 | tf_op jit(solution)/shard_map/all_to_all | solution.py:12
  44.3 5.0 %all-to-all-done.1 = bf16[2,16,16,512]{3,2,1,0:T(8,128)(2,1)S(1)} async-done(((bf16[2,16,16,512]{3,2,1,0:T(8,128)(2,1)}), bf16[2,16,16,512]{3,2,1,0:T(8,128)(2,1)S(1)}, u32[]{:S(2)}, u32[]{:S(2)}) %all-to-all-start.1) | async-done | bytes 524320 | tf_op jit(solution)/shard_map/all_to_all | solution.py:12
  49.5 4.6 %all_to_all.51 = bf16[2,2,16,16,512]{4,3,1,2,0:T(8,128)(2,1)S(1)} all-to-all(bf16[2,2,16,16,512]{4,3,1,2,0:T(8,128)(2,1)S(1)} %broadcast_in_dim.24), channel_id=1, replica_groups=mesh['z'=16,'yl'=2,'core'=2,'x'=4,'yh'=4] {'core'}, dimensions={0} | all-to-all | bytes 2097152 | tf_op jit(solution)/shard_map/all_to_all | solution.py:12
  54.9 28.1 %all_to_all.52 = bf16[16,32,512]{2,1,0:T(8,128)(2,1)S(1)} all-to-all(bf16[16,32,512]{2,1,0:T(8,128)(2,1)S(1)} %bitcast.80), channel_id=1, replica_groups=mesh['z'=16,'yl'=2,'core'=2,'x'=4,'yh'=4] {'x','yh'}, dimensions={0} | all-to-all | bytes 1048576 | tf_op jit(solution)/shard_map/all_to_all | solution.py:12
  84.7 3.4 %all-to-all-start.4 = ((bf16[4,32,1024]{2,1,0:T(8,128)(2,1)}), bf16[4,32,1024]{2,1,0:T(8,128)(2,1)S(1)}, u32[]{:S(2)}, u32[]{:S(2)}) async-start(bf16[4,32,1024]{2,1,0:T(8,128)(2,1)} %broadcast_in_dim.25), calls=%async_computation.4 | async-start | bytes 524288 | tf_op jit(solution)/shard_map/all_to_all | solution.py:12
  88.1 9.2 %all-to-all-done.4 = bf16[4,32,1024]{2,1,0:T(8,128)(2,1)S(1)} async-done(((bf16[4,32,1024]{2,1,0:T(8,128)(2,1)}), bf16[4,32,1024]{2,1,0:T(8,128)(2,1)S(1)}, u32[]{:S(2)}, u32[]{:S(2)}) %all-to-all-start.4) | async-done | bytes 262176 | tf_op jit(solution)/shard_map/all_to_all | solution.py:12
  98.7 3.5 %all-to-all-start.5 = ((bf16[4,160,512]{2,1,0:T(8,128)(2,1)}), bf16[4,160,512]{2,1,0:T(8,128)(2,1)S(1)}, u32[]{:S(2)}, u32[]{:S(2)}) async-start(bf16[4,160,512]{2,1,0:T(8,128)(2,1)} %pad_maximum_fusion), calls=%async_computation.5 | async-start | bytes 1310720 | tf_op jit(solution)/shard_map/all_to_all | solution.py:12
  102.1 8.7 %all-to-all-done.5 = bf16[4,160,512]{2,1,0:T(8,128)(2,1)S(1)} async-done(((bf16[4,160,512]{2,1,0:T(8,128)(2,1)}), bf16[4,160,512]{2,1,0:T(8,128)(2,1)S(1)}, u32[]{:S(2)}, u32[]{:S(2)}) %all-to-all-start.5) | async-done | bytes 655392 | tf_op jit(solution)/shard_map/all_to_all | solution.py:12
  111.7 2.1 %convolution_convert_fusion = bf16[1024,512]{1,0:T(8,128)(2,1)S(1)} fusion(bf16[512,1024]{1,0:T(8,128)(2,1)S(1)} %mul.24, bf16[512,512]{1,0:T(8,128)(2,1)} %bitcast.81, bf16[512,512]{1,0:T(8,128)(2,1)S(1)} %copy-done), kind=kOutput, calls=%fused_computation | convolution fusion | flops 806092800 | bytes 3145728 | tf_op jit(solution)/shard_map/dot_general | solution.py:74
  113.9 1.9 %collective-permute-start = (bf16[2,16,16,512]{3,2,0,1:T(8,128)(2,1)S(1)}, bf16[2,16,16,512]{3,2,0,1:T(8,128)(2,1)S(1)}, u32[]{:S(2)}, u32[]{:S(2)}) collective-permute-start(bf16[2,16,16,512]{3,2,0,1:T(8,128)(2,1)S(1)} %dynamic-slice_bitcast_fusion), channel_id=1, source_target_pairs={{0,16},{16,0},{1,17},{17,1},{2,18},{18,2},{3,19},{19,3},{4,20},{20... | collective-permute-start | bytes 1572872 | tf_op jit(solution)/shard_map/ppermute | solution.py:24
  115.9 6.3 %all_to_all.53 = bf16[4,8,512]{2,1,0:T(8,128)(2,1)S(1)} all-to-all(bf16[4,8,512]{2,1,0:T(8,128)(2,1)S(1)} %bitcast.82), channel_id=1, replica_groups=mesh['z'=16,'yl'=2,'core'=2,'x'=4,'yh'=4] {'yl','core'}, dimensions={0} | all-to-all | bytes 65536 | tf_op jit(solution)/shard_map/all_to_all | solution.py:12
  122.8 7.0 %all-to-all-start.7 = ((bf16[16,8,512]{2,1,0:T(8,128)(2,1)}), bf16[16,8,512]{2,1,0:T(8,128)(2,1)S(1)}, u32[]{:S(2)}, u32[]{:S(2)}) async-start(bf16[16,8,512]{2,1,0:T(8,128)(2,1)} %broadcast_in_dim.27), calls=%async_computation.7 | async-start | bytes 262144 | tf_op jit(solution)/shard_map/all_to_all | solution.py:12
  130.1 1.9 %collective-permute-start.1 = (bf16[16,16,512]{2,1,0:T(8,128)(2,1)S(1)}, bf16[16,16,512]{2,1,0:T(8,128)(2,1)S(1)}, u32[]{:S(2)}, u32[]{:S(2)}) collective-permute-start(bf16[16,16,512]{2,1,0:T(8,128)(2,1)S(1)} %dynamic-slice_bitcast_fusion.1), channel_id=1, source_target_pairs={{0,32},{32,0},{1,33},{33,1},{2,34},{34,2},{3,35},{35,3},{4,36},{36... | collective-permute-start | bytes 786440 | tf_op jit(solution)/shard_map/ppermute | solution.py:24
  132.0 11.8 %all-to-all-done.7 = bf16[16,8,512]{2,1,0:T(8,128)(2,1)S(1)} async-done(((bf16[16,8,512]{2,1,0:T(8,128)(2,1)}), bf16[16,8,512]{2,1,0:T(8,128)(2,1)S(1)}, u32[]{:S(2)}, u32[]{:S(2)}) %all-to-all-start.7) | async-done | bytes 131104 | tf_op jit(solution)/shard_map/all_to_all | solution.py:12
  146.6 2.2 %collective-permute-start.3 = (bf16[8,512]{1,0:T(8,128)(2,1)S(1)}, bf16[8,512]{1,0:T(8,128)(2,1)S(1)}, u32[]{:S(2)}, u32[]{:S(2)}) collective-permute-start(bf16[8,512]{1,0:T(8,128)(2,1)S(1)} %multiply_convert_fusion.2), channel_id=1, source_target_pairs={{32,0},{48,16},{0,32},{16,48},{33,1},{49,17},{1,33},{17,49},{34,2}... | collective-permute-start | bytes 24584 | tf_op jit(solution)/shard_map/ppermute | solution.py:32
  148.7 3.4 %collective-permute-start.2 = (bf16[8,512]{1,0:T(8,128)(2,1)S(1)}, bf16[8,512]{1,0:T(8,128)(2,1)S(1)}, u32[]{:S(2)}, u32[]{:S(2)}) collective-permute-start(bf16[8,512]{1,0:T(8,128)(2,1)S(1)} %multiply_convert_fusion.2), channel_id=1, source_target_pairs={{16,0},{32,16},{48,32},{0,48},{17,1},{33,17},{49,33},{1,49},{18,2}... | collective-permute-start | bytes 24584 | tf_op jit(solution)/shard_map/ppermute | solution.py:32
  152.2 7.6 %all-to-all-start.8 = ((bf16[16,16,512]{2,1,0:T(8,128)(2,1)}), bf16[16,16,512]{2,1,0:T(8,128)(2,1)S(1)}, u32[]{:S(2)}, u32[]{:S(2)}) async-start(bf16[16,16,512]{2,1,0:T(8,128)(2,1)} %fusion.1), calls=%async_computation.8 | async-start | bytes 524288 | tf_op jit(solution)/shard_map/all_to_all | solution.py:12
  159.9 3.4 %collective-permute-start.7 = (bf16[32,512]{1,0:T(8,128)(2,1)S(1)}, bf16[32,512]{1,0:T(8,128)(2,1)S(1)}, u32[]{:S(2)}, u32[]{:S(2)}) collective-permute-start(bf16[32,512]{1,0:T(8,128)(2,1)S(1)} %dynamic-slice_bitcast_fusion.2), channel_id=1, source_target_pairs={{3,0},{0,1},{1,2},{2,3},{7,4},{4,5},{5,6},{6,7},{11,8},{8,9},{9,10... | collective-permute-start | bytes 98312 | tf_op jit(solution)/shard_map/ppermute | solution.py:32
  163.2 4.9 %collective-permute-start.6 = (bf16[32,512]{1,0:T(8,128)(2,1)S(1)}, bf16[32,512]{1,0:T(8,128)(2,1)S(1)}, u32[]{:S(2)}, u32[]{:S(2)}) collective-permute-start(bf16[32,512]{1,0:T(8,128)(2,1)S(1)} %dynamic-slice_bitcast_fusion.2), channel_id=1, source_target_pairs={{2,0},{3,1},{0,2},{1,3},{6,4},{7,5},{4,6},{5,7},{10,8},{11,9},{8,1... | collective-permute-start | bytes 98312 | tf_op jit(solution)/shard_map/ppermute | solution.py:32
  168.1 3.0 %collective-permute-start.5 = (bf16[32,512]{1,0:T(8,128)(2,1)S(1)}, bf16[32,512]{1,0:T(8,128)(2,1)S(1)}, u32[]{:S(2)}, u32[]{:S(2)}) collective-permute-start(bf16[32,512]{1,0:T(8,128)(2,1)S(1)} %dynamic-slice_bitcast_fusion.2), channel_id=1, source_target_pairs={{1,0},{2,1},{3,2},{0,3},{5,4},{6,5},{7,6},{4,7},{9,8},{10,9},{11,1... | collective-permute-start | bytes 98312 | tf_op jit(solution)/shard_map/ppermute | solution.py:32
  171.1 3.8 %collective-permute-done.5 = bf16[32,512]{1,0:T(8,128)(2,1)S(1)} collective-permute-done((bf16[32,512]{1,0:T(8,128)(2,1)S(1)}, bf16[32,512]{1,0:T(8,128)(2,1)S(1)}, u32[]{:S(2)}, u32[]{:S(2)}) %collective-permute-start.5) | collective-permute-done | bytes 32800 | tf_op jit(solution)/shard_map/ppermute | solution.py:32
  175.0 3.1 %all-to-all-done.8 = bf16[16,16,512]{2,1,0:T(8,128)(2,1)S(1)} async-done(((bf16[16,16,512]{2,1,0:T(8,128)(2,1)}), bf16[16,16,512]{2,1,0:T(8,128)(2,1)S(1)}, u32[]{:S(2)}, u32[]{:S(2)}) %all-to-all-start.8) | async-done | bytes 262176 | tf_op jit(solution)/shard_map/all_to_all | solution.py:12
  178.8 11.5 %all_to_all.54 = bf16[4,128,512]{2,1,0:T(8,128)(2,1)S(1)} all-to-all(bf16[4,128,512]{2,1,0:T(8,128)(2,1)S(1)} %broadcast_in_dim.58), channel_id=1, replica_groups=mesh['z'=16,'yl'=2,'core'=2,'x'=4,'yh'=4] {'x'}, dimensions={0} | all-to-all | bytes 1048576 | tf_op jit(solution)/shard_map/all_to_all | solution.py:12
  (65 shorter events, 14.3 us)
Async XLA Ops:
  0.6 82.5 %copy-start = (bf16[512,512]{1,0:T(8,128)(2,1)S(1)}, bf16[512,512]{1,0:T(8,128)(2,1)}, u32[]{:S(2)}) copy-start(bf16[512,512]{1,0:T(8,128)(2,1)} %param.8) | copy-start | bytes 1572868
  37.6 4.4 %copy-start.3 = (s32[2,4]{1,0:T(2,128)S(1)}, s32[2,4]{1,0:T(2,128)}, u32[]{:S(2)}) copy-start(s32[2,4]{1,0:T(2,128)} %param.6) | copy-start | bytes 100
  38.4 10.9 %all-to-all-start.1 = ((bf16[2,16,16,512]{3,2,1,0:T(8,128)(2,1)}), bf16[2,16,16,512]{3,2,1,0:T(8,128)(2,1)S(1)}, u32[]{:S(2)}, u32[]{:S(2)}) async-start(bf16[2,16,16,512]{3,2,1,0:T(8,128)(2,1)} %broadcast_in_dim.23), calls=%async_computation.1 | async-start | bytes 1048576 | tf_op jit(solution)/shard_map/all_to_all | solution.py:12
  42.7 1.2 copy-start.1
  54.9 28.2 %copy-start.2 = (bf16[32,512]{1,0:T(8,128)(2,1)S(1)}, bf16[32,512]{1,0:T(8,128)(2,1)}, u32[]{:S(2)}) copy-start(bf16[32,512]{1,0:T(8,128)(2,1)} %param.9) | copy-start | bytes 98308
  84.7 12.7 %all-to-all-start.4 = ((bf16[4,32,1024]{2,1,0:T(8,128)(2,1)}), bf16[4,32,1024]{2,1,0:T(8,128)(2,1)S(1)}, u32[]{:S(2)}, u32[]{:S(2)}) async-start(bf16[4,32,1024]{2,1,0:T(8,128)(2,1)} %broadcast_in_dim.25), calls=%async_computation.4 | async-start | bytes 524288 | tf_op jit(solution)/shard_map/all_to_all | solution.py:12
  98.7 12.2 %all-to-all-start.5 = ((bf16[4,160,512]{2,1,0:T(8,128)(2,1)}), bf16[4,160,512]{2,1,0:T(8,128)(2,1)S(1)}, u32[]{:S(2)}, u32[]{:S(2)}) async-start(bf16[4,160,512]{2,1,0:T(8,128)(2,1)} %pad_maximum_fusion), calls=%async_computation.5 | async-start | bytes 1310720 | tf_op jit(solution)/shard_map/all_to_all | solution.py:12
  113.9 16.0 %collective-permute-start = (bf16[2,16,16,512]{3,2,0,1:T(8,128)(2,1)S(1)}, bf16[2,16,16,512]{3,2,0,1:T(8,128)(2,1)S(1)}, u32[]{:S(2)}, u32[]{:S(2)}) collective-permute-start(bf16[2,16,16,512]{3,2,0,1:T(8,128)(2,1)S(1)} %dynamic-slice_bitcast_fusion), channel_id=1, source_target_pairs={{0,16},{16,0},{1,17},{17,1},{2,18},{18,2},{3,19},{19,3},{4,20},{20... | collective-permute-start | bytes 1572872 | tf_op jit(solution)/shard_map/ppermute | solution.py:24
  122.8 21.0 %all-to-all-start.7 = ((bf16[16,8,512]{2,1,0:T(8,128)(2,1)}), bf16[16,8,512]{2,1,0:T(8,128)(2,1)S(1)}, u32[]{:S(2)}, u32[]{:S(2)}) async-start(bf16[16,8,512]{2,1,0:T(8,128)(2,1)} %broadcast_in_dim.27), calls=%async_computation.7 | async-start | bytes 262144 | tf_op jit(solution)/shard_map/all_to_all | solution.py:12
  130.1 13.7 %collective-permute-start.1 = (bf16[16,16,512]{2,1,0:T(8,128)(2,1)S(1)}, bf16[16,16,512]{2,1,0:T(8,128)(2,1)S(1)}, u32[]{:S(2)}, u32[]{:S(2)}) collective-permute-start(bf16[16,16,512]{2,1,0:T(8,128)(2,1)S(1)} %dynamic-slice_bitcast_fusion.1), channel_id=1, source_target_pairs={{0,32},{32,0},{1,33},{33,1},{2,34},{34,2},{3,35},{35,3},{4,36},{36... | collective-permute-start | bytes 786440 | tf_op jit(solution)/shard_map/ppermute | solution.py:24
  144.6 15.1 %collective-permute-start.4 = (bf16[8,512]{1,0:T(8,128)(2,1)S(1)}, bf16[8,512]{1,0:T(8,128)(2,1)S(1)}, u32[]{:S(2)}, u32[]{:S(2)}) collective-permute-start(bf16[8,512]{1,0:T(8,128)(2,1)S(1)} %multiply_convert_fusion.2), channel_id=1, source_target_pairs={{48,0},{0,16},{16,32},{32,48},{49,1},{1,17},{17,33},{33,49},{50,2}... | collective-permute-start | bytes 24584 | tf_op jit(solution)/shard_map/ppermute | solution.py:32
  146.6 13.2 %collective-permute-start.3 = (bf16[8,512]{1,0:T(8,128)(2,1)S(1)}, bf16[8,512]{1,0:T(8,128)(2,1)S(1)}, u32[]{:S(2)}, u32[]{:S(2)}) collective-permute-start(bf16[8,512]{1,0:T(8,128)(2,1)S(1)} %multiply_convert_fusion.2), channel_id=1, source_target_pairs={{32,0},{48,16},{0,32},{16,48},{33,1},{49,17},{1,33},{17,49},{34,2}... | collective-permute-start | bytes 24584 | tf_op jit(solution)/shard_map/ppermute | solution.py:32
  148.7 11.0 %collective-permute-start.2 = (bf16[8,512]{1,0:T(8,128)(2,1)S(1)}, bf16[8,512]{1,0:T(8,128)(2,1)S(1)}, u32[]{:S(2)}, u32[]{:S(2)}) collective-permute-start(bf16[8,512]{1,0:T(8,128)(2,1)S(1)} %multiply_convert_fusion.2), channel_id=1, source_target_pairs={{16,0},{32,16},{48,32},{0,48},{17,1},{33,17},{49,33},{1,49},{18,2}... | collective-permute-start | bytes 24584 | tf_op jit(solution)/shard_map/ppermute | solution.py:32
  152.2 25.9 %all-to-all-start.8 = ((bf16[16,16,512]{2,1,0:T(8,128)(2,1)}), bf16[16,16,512]{2,1,0:T(8,128)(2,1)S(1)}, u32[]{:S(2)}, u32[]{:S(2)}) async-start(bf16[16,16,512]{2,1,0:T(8,128)(2,1)} %fusion.1), calls=%async_computation.8 | async-start | bytes 524288 | tf_op jit(solution)/shard_map/all_to_all | solution.py:12
  159.9 15.1 %collective-permute-start.7 = (bf16[32,512]{1,0:T(8,128)(2,1)S(1)}, bf16[32,512]{1,0:T(8,128)(2,1)S(1)}, u32[]{:S(2)}, u32[]{:S(2)}) collective-permute-start(bf16[32,512]{1,0:T(8,128)(2,1)S(1)} %dynamic-slice_bitcast_fusion.2), channel_id=1, source_target_pairs={{3,0},{0,1},{1,2},{2,3},{7,4},{4,5},{5,6},{6,7},{11,8},{8,9},{9,10... | collective-permute-start | bytes 98312 | tf_op jit(solution)/shard_map/ppermute | solution.py:32
  163.2 11.7 %collective-permute-start.6 = (bf16[32,512]{1,0:T(8,128)(2,1)S(1)}, bf16[32,512]{1,0:T(8,128)(2,1)S(1)}, u32[]{:S(2)}, u32[]{:S(2)}) collective-permute-start(bf16[32,512]{1,0:T(8,128)(2,1)S(1)} %dynamic-slice_bitcast_fusion.2), channel_id=1, source_target_pairs={{2,0},{3,1},{0,2},{1,3},{6,4},{7,5},{4,6},{5,7},{10,8},{11,9},{8,1... | collective-permute-start | bytes 98312 | tf_op jit(solution)/shard_map/ppermute | solution.py:32
  168.1 6.8 %collective-permute-start.5 = (bf16[32,512]{1,0:T(8,128)(2,1)S(1)}, bf16[32,512]{1,0:T(8,128)(2,1)S(1)}, u32[]{:S(2)}, u32[]{:S(2)}) collective-permute-start(bf16[32,512]{1,0:T(8,128)(2,1)S(1)} %dynamic-slice_bitcast_fusion.2), channel_id=1, source_target_pairs={{1,0},{2,1},{3,2},{0,3},{5,4},{6,5},{7,6},{4,7},{9,8},{10,9},{11,1... | collective-permute-start | bytes 98312 | tf_op jit(solution)/shard_map/ppermute | solution.py:32

commit v5 on v4

--- a/solution.py
+++ b/solution.py
@@ -23,15 +23,6 @@
     mine = lax.dynamic_index_in_dim(pair, me, 0, keepdims=False)
     got = lax.ppermute(theirs, axis, [(0, 1), (1, 0)])
     return (mine.astype(F32) + got.astype(F32)).astype(BF16)
-
-
-def pass_round(block, axis):
-    n, me = lax.axis_size(axis), lax.axis_index(axis)
-    got = [block]
-    for k in range(1, n):
-        got.append(lax.ppermute(block, axis, [((i + k) % n, i) for i in range(n)]))
-    both = jnp.stack(got + got[:-1])
-    return lax.dynamic_slice_in_dim(both, (n - me) % n, n, axis=0)
 
 
 def shards(adjacency, block_mask, features, weight, upstream):
@@ -78,10 +69,11 @@
     fg, w = lax.optimization_barrier((fg, w))
     feature_grad = exchange(fg, "z").astype(F32).sum(0)
 
-    w = pass_round(w, ("yl", "core"))
-    w = pass_round(w.reshape(slab, width), "yh")
+    w = lax.all_gather(w, "core", axis=0, tiled=True)
+    w = lax.all_gather(w, "yl", axis=0, tiled=True)
+    w = lax.all_gather(w, "yh", axis=0, tiled=True)
     w, feature_grad = lax.optimization_barrier((w, feature_grad))
-    w = gather(w.reshape(slab * nyh, width), "x")
+    w = gather(w, "x")
     return (output, feature_grad, w.astype(F32).reshape(width, width))
 
 

time: 192 us -> 185 us (0.964)
  the two profiles are of different devices: /device:TPU:64 before, /device:TPU:1 now
where the time goes in v5:
time: 185 us; the launch traced here: 182 us
  blocking collectives  104 us (56%)
  starting transfers between devices  33.5 us (18%)
  waiting for transfers between devices  29.2 us (16%)
  local copies, waits for them, and re-layouts  6.26 us (3%)
  other arithmetic  4.21 us (2%)
  matrix products  3.99 us (2%)
    all_to_all x5, blocking collectives, exchange(): return lax.all_to_all(chunks, axis, split_axis=0, concat_axis=0, tiled=True)  84.7 us
    all_to_all x5, waiting for transfers between devices, exchange(): return lax.all_to_all(chunks, axis, split_axis=0, concat_axis=0, tiled=True)  29.2 us
    all_to_all x5, starting transfers between devices, exchange(): return lax.all_to_all(chunks, axis, split_axis=0, concat_axis=0, tiled=True)  25.8 us
    all_gather x1, blocking collectives, shards(): w = lax.all_gather(w, 'yh', axis=0, tiled=True)  12 us
    ppermute x2, starting transfers between devices, halve(): got = lax.ppermute(theirs, axis, [(0, 1), (1, 0)])  7.77 us
    all_gather x1, blocking collectives, shards(): w = lax.all_gather(w, 'core', axis=0, tiled=True)  4.03 us
  transfers between devices with their start and end apart: 7, of which 4 were waited for; matrix products, arithmetic and copies ran while one was open for 1% of the time, Pallas kernels for 0%

profile of v5, /device:TPU:1, one launch (start us, length us, event | category | flops | bytes accessed | tf_op | source)
XLA Modules:
  0.0 182.0 jit_solution(3803825755126282268)
XLA Ops:
  1.4 32.4 %all_to_all.50 = bf16[16,16,512]{2,1,0:T(8,128)(2,1)S(1)} all-to-all(bf16[16,16,512]{2,1,0:T(8,128)(2,1)S(1)} %broadcast_in_dim.20), channel_id=1, replica_groups=mesh['z'=16,'yl'=2,'core'=2,'x'=4,'yh'=4] {'z'}, dimensions={0} | all-to-all | bytes 524288 | tf_op jit(solution)/shard_map/all_to_all | solution.py:12
  33.8 0.9 broadcast_in_dim.21
  34.7 3.5 %all-to-all-start.1 = ((bf16[2,16,16,512]{3,2,1,0:T(8,128)(2,1)}), bf16[2,16,16,512]{3,2,1,0:T(8,128)(2,1)S(1)}, u32[]{:S(2)}, u32[]{:S(2)}) async-start(bf16[2,16,16,512]{3,2,1,0:T(8,128)(2,1)} %broadcast_in_dim.21), calls=%async_computation.1 | async-start | bytes 1048576 | tf_op jit(solution)/shard_map/all_to_all | solution.py:12
  39.2 1.0 copy-done.1
  40.6 3.0 %all-to-all-done.1 = bf16[2,16,16,512]{3,2,1,0:T(8,128)(2,1)S(1)} async-done(((bf16[2,16,16,512]{3,2,1,0:T(8,128)(2,1)}), bf16[2,16,16,512]{3,2,1,0:T(8,128)(2,1)S(1)}, u32[]{:S(2)}, u32[]{:S(2)}) %all-to-all-start.1) | async-done | bytes 524320 | tf_op jit(solution)/shard_map/all_to_all | solution.py:12
  43.7 11.5 %all_to_all.51 = bf16[2,2,16,16,512]{4,3,1,2,0:T(8,128)(2,1)S(1)} all-to-all(bf16[2,2,16,16,512]{4,3,1,2,0:T(8,128)(2,1)S(1)} %broadcast_in_dim.22), channel_id=1, replica_groups=mesh['z'=16,'yl'=2,'core'=2,'x'=4,'yh'=4] {'core'}, dimensions={0} | all-to-all | bytes 2097152 | tf_op jit(solution)/shard_map/all_to_all | solution.py:12
  56.1 25.9 %all_to_all.52 = bf16[16,32,512]{2,1,0:T(8,128)(2,1)S(1)} all-to-all(bf16[16,32,512]{2,1,0:T(8,128)(2,1)S(1)} %bitcast.54), channel_id=1, replica_groups=mesh['z'=16,'yl'=2,'core'=2,'x'=4,'yh'=4] {'x','yh'}, dimensions={0} | all-to-all | bytes 1048576 | tf_op jit(solution)/shard_map/all_to_all | solution.py:12
  83.7 3.8 %all-to-all-start.4 = ((bf16[4,32,1024]{2,1,0:T(8,128)(2,1)}), bf16[4,32,1024]{2,1,0:T(8,128)(2,1)S(1)}, u32[]{:S(2)}, u32[]{:S(2)}) async-start(bf16[4,32,1024]{2,1,0:T(8,128)(2,1)} %broadcast_in_dim.23), calls=%async_computation.4 | async-start | bytes 524288 | tf_op jit(solution)/shard_map/all_to_all | solution.py:12
  87.5 8.5 %all-to-all-done.4 = bf16[4,32,1024]{2,1,0:T(8,128)(2,1)S(1)} async-done(((bf16[4,32,1024]{2,1,0:T(8,128)(2,1)}), bf16[4,32,1024]{2,1,0:T(8,128)(2,1)S(1)}, u32[]{:S(2)}, u32[]{:S(2)}) %all-to-all-start.4) | async-done | bytes 262176 | tf_op jit(solution)/shard_map/all_to_all | solution.py:12
  96.4 0.9 pad_maximum_fusion
  97.3 3.5 %all-to-all-start.5 = ((bf16[4,160,512]{2,1,0:T(8,128)(2,1)}), bf16[4,160,512]{2,1,0:T(8,128)(2,1)S(1)}, u32[]{:S(2)}, u32[]{:S(2)}) async-start(bf16[4,160,512]{2,1,0:T(8,128)(2,1)} %pad_maximum_fusion), calls=%async_computation.5 | async-start | bytes 1310720 | tf_op jit(solution)/shard_map/all_to_all | solution.py:12
  100.8 7.8 %all-to-all-done.5 = bf16[4,160,512]{2,1,0:T(8,128)(2,1)S(1)} async-done(((bf16[4,160,512]{2,1,0:T(8,128)(2,1)}), bf16[4,160,512]{2,1,0:T(8,128)(2,1)S(1)}, u32[]{:S(2)}, u32[]{:S(2)}) %all-to-all-start.5) | async-done | bytes 655392 | tf_op jit(solution)/shard_map/all_to_all | solution.py:12
  109.5 2.1 %convolution_convert_fusion = bf16[1024,512]{1,0:T(8,128)(2,1)S(1)} fusion(bf16[512,1024]{1,0:T(8,128)(2,1)S(1)} %mul.21, bf16[512,512]{1,0:T(8,128)(2,1)} %bitcast.55, bf16[512,512]{1,0:T(8,128)(2,1)S(1)} %copy-done), kind=kOutput, calls=%fused_computation | convolution fusion | flops 806092800 | bytes 3145728 | tf_op jit(solution)/shard_map/dot_general | solution.py:65
  111.7 5.9 %collective-permute-start = (bf16[2,16,16,512]{3,2,0,1:T(8,128)(2,1)S(1)}, bf16[2,16,16,512]{3,2,0,1:T(8,128)(2,1)S(1)}, u32[]{:S(2)}, u32[]{:S(2)}) collective-permute-start(bf16[2,16,16,512]{3,2,0,1:T(8,128)(2,1)S(1)} %dynamic-slice_bitcast_fusion), channel_id=1, source_target_pairs={{0,16},{16,0},{1,17},{17,1},{2,18},{18,2},{3,19},{19,3},{4,20},{20... | collective-permute-start | bytes 1572872 | tf_op jit(solution)/shard_map/ppermute | solution.py:24
  117.5 5.5 %all_to_all.53 = bf16[4,8,512]{2,1,0:T(8,128)(2,1)S(1)} all-to-all(bf16[4,8,512]{2,1,0:T(8,128)(2,1)S(1)} %bitcast.56), channel_id=1, replica_groups=mesh['z'=16,'yl'=2,'core'=2,'x'=4,'yh'=4] {'yl','core'}, dimensions={0} | all-to-all | bytes 65536 | tf_op jit(solution)/shard_map/all_to_all | solution.py:12
  123.8 7.0 %all-to-all-start.7 = ((bf16[16,8,512]{2,1,0:T(8,128)(2,1)}), bf16[16,8,512]{2,1,0:T(8,128)(2,1)S(1)}, u32[]{:S(2)}, u32[]{:S(2)}) async-start(bf16[16,8,512]{2,1,0:T(8,128)(2,1)} %broadcast_in_dim.25), calls=%async_computation.7 | async-start | bytes 262144 | tf_op jit(solution)/shard_map/all_to_all | solution.py:12
  131.0 1.9 %collective-permute-start.1 = (bf16[16,16,512]{2,1,0:T(8,128)(2,1)S(1)}, bf16[16,16,512]{2,1,0:T(8,128)(2,1)S(1)}, u32[]{:S(2)}, u32[]{:S(2)}) collective-permute-start(bf16[16,16,512]{2,1,0:T(8,128)(2,1)S(1)} %dynamic-slice_bitcast_fusion.1), channel_id=1, source_target_pairs={{0,32},{32,0},{1,33},{33,1},{2,34},{34,2},{3,35},{35,3},{4,36},{36... | collective-permute-start | bytes 786440 | tf_op jit(solution)/shard_map/ppermute | solution.py:24
  132.9 9.8 %all-to-all-done.7 = bf16[16,8,512]{2,1,0:T(8,128)(2,1)S(1)} async-done(((bf16[16,8,512]{2,1,0:T(8,128)(2,1)}), bf16[16,8,512]{2,1,0:T(8,128)(2,1)S(1)}, u32[]{:S(2)}, u32[]{:S(2)}) %all-to-all-start.7) | async-done | bytes 131104 | tf_op jit(solution)/shard_map/all_to_all | solution.py:12
  143.6 8.0 %all-to-all-start.8 = ((bf16[16,16,512]{2,1,0:T(8,128)(2,1)}), bf16[16,16,512]{2,1,0:T(8,128)(2,1)S(1)}, u32[]{:S(2)}, u32[]{:S(2)}) async-start(bf16[16,16,512]{2,1,0:T(8,128)(2,1)} %fusion.1), calls=%async_computation.8 | async-start | bytes 524288 | tf_op jit(solution)/shard_map/all_to_all | solution.py:12
  151.6 4.0 %all_gather.9 = bf16[16,512]{1,0:T(8,128)(2,1)S(1)} all-gather(bf16[8,512]{1,0:T(8,128)(2,1)S(1)} %multiply_convert_fusion.2), channel_id=1, replica_groups=mesh['z'=16,'yl'=2,'core'=2,'x'=4,'yh'=4] {'core'}, dimensions={0}, use_global_device_ids=true | all-gather | bytes 24576 | tf_op jit(solution)/shard_map/all_gather | solution.py:72
  155.6 3.3 %all_gather.10 = bf16[32,512]{1,0:T(8,128)(2,1)S(1)} all-gather(bf16[16,512]{1,0:T(8,128)(2,1)S(1)} %all_gather.9), channel_id=1, replica_groups=mesh['z'=16,'yl'=2,'core'=2,'x'=4,'yh'=4] {'yl'}, dimensions={0}, use_global_device_ids=true | all-gather | bytes 49152 | tf_op jit(solution)/shard_map/all_gather | solution.py:73
  158.9 12.0 %all_gather.11 = bf16[128,512]{1,0:T(8,128)(2,1)S(1)} all-gather(bf16[32,512]{1,0:T(8,128)(2,1)S(1)} %all_gather.10), channel_id=1, replica_groups=mesh['z'=16,'yl'=2,'core'=2,'x'=4,'yh'=4] {'yh'}, dimensions={0}, use_global_device_ids=true | all-gather | bytes 163840 | tf_op jit(solution)/shard_map/all_gather | solution.py:74
  171.6 9.3 %all_to_all.54 = bf16[4,128,512]{2,1,0:T(8,128)(2,1)S(1)} all-to-all(bf16[4,128,512]{2,1,0:T(8,128)(2,1)S(1)} %broadcast_in_dim.26), channel_id=1, replica_groups=mesh['z'=16,'yl'=2,'core'=2,'x'=4,'yh'=4] {'x'}, dimensions={0} | all-to-all | bytes 1048576 | tf_op jit(solution)/shard_map/all_to_all | solution.py:12
  180.9 1.1 bitcast_convert_fusion
  (40 shorter events, 8.5 us)
Async XLA Ops:
  0.6 81.5 %copy-start = (bf16[512,512]{1,0:T(8,128)(2,1)S(1)}, bf16[512,512]{1,0:T(8,128)(2,1)}, u32[]{:S(2)}) copy-start(bf16[512,512]{1,0:T(8,128)(2,1)} %param.8) | copy-start | bytes 1572868
  33.8 4.4 %copy-start.3 = (s32[2,4]{1,0:T(2,128)S(1)}, s32[2,4]{1,0:T(2,128)}, u32[]{:S(2)}) copy-start(s32[2,4]{1,0:T(2,128)} %param.6) | copy-start | bytes 100
  34.7 8.9 %all-to-all-start.1 = ((bf16[2,16,16,512]{3,2,1,0:T(8,128)(2,1)}), bf16[2,16,16,512]{3,2,1,0:T(8,128)(2,1)S(1)}, u32[]{:S(2)}, u32[]{:S(2)}) async-start(bf16[2,16,16,512]{3,2,1,0:T(8,128)(2,1)} %broadcast_in_dim.21), calls=%async_computation.1 | async-start | bytes 1048576 | tf_op jit(solution)/shard_map/all_to_all | solution.py:12
  38.9 1.2 copy-start.1
  56.1 26.0 %copy-start.2 = (bf16[32,512]{1,0:T(8,128)(2,1)S(1)}, bf16[32,512]{1,0:T(8,128)(2,1)}, u32[]{:S(2)}) copy-start(bf16[32,512]{1,0:T(8,128)(2,1)} %param.9) | copy-start | bytes 98308
  83.7 12.3 %all-to-all-start.4 = ((bf16[4,32,1024]{2,1,0:T(8,128)(2,1)}), bf16[4,32,1024]{2,1,0:T(8,128)(2,1)S(1)}, u32[]{:S(2)}, u32[]{:S(2)}) async-start(bf16[4,32,1024]{2,1,0:T(8,128)(2,1)} %broadcast_in_dim.23), calls=%async_computation.4 | async-start | bytes 524288 | tf_op jit(solution)/shard_map/all_to_all | solution.py:12
  97.3 11.3 %all-to-all-start.5 = ((bf16[4,160,512]{2,1,0:T(8,128)(2,1)}), bf16[4,160,512]{2,1,0:T(8,128)(2,1)S(1)}, u32[]{:S(2)}, u32[]{:S(2)}) async-start(bf16[4,160,512]{2,1,0:T(8,128)(2,1)} %pad_maximum_fusion), calls=%async_computation.5 | async-start | bytes 1310720 | tf_op jit(solution)/shard_map/all_to_all | solution.py:12
  111.7 19.1 %collective-permute-start = (bf16[2,16,16,512]{3,2,0,1:T(8,128)(2,1)S(1)}, bf16[2,16,16,512]{3,2,0,1:T(8,128)(2,1)S(1)}, u32[]{:S(2)}, u32[]{:S(2)}) collective-permute-start(bf16[2,16,16,512]{3,2,0,1:T(8,128)(2,1)S(1)} %dynamic-slice_bitcast_fusion), channel_id=1, source_target_pairs={{0,16},{16,0},{1,17},{17,1},{2,18},{18,2},{3,19},{19,3},{4,20},{20... | collective-permute-start | bytes 1572872 | tf_op jit(solution)/shard_map/ppermute | solution.py:24
  123.8 19.0 %all-to-all-start.7 = ((bf16[16,8,512]{2,1,0:T(8,128)(2,1)}), bf16[16,8,512]{2,1,0:T(8,128)(2,1)S(1)}, u32[]{:S(2)}, u32[]{:S(2)}) async-start(bf16[16,8,512]{2,1,0:T(8,128)(2,1)} %broadcast_in_dim.25), calls=%async_computation.7 | async-start | bytes 262144 | tf_op jit(solution)/shard_map/all_to_all | solution.py:12
  131.0 11.8 %collective-permute-start.1 = (bf16[16,16,512]{2,1,0:T(8,128)(2,1)S(1)}, bf16[16,16,512]{2,1,0:T(8,128)(2,1)S(1)}, u32[]{:S(2)}, u32[]{:S(2)}) collective-permute-start(bf16[16,16,512]{2,1,0:T(8,128)(2,1)S(1)} %dynamic-slice_bitcast_fusion.1), channel_id=1, source_target_pairs={{0,32},{32,0},{1,33},{33,1},{2,34},{34,2},{3,35},{35,3},{4,36},{36... | collective-permute-start | bytes 786440 | tf_op jit(solution)/shard_map/ppermute | solution.py:24
  143.6 27.3 %all-to-all-start.8 = ((bf16[16,16,512]{2,1,0:T(8,128)(2,1)}), bf16[16,16,512]{2,1,0:T(8,128)(2,1)S(1)}, u32[]{:S(2)}, u32[]{:S(2)}) async-start(bf16[16,16,512]{2,1,0:T(8,128)(2,1)} %fusion.1), calls=%async_computation.8 | async-start | bytes 524288 | tf_op jit(solution)/shard_map/all_to_all | solution.py:12

commit v6 on v5

v6 whole, which is shorter than its diff:
```python
import jax
import jax.numpy as jnp
from jax import lax
from jax.sharding import Mesh, PartitionSpec as P

TILE = 256
F32 = jnp.float32
BF16 = jnp.bfloat16


def exchange(chunks, axis):
    return lax.all_to_all(chunks, axis, split_axis=0, concat_axis=0, tiled=True)


def gather(block, axis):
    n = lax.axis_size(axis)
    return exchange(jnp.broadcast_to(block[None], (n,) + block.shape), axis)


def halve(pair, axis, at):
    theirs = lax.dynamic_index_in_dim(pair, at["other_" + axis], 0, keepdims=False)
    mine = lax.dynamic_index_in_dim(pair, at[axis], 0, keepdims=False)
    got = lax.ppermute(theirs, axis, [(0, 1), (1, 0)])
    return (mine.astype(F32) + got.astype(F32)).astype(BF16)


def shards(adjacency, block_mask, features, weight, upstream):
    rows, cols = adjacency.shape
    width = features.shape[1]
    nz, nyl, ncore, nx, nyh = (lax.axis_size(a) for a in ("z", "yl", "core", "x", "yh"))
    n_row, n_col = nz * nyl * ncore, nx * nyh
    own = rows // n_col
    at = {a: lax.axis_index(a).astype(jnp.uint32) for a in ("yl", "core", "yh")}
    at.update(other_yl=1 - at["yl"], other_core=1 - at["core"], own_row=at["yh"] * own)
    features, at = lax.optimization_barrier((features, at))

    by_z = gather(features, "z")
    masked = adjacency * jnp.repeat(jnp.repeat(block_mask, TILE, 0), TILE, 1).astype(BF16)
    upstream_x = lax.all_gather(upstream, "yh", axis=0, tiled=True)
    by_z, masked, upstream_x = lax.optimization_barrier((by_z, masked, upstream_x))
    panel = gather(gather(by_z, "yl"), "core")
    panel = panel.transpose(2, 1, 0, 3, 4).reshape(cols, width)

    partial = jnp.dot(masked, panel, preferred_element_type=F32).astype(BF16)
    over_x = exchange(partial.reshape(nx, rows // nx, width), "x")
    agg_x = gather(over_x.astype(F32).sum(0).astype(BF16), "yh").astype(F32).sum(0).astype(BF16)
    pre = jnp.dot(agg_x, weight, preferred_element_type=F32)
    sigma = jax.nn.sigmoid(pre)
    output_x = (pre * sigma).astype(BF16)
    dpre_x = (upstream_x.astype(F32) * sigma * (1.0 + pre * (1.0 - sigma))).astype(BF16)

    w = lax.dot_general(agg_x, dpre_x, (((0,), (0,)), ((), ())), preferred_element_type=F32)
    slab = width // n_col
    w = w.reshape(nx, nyl, nyh, slab // nyl, width)
    w = lax.dynamic_index_in_dim(w, at["yh"], axis=2, keepdims=False).reshape(nx, slab, width)
    dpre_x = jnp.broadcast_to(dpre_x[None], (nx,) + dpre_x.shape)
    both = exchange(jnp.concatenate([dpre_x, w.astype(BF16)], axis=1), "x")
    dpre_all = both[:, : rows // nx].reshape(rows, width)
    w = both[:, rows // nx :].astype(F32).sum(0).astype(BF16)

    chunk, piece = cols // n_row, slab // (ncore * nyl)
    w = exchange(w.reshape(nyl * ncore, piece, width), ("yl", "core")).astype(F32).sum(0).astype(BF16)
    w, output_x = lax.optimization_barrier((w, output_x))
    output = lax.dynamic_slice_in_dim(output_x, at["own_row"], own, axis=0)
    w = gather(w, "z").astype(F32).sum(0) * (rows * n_row) ** (-0.5)
    w = w.astype(BF16)

    grad_in = lax.dot_general(
        dpre_all, weight, (((1,), (1,)), ((), ())), preferred_element_type=F32
    ).astype(BF16)
    partial_fg = lax.dot_general(masked, grad_in, (((0,), (0,)), ((), ())), preferred_element_type=F32)
    fg = partial_fg.astype(BF16).reshape(nz, nyl, ncore, chunk, width).transpose(2, 1, 0, 3, 4)
    fg = halve(fg, "core", at)
    fg = halve(fg, "yl", at)
    fg, w, output = lax.optimization_barrier((fg, w, output))
    feature_grad = exchange(fg, "z").astype(F32).sum(0)

    w = lax.all_gather(w, "core", axis=0, tiled=True)
    w = lax.all_gather(w, ("yl", "yh"), axis=0, tiled=True)
    w, feature_grad = lax.optimization_barrier((w, feature_grad))
    w = gather(w, "x")
    return (output, feature_grad, w.astype(F32).reshape(width, width))


def solution(mesh):
    fine = Mesh(mesh.devices.reshape(16, 2, 2, 4, 4), ("z", "yl", "core", "x", "yh"))
    row, col = ("z", "yl", "core"), ("x", "yh")
    return jax.shard_map(
        shards,
        mesh=fine,
        in_specs=(P(row, col), P(row, col), P(col + row, None), P(), P(row + col, None)),
        out_specs=(P(row + col, None), P(col + row, None), P()),
        check_vma=False,
    )
```

time: 185 us -> 194 us (1.049)
  the two profiles are of different devices: /device:TPU:1 before, /device:TPU:8 now
where the time goes in v6:
time: 194 us; the launch traced here: 193 us
  blocking collectives  125 us (64%)
  starting transfers between devices  43.6 us (22%)
  waiting for transfers between devices  9.9 us (5%)
  local copies, waits for them, and re-layouts  6.54 us (3%)
  other arithmetic  4.13 us (2%)
  matrix products  3.43 us (2%)
    all_to_all x7, blocking collectives, exchange(): return lax.all_to_all(chunks, axis, split_axis=0, concat_axis=0, tiled=True)  75.4 us
    all_to_all x3, starting transfers between devices, exchange(): return lax.all_to_all(chunks, axis, split_axis=0, concat_axis=0, tiled=True)  37.7 us
    all_gather x1, blocking collectives, shards(): w = lax.all_gather(w, ('yl', 'yh'), axis=0, tiled=True)  32.2 us
    all_gather x1, blocking collectives, shards(): upstream_x = lax.all_gather(upstream, 'yh', axis=0, tiled=True)  15.4 us
    all_to_all x3, waiting for transfers between devices, exchange(): return lax.all_to_all(chunks, axis, split_axis=0, concat_axis=0, tiled=True)  9.89 us
    ppermute x2, starting transfers between devices, halve(): got = lax.ppermute(theirs, axis, [(0, 1), (1, 0)])  5.83 us
  transfers between devices with their start and end apart: 5, of which 1 were waited for; matrix products, arithmetic and copies ran while one was open for 2% of the time, Pallas kernels for 0%

profile of v6, /device:TPU:8, one launch (start us, length us, event | category | flops | bytes accessed | tf_op | source)
XLA Modules:
  0.0 193.3 jit_solution(886587158401100324)
XLA Ops:
  0.7 1.5 broadcast_in_dim.18
  2.2 18.9 %all-to-all-start = ((bf16[16,16,512]{2,1,0:T(8,128)(2,1)}), bf16[16,16,512]{2,1,0:T(8,128)(2,1)S(1)}, u32[]{:S(2)}, u32[]{:S(2)}) async-start(bf16[16,16,512]{2,1,0:T(8,128)(2,1)} %broadcast_in_dim.18), calls=%async_computation | async-start | bytes 524288 | tf_op jit(solution)/shard_map/all_to_all | solution.py:12
  21.7 0.7 broadcast_in_dim.20
  22.7 1.0 copy-done.1
  24.4 15.4 %all_gather.9 = bf16[128,512]{1,0:T(8,128)(2,1)S(1)} all-gather(bf16[32,512]{1,0:T(8,128)(2,1)S(1)} %copy-done.2), channel_id=1, replica_groups=mesh['z'=16,'yl'=2,'core'=2,'x'=4,'yh'=4] {'yh'}, dimensions={0}, use_global_device_ids=true | all-gather | bytes 163840 | tf_op jit(solution)/shard_map/all_gather | solution.py:39
  39.9 8.1 %all_to_all.50 = bf16[2,16,16,512]{3,2,1,0:T(8,128)(2,1)S(1)} all-to-all(bf16[2,16,16,512]{3,2,1,0:T(8,128)(2,1)S(1)} %broadcast_in_dim.21), channel_id=1, replica_groups=mesh['z'=16,'yl'=2,'core'=2,'x'=4,'yh'=4] {'yl'}, dimensions={0} | all-to-all | bytes 1048576 | tf_op jit(solution)/shard_map/all_to_all | solution.py:12
  48.2 4.6 %all_to_all.51 = bf16[2,2,16,16,512]{4,3,1,2,0:T(8,128)(2,1)S(1)} all-to-all(bf16[2,2,16,16,512]{4,3,1,2,0:T(8,128)(2,1)S(1)} %broadcast_in_dim.22), channel_id=1, replica_groups=mesh['z'=16,'yl'=2,'core'=2,'x'=4,'yh'=4] {'core'}, dimensions={0} | all-to-all | bytes 2097152 | tf_op jit(solution)/shard_map/all_to_all | solution.py:12
  52.9 0.7 convolution_convert_fusion.2
  53.6 13.9 %all_to_all.52 = bf16[4,128,512]{2,1,0:T(8,128)(2,1)S(1)} all-to-all(bf16[4,128,512]{2,1,0:T(8,128)(2,1)S(1)} %bitcast.53), channel_id=1, replica_groups=mesh['z'=16,'yl'=2,'core'=2,'x'=4,'yh'=4] {'x'}, dimensions={0} | all-to-all | bytes 1048576 | tf_op jit(solution)/shard_map/all_to_all | solution.py:12
  67.6 19.5 %all_to_all.53 = bf16[4,128,512]{2,1,0:T(8,128)(2,1)S(1)} all-to-all(bf16[4,128,512]{2,1,0:T(8,128)(2,1)S(1)} %broadcast_in_dim.23), channel_id=1, replica_groups=mesh['z'=16,'yl'=2,'core'=2,'x'=4,'yh'=4] {'yh'}, dimensions={0} | all-to-all | bytes 1048576 | tf_op jit(solution)/shard_map/all_to_all | solution.py:12
  88.1 11.2 %all_to_all.54 = bf16[4,160,512]{2,1,0:T(8,128)(2,1)S(1)} all-to-all(bf16[4,160,512]{2,1,0:T(8,128)(2,1)S(1)} %pad_maximum_fusion), channel_id=1, replica_groups=mesh['z'=16,'yl'=2,'core'=2,'x'=4,'yh'=4] {'x'}, dimensions={0} | all-to-all | bytes 1310720 | tf_op jit(solution)/shard_map/all_to_all | solution.py:12
  99.3 0.8 slice.8
  100.1 2.1 %convolution_convert_fusion = bf16[1024,512]{1,0:T(8,128)(2,1)S(1)} fusion(bf16[512,1024]{1,0:T(8,128)(2,1)S(1)} %mul.25, bf16[512,512]{1,0:T(8,128)(2,1)} %bitcast.54, bf16[512,512]{1,0:T(8,128)(2,1)S(1)} %copy-done), kind=kOutput, calls=%fused_computation | convolution fusion | flops 806092800 | bytes 3145728 | tf_op jit(solution)/shard_map/dot_general | solution.py:71
  102.3 1.9 collective-permute-start
  104.2 7.7 %all_to_all.55 = bf16[4,8,512]{2,1,0:T(8,128)(2,1)S(1)} all-to-all(bf16[4,8,512]{2,1,0:T(8,128)(2,1)S(1)} %bitcast.57), channel_id=1, replica_groups=mesh['z'=16,'yl'=2,'core'=2,'x'=4,'yh'=4] {'yl','core'}, dimensions={0} | all-to-all | bytes 65536 | tf_op jit(solution)/shard_map/all_to_all | solution.py:12
  112.6 11.2 %all-to-all-start.7 = ((bf16[16,8,512]{2,1,0:T(8,128)(2,1)}), bf16[16,8,512]{2,1,0:T(8,128)(2,1)S(1)}, u32[]{:S(2)}, u32[]{:S(2)}) async-start(bf16[16,8,512]{2,1,0:T(8,128)(2,1)} %broadcast_in_dim.25), calls=%async_computation.7 | async-start | bytes 262144 | tf_op jit(solution)/shard_map/all_to_all | solution.py:12
  124.6 3.9 %collective-permute-start.1 = (bf16[16,16,512]{2,1,0:T(8,128)(2,1)S(1)}, bf16[16,16,512]{2,1,0:T(8,128)(2,1)S(1)}, u32[]{:S(2)}, u32[]{:S(2)}) collective-permute-start(bf16[16,16,512]{2,1,0:T(8,128)(2,1)S(1)} %dynamic-slice_bitcast_fusion.1), channel_id=1, source_target_pairs={{0,32},{32,0},{1,33},{33,1},{2,34},{34,2},{3,35},{35,3},{4,36},{36... | collective-permute-start | bytes 786440 | tf_op jit(solution)/shard_map/ppermute | solution.py:23
  128.5 9.9 %all-to-all-done.7 = bf16[16,8,512]{2,1,0:T(8,128)(2,1)S(1)} async-done(((bf16[16,8,512]{2,1,0:T(8,128)(2,1)}), bf16[16,8,512]{2,1,0:T(8,128)(2,1)S(1)}, u32[]{:S(2)}, u32[]{:S(2)}) %all-to-all-start.7) | async-done | bytes 131104 | tf_op jit(solution)/shard_map/all_to_all | solution.py:12
  138.5 0.8 fusion.1
  139.3 7.7 %all-to-all-start.8 = ((bf16[16,16,512]{2,1,0:T(8,128)(2,1)}), bf16[16,16,512]{2,1,0:T(8,128)(2,1)S(1)}, u32[]{:S(2)}, u32[]{:S(2)}) async-start(bf16[16,16,512]{2,1,0:T(8,128)(2,1)} %fusion.1), calls=%async_computation.8 | async-start | bytes 524288 | tf_op jit(solution)/shard_map/all_to_all | solution.py:12
  147.0 1.8 all_gather.10
  148.8 32.2 %all_gather.11 = bf16[128,512]{1,0:T(8,128)(2,1)S(1)} all-gather(bf16[16,512]{1,0:T(8,128)(2,1)S(1)} %all_gather.10), channel_id=1, replica_groups=mesh['z'=16,'yl'=2,'core'=2,'x'=4,'yh'=4] {'yl','yh'}, dimensions={0}, use_global_device_ids=true | all-gather | bytes 147456 | tf_op jit(solution)/shard_map/all_gather | solution.py:79
  181.7 10.5 %all_to_all.56 = bf16[4,128,512]{2,1,0:T(8,128)(2,1)S(1)} all-to-all(bf16[4,128,512]{2,1,0:T(8,128)(2,1)S(1)} %broadcast_in_dim.26), channel_id=1, replica_groups=mesh['z'=16,'yl'=2,'core'=2,'x'=4,'yh'=4] {'x'}, dimensions={0} | all-to-all | bytes 1048576 | tf_op jit(solution)/shard_map/all_to_all | solution.py:12
  192.2 1.1 bitcast_convert_fusion
  (37 shorter events, 5.3 us)
Async XLA Ops:
  0.6 86.7 %copy-start = (bf16[512,512]{1,0:T(8,128)(2,1)S(1)}, bf16[512,512]{1,0:T(8,128)(2,1)}, u32[]{:S(2)}) copy-start(bf16[512,512]{1,0:T(8,128)(2,1)} %param.8) | copy-start | bytes 1572868
  2.2 37.7 %all-to-all-start = ((bf16[16,16,512]{2,1,0:T(8,128)(2,1)}), bf16[16,16,512]{2,1,0:T(8,128)(2,1)S(1)}, u32[]{:S(2)}, u32[]{:S(2)}) async-start(bf16[16,16,512]{2,1,0:T(8,128)(2,1)} %broadcast_in_dim.18), calls=%async_computation | async-start | bytes 524288 | tf_op jit(solution)/shard_map/all_to_all | solution.py:12
  22.5 1.2 copy-start.1
  23.7 0.8 copy-start.2
  102.3 22.1 %collective-permute-start = (bf16[2,16,16,512]{3,2,0,1:T(8,128)(2,1)S(1)}, bf16[2,16,16,512]{3,2,0,1:T(8,128)(2,1)S(1)}, u32[]{:S(2)}, u32[]{:S(2)}) collective-permute-start(bf16[2,16,16,512]{3,2,0,1:T(8,128)(2,1)S(1)} %dynamic-slice_bitcast_fusion), channel_id=1, source_target_pairs={{0,16},{16,0},{1,17},{17,1},{2,18},{18,2},{3,19},{19,3},{4,20},{20... | collective-permute-start | bytes 1572872 | tf_op jit(solution)/shard_map/ppermute | solution.py:23
  112.6 25.8 %all-to-all-start.7 = ((bf16[16,8,512]{2,1,0:T(8,128)(2,1)}), bf16[16,8,512]{2,1,0:T(8,128)(2,1)S(1)}, u32[]{:S(2)}, u32[]{:S(2)}) async-start(bf16[16,8,512]{2,1,0:T(8,128)(2,1)} %broadcast_in_dim.25), calls=%async_computation.7 | async-start | bytes 262144 | tf_op jit(solution)/shard_map/all_to_all | solution.py:12
  124.6 13.8 %collective-permute-start.1 = (bf16[16,16,512]{2,1,0:T(8,128)(2,1)S(1)}, bf16[16,16,512]{2,1,0:T(8,128)(2,1)S(1)}, u32[]{:S(2)}, u32[]{:S(2)}) collective-permute-start(bf16[16,16,512]{2,1,0:T(8,128)(2,1)S(1)} %dynamic-slice_bitcast_fusion.1), channel_id=1, source_target_pairs={{0,32},{32,0},{1,33},{33,1},{2,34},{34,2},{3,35},{35,3},{4,36},{36... | collective-permute-start | bytes 786440 | tf_op jit(solution)/shard_map/ppermute | solution.py:23
  139.3 41.8 %all-to-all-start.8 = ((bf16[16,16,512]{2,1,0:T(8,128)(2,1)}), bf16[16,16,512]{2,1,0:T(8,128)(2,1)S(1)}, u32[]{:S(2)}, u32[]{:S(2)}) async-start(bf16[16,16,512]{2,1,0:T(8,128)(2,1)} %fusion.1), calls=%async_computation.8 | async-start | bytes 524288 | tf_op jit(solution)/shard_map/all_to_all | solution.py:12

commit v7 on v6

v7 whole, which is shorter than its diff:
```python
import jax
import jax.numpy as jnp
from jax import lax
from jax.sharding import Mesh, PartitionSpec as P

TILE = 256
F32 = jnp.float32
BF16 = jnp.bfloat16


def exchange(chunks, axis):
    return lax.all_to_all(chunks, axis, split_axis=0, concat_axis=0, tiled=True)


def gather(block, axis):
    n = lax.axis_size(axis)
    return exchange(jnp.broadcast_to(block[None], (n,) + block.shape), axis)


def shards(adjacency, block_mask, features, weight, upstream):
    rows, cols = adjacency.shape
    width = features.shape[1]
    nz, nyl, ncore, nx, nyh = (lax.axis_size(a) for a in ("z", "yl", "core", "x", "yh"))
    n_row, n_col = nz * nyl * ncore, nx * nyh
    own = rows // n_col
    at = {a: lax.axis_index(a).astype(jnp.uint32) for a in ("yh",)}
    at.update(own_row=at["yh"] * own)
    features, at = lax.optimization_barrier((features, at))

    by_z = gather(features, "z")
    masked = adjacency * jnp.repeat(jnp.repeat(block_mask, TILE, 0), TILE, 1).astype(BF16)
    upstream_x = lax.all_gather(upstream, "yh", axis=0, tiled=True)
    by_z, masked, upstream_x = lax.optimization_barrier((by_z, masked, upstream_x))
    panel = gather(gather(by_z, "yl"), "core")
    panel = panel.transpose(2, 1, 0, 3, 4).reshape(cols, width)

    partial = jnp.dot(masked, panel, preferred_element_type=F32).astype(BF16)
    over_x = exchange(partial.reshape(nx, rows // nx, width), "x")
    agg_x = gather(over_x.astype(F32).sum(0).astype(BF16), "yh").astype(F32).sum(0).astype(BF16)
    pre = jnp.dot(agg_x, weight, preferred_element_type=F32)
    sigma = jax.nn.sigmoid(pre)
    output_x = (pre * sigma).astype(BF16)
    dpre_x = (upstream_x.astype(F32) * sigma * (1.0 + pre * (1.0 - sigma))).astype(BF16)

    w = lax.dot_general(agg_x, dpre_x, (((0,), (0,)), ((), ())), preferred_element_type=F32)
    slab = width // n_col
    chunk, piece = cols // n_row, slab // (ncore * nyl)
    w = w.astype(BF16).reshape(nx, nyl * ncore, nyh, piece, width)
    w = lax.dynamic_index_in_dim(w, at["yh"], axis=2, keepdims=False).reshape(nx, slab, width)
    output = lax.dynamic_slice_in_dim(output_x, at["own_row"], own, axis=0)
    w, dpre_x, output = lax.optimization_barrier((w, dpre_x, output))
    dpre_x = jnp.broadcast_to(dpre_x[None], (nx,) + dpre_x.shape)
    both = exchange(jnp.concatenate([dpre_x, w], axis=1), "x")
    dpre_all = both[:, : rows // nx].reshape(rows, width)
    w = both[:, rows // nx :].astype(F32).sum(0).astype(BF16)

    grad_in = lax.dot_general(
        dpre_all, weight, (((1,), (1,)), ((), ())), preferred_element_type=F32
    ).astype(BF16)
    partial_fg = lax.dot_general(masked, grad_in, (((0,), (0,)), ((), ())), preferred_element_type=F32)
    fg = partial_fg.astype(BF16).reshape(nz, nyl, ncore, chunk, width).transpose(2, 1, 0, 3, 4)
    fg = fg.reshape(ncore, nyl * nz * chunk, width)
    w = w.reshape(nyl, ncore, piece, width).transpose(1, 0, 2, 3).reshape(ncore, nyl * piece, width)
    both = exchange(jnp.concatenate([fg, w], axis=1), "core").astype(F32).sum(0).astype(BF16)
    fg = both[: nyl * nz * chunk].reshape(nyl, nz * chunk, width)
    w = both[nyl * nz * chunk :].reshape(nyl, piece, width)
    both = exchange(jnp.concatenate([fg, w], axis=1), "yl").astype(F32).sum(0).astype(BF16)
    fg = both[: nz * chunk].reshape(nz, chunk, width)
    w = jnp.broadcast_to(both[nz * chunk :][None], (nz, piece, width))
    both = exchange(jnp.concatenate([fg, w], axis=1), "z").astype(F32).sum(0)
    w = (both[chunk:] * (rows * n_row) ** (-0.5)).astype(BF16)
    feature_grad, w = lax.optimization_barrier((both[:chunk], w))

    w = gather(w, ("yl", "core", "yh")).reshape(slab * nyh, width)
    w = gather(w, "x").reshape(width, width)
    return (output, feature_grad, w.astype(F32))


def solution(mesh):
    fine = Mesh(mesh.devices.reshape(16, 2, 2, 4, 4), ("z", "yl", "core", "x", "yh"))
    row, col = ("z", "yl", "core"), ("x", "yh")
    return jax.shard_map(
        shards,
        mesh=fine,
        in_specs=(P(row, col), P(row, col), P(col + row, None), P(), P(row + col, None)),
        out_specs=(P(row + col, None), P(col + row, None), P()),
        check_vma=False,
    )
```

time: 194 us -> 187 us (0.964)
  the two profiles are of different devices: /device:TPU:8 before, /device:TPU:1 now
where the time goes in v7:
time: 187 us; the launch traced here: 186 us
  blocking collectives  152 us (81%)
  starting transfers between devices  19.4 us (10%)
  local copies, waits for them, and re-layouts  5.83 us (3%)
  other arithmetic  3.9 us (2%)
  matrix products  3.46 us (2%)
    all_to_all x10, blocking collectives, exchange(): return lax.all_to_all(chunks, axis, split_axis=0, concat_axis=0, tiled=True)  138 us
    all_to_all x1, starting transfers between devices, exchange(): return lax.all_to_all(chunks, axis, split_axis=0, concat_axis=0, tiled=True)  19.4 us
    all_gather x1, blocking collectives, shards(): upstream_x = lax.all_gather(upstream, 'yh', axis=0, tiled=True)  14.3 us
  transfers between devices with their start and end apart: 1, of which 0 were waited for; matrix products, arithmetic and copies ran while one was open for 1% of the time, Pallas kernels for 0%

profile of v7, /device:TPU:1, one launch (start us, length us, event | category | flops | bytes accessed | tf_op | source)
XLA Modules:
  0.0 185.8 jit_solution(1634418831495765278)
XLA Ops:
  0.6 1.5 broadcast_in_dim.22
  2.2 19.4 %all-to-all-start = ((bf16[16,16,512]{2,1,0:T(8,128)(2,1)}), bf16[16,16,512]{2,1,0:T(8,128)(2,1)S(1)}, u32[]{:S(2)}, u32[]{:S(2)}) async-start(bf16[16,16,512]{2,1,0:T(8,128)(2,1)} %broadcast_in_dim.22), calls=%async_computation | async-start | bytes 524288 | tf_op jit(solution)/shard_map/all_to_all | solution.py:12
  21.6 0.7 convert_element_type.58
  22.3 0.7 broadcast_in_dim.24
  23.2 1.0 copy-done.1
  24.2 0.4 mul.25
  25.0 14.3 %all_gather.3 = bf16[128,512]{1,0:T(8,128)(2,1)S(1)} all-gather(bf16[32,512]{1,0:T(8,128)(2,1)S(1)} %copy-done.2), channel_id=1, replica_groups=mesh['z'=16,'yl'=2,'core'=2,'x'=4,'yh'=4] {'yh'}, dimensions={0}, use_global_device_ids=true | all-gather | bytes 163840 | tf_op jit(solution)/shard_map/all_gather | solution.py:32
  39.3 7.8 %all_to_all.55 = bf16[2,16,16,512]{3,2,1,0:T(8,128)(2,1)S(1)} all-to-all(bf16[2,16,16,512]{3,2,1,0:T(8,128)(2,1)S(1)} %broadcast_in_dim.25), channel_id=1, replica_groups=mesh['z'=16,'yl'=2,'core'=2,'x'=4,'yh'=4] {'yl'}, dimensions={0} | all-to-all | bytes 1048576 | tf_op jit(solution)/shard_map/all_to_all | solution.py:12
  47.3 8.1 %all_to_all.56 = bf16[2,2,16,16,512]{4,3,1,2,0:T(8,128)(2,1)S(1)} all-to-all(bf16[2,2,16,16,512]{4,3,1,2,0:T(8,128)(2,1)S(1)} %broadcast_in_dim.26), channel_id=1, replica_groups=mesh['z'=16,'yl'=2,'core'=2,'x'=4,'yh'=4] {'core'}, dimensions={0} | all-to-all | bytes 2097152 | tf_op jit(solution)/shard_map/all_to_all | solution.py:12
  55.6 0.7 convolution_convert_fusion.3
  56.3 12.4 %all_to_all.57 = bf16[4,128,512]{2,1,0:T(8,128)(2,1)S(1)} all-to-all(bf16[4,128,512]{2,1,0:T(8,128)(2,1)S(1)} %bitcast.48), channel_id=1, replica_groups=mesh['z'=16,'yl'=2,'core'=2,'x'=4,'yh'=4] {'x'}, dimensions={0} | all-to-all | bytes 1048576 | tf_op jit(solution)/shard_map/all_to_all | solution.py:12
  68.8 19.6 %all_to_all.58 = bf16[4,128,512]{2,1,0:T(8,128)(2,1)S(1)} all-to-all(bf16[4,128,512]{2,1,0:T(8,128)(2,1)S(1)} %broadcast_in_dim.27), channel_id=1, replica_groups=mesh['z'=16,'yl'=2,'core'=2,'x'=4,'yh'=4] {'yh'}, dimensions={0} | all-to-all | bytes 1048576 | tf_op jit(solution)/shard_map/all_to_all | solution.py:12
  89.2 0.6 fusion
  89.9 10.7 %all_to_all.59 = bf16[4,160,512]{2,1,0:T(8,128)(2,1)S(1)} all-to-all(bf16[4,160,512]{2,1,0:T(8,128)(2,1)S(1)} %pad_maximum_fusion.1), channel_id=1, replica_groups=mesh['z'=16,'yl'=2,'core'=2,'x'=4,'yh'=4] {'x'}, dimensions={0} | all-to-all | bytes 1310720 | tf_op jit(solution)/shard_map/all_to_all | solution.py:12
  100.7 0.8 slice.32
  101.5 2.1 %convolution_convert_fusion = bf16[1024,512]{1,0:T(8,128)(2,1)S(1)} fusion(bf16[512,1024]{1,0:T(8,128)(2,1)S(1)} %mul.25, bf16[512,512]{1,0:T(8,128)(2,1)} %bitcast.49, bf16[512,512]{1,0:T(8,128)(2,1)S(1)} %copy-done), kind=kOutput, calls=%fused_computation | convolution fusion | flops 806092800 | bytes 3145728 | tf_op jit(solution)/shard_map/dot_general | solution.py:60
  103.8 7.7 %all_to_all.60 = bf16[2,528,512]{2,1,0:T(8,128)(2,1)S(1)} all-to-all(bf16[2,528,512]{2,1,0:T(8,128)(2,1)S(1)} %pad_maximum_fusion), channel_id=1, replica_groups=mesh['z'=16,'yl'=2,'core'=2,'x'=4,'yh'=4] {'core'}, dimensions={0} | all-to-all | bytes 2162688 | tf_op jit(solution)/shard_map/all_to_all | solution.py:12
  111.5 0.5 reduce_sum.72
  112.2 10.3 %all_to_all.61 = bf16[2,264,512]{2,1,0:T(8,128)(2,1)S(1)} all-to-all(bf16[2,264,512]{2,1,0:T(8,128)(2,1)S(1)} %pad_maximum_fusion.2), channel_id=1, replica_groups=mesh['z'=16,'yl'=2,'core'=2,'x'=4,'yh'=4] {'yl'}, dimensions={0} | all-to-all | bytes 1081344 | tf_op jit(solution)/shard_map/all_to_all | solution.py:12
  122.6 28.3 %all_to_all.62 = bf16[16,24,512]{2,1,0:T(8,128)(2,1)S(1)} all-to-all(bf16[16,24,512]{2,1,0:T(8,128)(2,1)S(1)} %pad_maximum_fusion.3), channel_id=1, replica_groups=mesh['z'=16,'yl'=2,'core'=2,'x'=4,'yh'=4] {'z'}, dimensions={0} | all-to-all | bytes 786432 | tf_op jit(solution)/shard_map/all_to_all | solution.py:12
  151.0 0.6 slice.38
  151.6 20.8 %all_to_all.63 = bf16[16,8,512]{2,1,0:T(8,128)(2,1)S(1)} all-to-all(bf16[16,8,512]{2,1,0:T(8,128)(2,1)S(1)} %broadcast_in_dim.30), channel_id=1, replica_groups=mesh['z'=16,'yl'=2,'core'=2,'x'=4,'yh'=4] {'yl','core','yh'}, dimensions={0} | all-to-all | bytes 262144 | tf_op jit(solution)/shard_map/all_to_all | solution.py:12
  172.4 12.2 %all_to_all.64 = bf16[4,128,512]{2,1,0:T(8,128)(2,1)S(1)} all-to-all(bf16[4,128,512]{2,1,0:T(8,128)(2,1)S(1)} %broadcast_in_dim.32), channel_id=1, replica_groups=mesh['z'=16,'yl'=2,'core'=2,'x'=4,'yh'=4] {'x'}, dimensions={0} | all-to-all | bytes 1048576 | tf_op jit(solution)/shard_map/all_to_all | solution.py:12
  184.6 1.1 bitcast_convert_fusion
  (36 shorter events, 2.3 us)
Async XLA Ops:
  0.6 87.9 %copy-start = (bf16[512,512]{1,0:T(8,128)(2,1)S(1)}, bf16[512,512]{1,0:T(8,128)(2,1)}, u32[]{:S(2)}) copy-start(bf16[512,512]{1,0:T(8,128)(2,1)} %param.8) | copy-start | bytes 1572868
  2.2 37.1 %all-to-all-start = ((bf16[16,16,512]{2,1,0:T(8,128)(2,1)}), bf16[16,16,512]{2,1,0:T(8,128)(2,1)S(1)}, u32[]{:S(2)}, u32[]{:S(2)}) async-start(bf16[16,16,512]{2,1,0:T(8,128)(2,1)} %broadcast_in_dim.22), calls=%async_computation | async-start | bytes 524288 | tf_op jit(solution)/shard_map/all_to_all | solution.py:12
  23.0 1.2 copy-start.1
  24.2 0.8 copy-start.2

commit v8 on v6

--- a/solution.py
+++ b/solution.py
@@ -43,7 +43,8 @@
 
     partial = jnp.dot(masked, panel, preferred_element_type=F32).astype(BF16)
     over_x = exchange(partial.reshape(nx, rows // nx, width), "x")
-    agg_x = gather(over_x.astype(F32).sum(0).astype(BF16), "yh").astype(F32).sum(0).astype(BF16)
+    over_yh = lax.all_gather(over_x.astype(F32).sum(0).astype(BF16), "yh")
+    agg_x = over_yh.astype(F32).sum(0).astype(BF16)
     pre = jnp.dot(agg_x, weight, preferred_element_type=F32)
     sigma = jax.nn.sigmoid(pre)
     output_x = (pre * sigma).astype(BF16)
@@ -51,15 +52,17 @@
 
     w = lax.dot_general(agg_x, dpre_x, (((0,), (0,)), ((), ())), preferred_element_type=F32)
     slab = width // n_col
-    w = w.reshape(nx, nyl, nyh, slab // nyl, width)
+    piece = slab // (ncore * nyl)
+    w = w.reshape(nx, ncore * nyl, nyh, piece, width)
     w = lax.dynamic_index_in_dim(w, at["yh"], axis=2, keepdims=False).reshape(nx, slab, width)
     dpre_x = jnp.broadcast_to(dpre_x[None], (nx,) + dpre_x.shape)
     both = exchange(jnp.concatenate([dpre_x, w.astype(BF16)], axis=1), "x")
     dpre_all = both[:, : rows // nx].reshape(rows, width)
     w = both[:, rows // nx :].astype(F32).sum(0).astype(BF16)
 
-    chunk, piece = cols // n_row, slab // (ncore * nyl)
-    w = exchange(w.reshape(nyl * ncore, piece, width), ("yl", "core")).astype(F32).sum(0).astype(BF16)
+    chunk = cols // n_row
+    w = w.reshape(ncore, nyl, piece, width).transpose(1, 0, 2, 3).reshape(nyl * ncore, piece, width)
+    w = exchange(w, ("yl", "core")).astype(F32).sum(0).astype(BF16)
     w, output_x = lax.optimization_barrier((w, output_x))
     output = lax.dynamic_slice_in_dim(output_x, at["own_row"], own, axis=0)
     w = gather(w, "z").astype(F32).sum(0) * (rows * n_row) ** (-0.5)
@@ -75,8 +78,8 @@
     fg, w, output = lax.optimization_barrier((fg, w, output))
     feature_grad = exchange(fg, "z").astype(F32).sum(0)
 
-    w = lax.all_gather(w, "core", axis=0, tiled=True)
-    w = lax.all_gather(w, ("yl", "yh"), axis=0, tiled=True)
+    for axis in ("yh", "yl", "core"):
+        w = lax.all_gather(w, axis, axis=0, tiled=True)
     w, feature_grad = lax.optimization_barrier((w, feature_grad))
     w = gather(w, "x")
     return (output, feature_grad, w.astype(F32).reshape(width, width))

time: 194 us -> 181 us (0.933)
  the two profiles are of different devices: /device:TPU:8 before, /device:TPU:1 now
where the time goes in v8:
time: 181 us; the launch traced here: 180 us
  blocking collectives  107 us (59%)
  starting transfers between devices  48.3 us (27%)
  waiting for transfers between devices  9.2 us (5%)
  local copies, waits for them, and re-layouts  6.51 us (4%)
  other arithmetic  4.13 us (2%)
  matrix products  3.44 us (2%)
    all_to_all x6, blocking collectives, exchange(): return lax.all_to_all(chunks, axis, split_axis=0, concat_axis=0, tiled=True)  55.6 us
    all_to_all x3, starting transfers between devices, exchange(): return lax.all_to_all(chunks, axis, split_axis=0, concat_axis=0, tiled=True)  39 us
    all_gather x3, blocking collectives, shards(): w = lax.all_gather(w, axis, axis=0, tiled=True)  22.4 us
    all_gather x1, blocking collectives, shards(): over_yh = lax.all_gather(over_x.astype(F32).sum(0).astype(BF16), 'yh')  15.1 us
    all_gather x1, blocking collectives, shards(): upstream_x = lax.all_gather(upstream, 'yh', axis=0, tiled=True)  14.3 us
    ppermute x2, starting transfers between devices, halve(): got = lax.ppermute(theirs, axis, [(0, 1), (1, 0)])  9.3 us
    all_to_all x3, waiting for transfers between devices, exchange(): return lax.all_to_all(chunks, axis, split_axis=0, concat_axis=0, tiled=True)  9.19 us
  transfers between devices with their start and end apart: 5, of which 1 were waited for; matrix products, arithmetic and copies ran while one was open for 2% of the time, Pallas kernels for 0%

profile of v8, /device:TPU:1, one launch (start us, length us, event | category | flops | bytes accessed | tf_op | source)
XLA Modules:
  0.0 179.8 jit_solution(12755573643312699970)
XLA Ops:
  0.7 1.5 broadcast_in_dim.16
  2.2 19.4 %all-to-all-start = ((bf16[16,16,512]{2,1,0:T(8,128)(2,1)}), bf16[16,16,512]{2,1,0:T(8,128)(2,1)S(1)}, u32[]{:S(2)}, u32[]{:S(2)}) async-start(bf16[16,16,512]{2,1,0:T(8,128)(2,1)} %broadcast_in_dim.16), calls=%async_computation | async-start | bytes 524288 | tf_op jit(solution)/shard_map/all_to_all | solution.py:12
  22.3 0.7 broadcast_in_dim.18
  23.2 1.0 copy-done.1
  25.0 14.3 %all_gather.18 = bf16[128,512]{1,0:T(8,128)(2,1)S(1)} all-gather(bf16[32,512]{1,0:T(8,128)(2,1)S(1)} %copy-done.2), channel_id=1, replica_groups=mesh['z'=16,'yl'=2,'core'=2,'x'=4,'yh'=4] {'yh'}, dimensions={0}, use_global_device_ids=true | all-gather | bytes 163840 | tf_op jit(solution)/shard_map/all_gather | solution.py:39
  39.3 7.8 %all_to_all.45 = bf16[2,16,16,512]{3,2,1,0:T(8,128)(2,1)S(1)} all-to-all(bf16[2,16,16,512]{3,2,1,0:T(8,128)(2,1)S(1)} %broadcast_in_dim.19), channel_id=1, replica_groups=mesh['z'=16,'yl'=2,'core'=2,'x'=4,'yh'=4] {'yl'}, dimensions={0} | all-to-all | bytes 1048576 | tf_op jit(solution)/shard_map/all_to_all | solution.py:12
  47.3 8.1 %all_to_all.46 = bf16[2,2,16,16,512]{4,3,1,2,0:T(8,128)(2,1)S(1)} all-to-all(bf16[2,2,16,16,512]{4,3,1,2,0:T(8,128)(2,1)S(1)} %broadcast_in_dim.20), channel_id=1, replica_groups=mesh['z'=16,'yl'=2,'core'=2,'x'=4,'yh'=4] {'core'}, dimensions={0} | all-to-all | bytes 2097152 | tf_op jit(solution)/shard_map/all_to_all | solution.py:12
  56.3 12.4 %all_to_all.47 = bf16[4,128,512]{2,1,0:T(8,128)(2,1)S(1)} all-to-all(bf16[4,128,512]{2,1,0:T(8,128)(2,1)S(1)} %bitcast.58), channel_id=1, replica_groups=mesh['z'=16,'yl'=2,'core'=2,'x'=4,'yh'=4] {'x'}, dimensions={0} | all-to-all | bytes 1048576 | tf_op jit(solution)/shard_map/all_to_all | solution.py:12
  68.8 15.1 %all-gather = bf16[512,512]{1,0:T(8,128)(2,1)S(1)} all-gather(bf16[128,512]{1,0:T(8,128)(2,1)S(1)} %reduce_sum.66), channel_id=2, replica_groups=mesh['z'=16,'yl'=2,'core'=2,'x'=4,'yh'=4] {'yh'}, dimensions={0}, use_global_device_ids=true | all-gather | bytes 655360 | tf_op jit(solution)/shard_map/all_gather | solution.py:46
  84.9 10.0 %all_to_all.48 = bf16[4,160,512]{2,1,0:T(8,128)(2,1)S(1)} all-to-all(bf16[4,160,512]{2,1,0:T(8,128)(2,1)S(1)} %pad_maximum_fusion), channel_id=1, replica_groups=mesh['z'=16,'yl'=2,'core'=2,'x'=4,'yh'=4] {'x'}, dimensions={0} | all-to-all | bytes 1310720 | tf_op jit(solution)/shard_map/all_to_all | solution.py:12
  94.9 0.8 slice.8
  95.7 2.1 %convolution_convert_fusion = bf16[1024,512]{1,0:T(8,128)(2,1)S(1)} fusion(bf16[512,1024]{1,0:T(8,128)(2,1)S(1)} %mul.25, bf16[512,512]{1,0:T(8,128)(2,1)} %bitcast.59, bf16[512,512]{1,0:T(8,128)(2,1)S(1)} %copy-done), kind=kOutput, calls=%fused_computation | convolution fusion | flops 806092800 | bytes 3145728 | tf_op jit(solution)/shard_map/dot_general | solution.py:74
  97.9 7.4 %collective-permute-start = (bf16[2,16,16,512]{3,2,0,1:T(8,128)(2,1)S(1)}, bf16[2,16,16,512]{3,2,0,1:T(8,128)(2,1)S(1)}, u32[]{:S(2)}, u32[]{:S(2)}) collective-permute-start(bf16[2,16,16,512]{3,2,0,1:T(8,128)(2,1)S(1)} %dynamic-slice_bitcast_fusion), channel_id=1, source_target_pairs={{0,16},{16,0},{1,17},{17,1},{2,18},{18,2},{3,19},{19,3},{4,20},{20... | collective-permute-start | bytes 1572872 | tf_op jit(solution)/shard_map/ppermute | solution.py:23
  105.3 5.5 %all_to_all.49 = bf16[4,8,512]{2,1,0:T(8,128)(2,1)S(1)} all-to-all(bf16[4,8,512]{2,1,0:T(8,128)(2,1)S(1)} %bitcast.63), channel_id=1, replica_groups=mesh['z'=16,'yl'=2,'core'=2,'x'=4,'yh'=4] {'yl','core'}, dimensions={0} | all-to-all | bytes 65536 | tf_op jit(solution)/shard_map/all_to_all | solution.py:12
  111.6 10.9 %all-to-all-start.6 = ((bf16[16,8,512]{2,1,0:T(8,128)(2,1)}), bf16[16,8,512]{2,1,0:T(8,128)(2,1)S(1)}, u32[]{:S(2)}, u32[]{:S(2)}) async-start(bf16[16,8,512]{2,1,0:T(8,128)(2,1)} %broadcast_in_dim.22), calls=%async_computation.6 | async-start | bytes 262144 | tf_op jit(solution)/shard_map/all_to_all | solution.py:12
  123.3 1.9 %collective-permute-start.1 = (bf16[16,16,512]{2,1,0:T(8,128)(2,1)S(1)}, bf16[16,16,512]{2,1,0:T(8,128)(2,1)S(1)}, u32[]{:S(2)}, u32[]{:S(2)}) collective-permute-start(bf16[16,16,512]{2,1,0:T(8,128)(2,1)S(1)} %dynamic-slice_bitcast_fusion.1), channel_id=1, source_target_pairs={{0,32},{32,0},{1,33},{33,1},{2,34},{34,2},{3,35},{35,3},{4,36},{36... | collective-permute-start | bytes 786440 | tf_op jit(solution)/shard_map/ppermute | solution.py:23
  125.3 9.2 %all-to-all-done.6 = bf16[16,8,512]{2,1,0:T(8,128)(2,1)S(1)} async-done(((bf16[16,8,512]{2,1,0:T(8,128)(2,1)}), bf16[16,8,512]{2,1,0:T(8,128)(2,1)S(1)}, u32[]{:S(2)}, u32[]{:S(2)}) %all-to-all-start.6) | async-done | bytes 131104 | tf_op jit(solution)/shard_map/all_to_all | solution.py:12
  134.5 0.8 fusion.1
  135.3 8.6 %all-to-all-start.7 = ((bf16[16,16,512]{2,1,0:T(8,128)(2,1)}), bf16[16,16,512]{2,1,0:T(8,128)(2,1)S(1)}, u32[]{:S(2)}, u32[]{:S(2)}) async-start(bf16[16,16,512]{2,1,0:T(8,128)(2,1)} %fusion.1), calls=%async_computation.7 | async-start | bytes 524288 | tf_op jit(solution)/shard_map/all_to_all | solution.py:12
  143.9 11.4 %all_gather.21 = bf16[32,512]{1,0:T(8,128)(2,1)S(1)} all-gather(bf16[8,512]{1,0:T(8,128)(2,1)S(1)} %multiply_convert_fusion.2), channel_id=1, replica_groups=mesh['z'=16,'yl'=2,'core'=2,'x'=4,'yh'=4] {'yh'}, dimensions={0}, use_global_device_ids=true | all-gather | bytes 40960 | tf_op jit(solution)/shard_map/all_gather | solution.py:82
  155.3 3.7 %all_gather.22 = bf16[64,512]{1,0:T(8,128)(2,1)S(1)} all-gather(bf16[32,512]{1,0:T(8,128)(2,1)S(1)} %all_gather.21), channel_id=1, replica_groups=mesh['z'=16,'yl'=2,'core'=2,'x'=4,'yh'=4] {'yl'}, dimensions={0}, use_global_device_ids=true | all-gather | bytes 98304 | tf_op jit(solution)/shard_map/all_gather | solution.py:82
  159.0 7.3 %all_gather.23 = bf16[128,512]{1,0:T(8,128)(2,1)S(1)} all-gather(bf16[64,512]{1,0:T(8,128)(2,1)S(1)} %all_gather.22), channel_id=1, replica_groups=mesh['z'=16,'yl'=2,'core'=2,'x'=4,'yh'=4] {'core'}, dimensions={0}, use_global_device_ids=true | all-gather | bytes 196608 | tf_op jit(solution)/shard_map/all_gather | solution.py:82
  167.0 11.6 %all_to_all.50 = bf16[4,128,512]{2,1,0:T(8,128)(2,1)S(1)} all-to-all(bf16[4,128,512]{2,1,0:T(8,128)(2,1)S(1)} %broadcast_in_dim.23), channel_id=1, replica_groups=mesh['z'=16,'yl'=2,'core'=2,'x'=4,'yh'=4] {'x'}, dimensions={0} | all-to-all | bytes 1048576 | tf_op jit(solution)/shard_map/all_to_all | solution.py:12
  178.7 1.1 bitcast_convert_fusion
  (38 shorter events, 6.0 us)
Async XLA Ops:
  0.6 83.5 %copy-start = (bf16[512,512]{1,0:T(8,128)(2,1)S(1)}, bf16[512,512]{1,0:T(8,128)(2,1)}, u32[]{:S(2)}) copy-start(bf16[512,512]{1,0:T(8,128)(2,1)} %param.8) | copy-start | bytes 1572868
  2.2 37.1 %all-to-all-start = ((bf16[16,16,512]{2,1,0:T(8,128)(2,1)}), bf16[16,16,512]{2,1,0:T(8,128)(2,1)S(1)}, u32[]{:S(2)}, u32[]{:S(2)}) async-start(bf16[16,16,512]{2,1,0:T(8,128)(2,1)} %broadcast_in_dim.16), calls=%async_computation | async-start | bytes 524288 | tf_op jit(solution)/shard_map/all_to_all | solution.py:12
  23.0 1.2 copy-start.1
  24.2 0.8 copy-start.2
  97.9 25.2 %collective-permute-start = (bf16[2,16,16,512]{3,2,0,1:T(8,128)(2,1)S(1)}, bf16[2,16,16,512]{3,2,0,1:T(8,128)(2,1)S(1)}, u32[]{:S(2)}, u32[]{:S(2)}) collective-permute-start(bf16[2,16,16,512]{3,2,0,1:T(8,128)(2,1)S(1)} %dynamic-slice_bitcast_fusion), channel_id=1, source_target_pairs={{0,16},{16,0},{1,17},{17,1},{2,18},{18,2},{3,19},{19,3},{4,20},{20... | collective-permute-start | bytes 1572872 | tf_op jit(solution)/shard_map/ppermute | solution.py:23
  111.6 22.9 %all-to-all-start.6 = ((bf16[16,8,512]{2,1,0:T(8,128)(2,1)}), bf16[16,8,512]{2,1,0:T(8,128)(2,1)S(1)}, u32[]{:S(2)}, u32[]{:S(2)}) async-start(bf16[16,8,512]{2,1,0:T(8,128)(2,1)} %broadcast_in_dim.22), calls=%async_computation.6 | async-start | bytes 262144 | tf_op jit(solution)/shard_map/all_to_all | solution.py:12
  123.3 11.2 %collective-permute-start.1 = (bf16[16,16,512]{2,1,0:T(8,128)(2,1)S(1)}, bf16[16,16,512]{2,1,0:T(8,128)(2,1)S(1)}, u32[]{:S(2)}, u32[]{:S(2)}) collective-permute-start(bf16[16,16,512]{2,1,0:T(8,128)(2,1)S(1)} %dynamic-slice_bitcast_fusion.1), channel_id=1, source_target_pairs={{0,32},{32,0},{1,33},{33,1},{2,34},{34,2},{3,35},{35,3},{4,36},{36... | collective-permute-start | bytes 786440 | tf_op jit(solution)/shard_map/ppermute | solution.py:23
  135.3 31.0 %all-to-all-start.7 = ((bf16[16,16,512]{2,1,0:T(8,128)(2,1)}), bf16[16,16,512]{2,1,0:T(8,128)(2,1)S(1)}, u32[]{:S(2)}, u32[]{:S(2)}) async-start(bf16[16,16,512]{2,1,0:T(8,128)(2,1)} %fusion.1), calls=%async_computation.7 | async-start | bytes 524288 | tf_op jit(solution)/shard_map/all_to_all | solution.py:12

commit v9 on v8

--- a/solution.py
+++ b/solution.py
@@ -53,17 +53,13 @@
     w = lax.dot_general(agg_x, dpre_x, (((0,), (0,)), ((), ())), preferred_element_type=F32)
     slab = width // n_col
     piece = slab // (ncore * nyl)
-    w = w.reshape(nx, ncore * nyl, nyh, piece, width)
-    w = lax.dynamic_index_in_dim(w, at["yh"], axis=2, keepdims=False).reshape(nx, slab, width)
-    dpre_x = jnp.broadcast_to(dpre_x[None], (nx,) + dpre_x.shape)
-    both = exchange(jnp.concatenate([dpre_x, w.astype(BF16)], axis=1), "x")
-    dpre_all = both[:, : rows // nx].reshape(rows, width)
-    w = both[:, rows // nx :].astype(F32).sum(0).astype(BF16)
-
+    w = w.reshape(ncore, nx, nyl, nyh, piece, width)
+    w = lax.dynamic_index_in_dim(w, at["yh"], axis=3, keepdims=False)
+    w = w.transpose(2, 0, 1, 3, 4).reshape(nyl * ncore * nx, piece, width).astype(BF16)
+    w = exchange(w, ("yl", "core", "x")).astype(F32).sum(0).astype(BF16)
+    dpre_all = lax.all_gather(dpre_x, "x", axis=0, tiled=True)
     chunk = cols // n_row
-    w = w.reshape(ncore, nyl, piece, width).transpose(1, 0, 2, 3).reshape(nyl * ncore, piece, width)
-    w = exchange(w, ("yl", "core")).astype(F32).sum(0).astype(BF16)
-    w, output_x = lax.optimization_barrier((w, output_x))
+    w, dpre_all, output_x = lax.optimization_barrier((w, dpre_all, output_x))
     output = lax.dynamic_slice_in_dim(output_x, at["own_row"], own, axis=0)
     w = gather(w, "z").astype(F32).sum(0) * (rows * n_row) ** (-0.5)
     w = w.astype(BF16)
@@ -78,10 +74,10 @@
     fg, w, output = lax.optimization_barrier((fg, w, output))
     feature_grad = exchange(fg, "z").astype(F32).sum(0)
 
-    for axis in ("yh", "yl", "core"):
+    for axis in ("yh", "yl"):
         w = lax.all_gather(w, axis, axis=0, tiled=True)
     w, feature_grad = lax.optimization_barrier((w, feature_grad))
-    w = gather(w, "x")
+    w = lax.all_gather(gather(w, "x").reshape(width // ncore, width), "core", axis=0, tiled=True)
     return (output, feature_grad, w.astype(F32).reshape(width, width))
 
 

time: 181 us -> 179 us (0.989)
  blocking collectives: 107 us -> 101 us
  starting transfers between devices: 48.3 us -> 54.3 us
    all_gather x0 -> x2, blocking collectives: none -> 20 us  [the longest x1 11.8 us: shards(): dpre_all = lax.all_gather(dpre_x, 'x', axis=0, tiled=True)]
    all_to_all x6 -> x4, blocking collectives: 55.6 us -> 36.7 us  [exchange(): return lax.all_to_all(chunks, axis, split_axis=0, concat_axis=0, tiled=True)]
    all_to_all x3 -> x4, starting transfers between devices: 39 us -> 47 us  [exchange(): return lax.all_to_all(chunks, axis, split_axis=0, concat_axis=0, tiled=True)]
    all_gather x3 -> x2, blocking collectives: 22.4 us -> 15 us  [shards(): w = lax.all_gather(w, axis, axis=0, tiled=True)]
    ppermute x2, starting transfers between devices: 9.3 us -> 7.3 us  [halve(): got = lax.ppermute(theirs, axis, [(0, 1), (1, 0)])]
    all_to_all x3 -> x4, waiting for transfers between devices: 9.19 us -> 8.72 us  [exchange(): return lax.all_to_all(chunks, axis, split_axis=0, concat_axis=0, tiled=True)]
  transfers between devices with their start and end apart: 5 -> 6, of which waited for: 1 -> 1; matrix products, arithmetic and copies ran while one was open for 2% -> 2% of each run, Pallas kernels for 0% -> 0%
where the time goes in v9:
time: 179 us; the launch traced here: 178 us
  blocking collectives  101 us (56%)
  starting transfers between devices  54.3 us (30%)
  waiting for transfers between devices  8.72 us (5%)
  local copies, waits for them, and re-layouts  6.29 us (4%)
  other arithmetic  4.04 us (2%)
  matrix products  2.4 us (1%)
    all_to_all x4, starting transfers between devices, exchange(): return lax.all_to_all(chunks, axis, split_axis=0, concat_axis=0, tiled=True)  47 us
    all_to_all x4, blocking collectives, exchange(): return lax.all_to_all(chunks, axis, split_axis=0, concat_axis=0, tiled=True)  36.7 us
    all_gather x1, blocking collectives, shards(): over_yh = lax.all_gather(over_x.astype(F32).sum(0).astype(BF16), 'yh')  15.1 us
    all_gather x2, blocking collectives, shards(): w = lax.all_gather(w, axis, axis=0, tiled=True)  15 us
    all_gather x1, blocking collectives, shards(): upstream_x = lax.all_gather(upstream, 'yh', axis=0, tiled=True)  14.3 us
    all_gather x1, blocking collectives, shards(): dpre_all = lax.all_gather(dpre_x, 'x', axis=0, tiled=True)  11.8 us
    all_to_all x4, waiting for transfers between devices, exchange(): return lax.all_to_all(chunks, axis, split_axis=0, concat_axis=0, tiled=True)  8.72 us
    all_gather x1, blocking collectives, shards(): lax.all_gather(gather(w, 'x').reshape(width // ncore, width), 'core', axi...  8.24 us
  transfers between devices with their start and end apart: 6, of which 1 were waited for; matrix products, arithmetic and copies ran while one was open for 2% of the time, Pallas kernels for 0%

profile of v9, /device:TPU:1, one launch (start us, length us, event | category | flops | bytes accessed | tf_op | source)
XLA Modules:
  0.0 177.7 jit_solution(7216491160323732416)
XLA Ops:
  0.7 1.5 broadcast_in_dim.14
  2.2 19.4 %all-to-all-start = ((bf16[16,16,512]{2,1,0:T(8,128)(2,1)}), bf16[16,16,512]{2,1,0:T(8,128)(2,1)S(1)}, u32[]{:S(2)}, u32[]{:S(2)}) async-start(bf16[16,16,512]{2,1,0:T(8,128)(2,1)} %broadcast_in_dim.14), calls=%async_computation | async-start | bytes 524288 | tf_op jit(solution)/shard_map/all_to_all | solution.py:12
  22.3 0.7 broadcast_in_dim.16
  23.2 1.0 copy-done.1
  25.0 14.3 %all_gather.21 = bf16[128,512]{1,0:T(8,128)(2,1)S(1)} all-gather(bf16[32,512]{1,0:T(8,128)(2,1)S(1)} %copy-done.2), channel_id=1, replica_groups=mesh['z'=16,'yl'=2,'core'=2,'x'=4,'yh'=4] {'yh'}, dimensions={0}, use_global_device_ids=true | all-gather | bytes 163840 | tf_op jit(solution)/shard_map/all_gather | solution.py:39
  39.3 7.8 %all_to_all.40 = bf16[2,16,16,512]{3,2,1,0:T(8,128)(2,1)S(1)} all-to-all(bf16[2,16,16,512]{3,2,1,0:T(8,128)(2,1)S(1)} %broadcast_in_dim.17), channel_id=1, replica_groups=mesh['z'=16,'yl'=2,'core'=2,'x'=4,'yh'=4] {'yl'}, dimensions={0} | all-to-all | bytes 1048576 | tf_op jit(solution)/shard_map/all_to_all | solution.py:12
  47.3 8.1 %all_to_all.41 = bf16[2,2,16,16,512]{4,3,1,2,0:T(8,128)(2,1)S(1)} all-to-all(bf16[2,2,16,16,512]{4,3,1,2,0:T(8,128)(2,1)S(1)} %broadcast_in_dim.18), channel_id=1, replica_groups=mesh['z'=16,'yl'=2,'core'=2,'x'=4,'yh'=4] {'core'}, dimensions={0} | all-to-all | bytes 2097152 | tf_op jit(solution)/shard_map/all_to_all | solution.py:12
  55.6 0.7 convolution_convert_fusion.2
  56.3 12.4 %all_to_all.42 = bf16[4,128,512]{2,1,0:T(8,128)(2,1)S(1)} all-to-all(bf16[4,128,512]{2,1,0:T(8,128)(2,1)S(1)} %bitcast.55), channel_id=1, replica_groups=mesh['z'=16,'yl'=2,'core'=2,'x'=4,'yh'=4] {'x'}, dimensions={0} | all-to-all | bytes 1048576 | tf_op jit(solution)/shard_map/all_to_all | solution.py:12
  68.8 15.1 %all-gather = bf16[512,512]{1,0:T(8,128)(2,1)S(1)} all-gather(bf16[128,512]{1,0:T(8,128)(2,1)S(1)} %reduce_sum.54), channel_id=2, replica_groups=mesh['z'=16,'yl'=2,'core'=2,'x'=4,'yh'=4] {'yh'}, dimensions={0}, use_global_device_ids=true | all-gather | bytes 655360 | tf_op jit(solution)/shard_map/all_gather | solution.py:46
  85.4 7.7 %all-to-all-start.4 = ((bf16[16,8,512]{2,1,0:T(8,128)(2,1)}), bf16[16,8,512]{2,1,0:T(8,128)(2,1)S(1)}, u32[]{:S(2)}, u32[]{:S(2)}) async-start(bf16[16,8,512]{2,1,0:T(8,128)(2,1)} %bitcast.11), calls=%async_computation.4 | async-start | bytes 262144 | tf_op jit(solution)/shard_map/all_to_all | solution.py:12
  93.1 11.8 %all_gather.24 = bf16[512,512]{1,0:T(8,128)(2,1)S(1)} all-gather(bf16[128,512]{1,0:T(8,128)(2,1)S(1)} %get-tuple-element.40), channel_id=1, replica_groups=mesh['z'=16,'yl'=2,'core'=2,'x'=4,'yh'=4] {'x'}, dimensions={0}, use_global_device_ids=true | all-gather | bytes 655360 | tf_op jit(solution)/shard_map/all_gather | solution.py:60
  104.9 1.1 convolution_convert_fusion
  106.0 4.4 %collective-permute-start = (bf16[2,16,16,512]{3,2,0,1:T(8,128)(2,1)S(1)}, bf16[2,16,16,512]{3,2,0,1:T(8,128)(2,1)S(1)}, u32[]{:S(2)}, u32[]{:S(2)}) collective-permute-start(bf16[2,16,16,512]{3,2,0,1:T(8,128)(2,1)S(1)} %dynamic-slice_bitcast_fusion), channel_id=1, source_target_pairs={{0,16},{16,0},{1,17},{17,1},{2,18},{18,2},{3,19},{19,3},{4,20},{20... | collective-permute-start | bytes 1572872 | tf_op jit(solution)/shard_map/ppermute | solution.py:23
  111.1 10.9 %all-to-all-start.5 = ((bf16[16,8,512]{2,1,0:T(8,128)(2,1)}), bf16[16,8,512]{2,1,0:T(8,128)(2,1)S(1)}, u32[]{:S(2)}, u32[]{:S(2)}) async-start(bf16[16,8,512]{2,1,0:T(8,128)(2,1)} %broadcast_in_dim.19), calls=%async_computation.5 | async-start | bytes 262144 | tf_op jit(solution)/shard_map/all_to_all | solution.py:12
  122.9 2.9 %collective-permute-start.1 = (bf16[16,16,512]{2,1,0:T(8,128)(2,1)S(1)}, bf16[16,16,512]{2,1,0:T(8,128)(2,1)S(1)}, u32[]{:S(2)}, u32[]{:S(2)}) collective-permute-start(bf16[16,16,512]{2,1,0:T(8,128)(2,1)S(1)} %dynamic-slice_bitcast_fusion.1), channel_id=1, source_target_pairs={{0,32},{32,0},{1,33},{33,1},{2,34},{34,2},{3,35},{35,3},{4,36},{36... | collective-permute-start | bytes 786440 | tf_op jit(solution)/shard_map/ppermute | solution.py:23
  125.8 8.7 %all-to-all-done.5 = bf16[16,8,512]{2,1,0:T(8,128)(2,1)S(1)} async-done(((bf16[16,8,512]{2,1,0:T(8,128)(2,1)}), bf16[16,8,512]{2,1,0:T(8,128)(2,1)S(1)}, u32[]{:S(2)}, u32[]{:S(2)}) %all-to-all-start.5) | async-done | bytes 131104 | tf_op jit(solution)/shard_map/all_to_all | solution.py:12
  134.5 0.8 fusion.1
  135.3 9.0 %all-to-all-start.6 = ((bf16[16,16,512]{2,1,0:T(8,128)(2,1)}), bf16[16,16,512]{2,1,0:T(8,128)(2,1)S(1)}, u32[]{:S(2)}, u32[]{:S(2)}) async-start(bf16[16,16,512]{2,1,0:T(8,128)(2,1)} %fusion.1), calls=%async_computation.6 | async-start | bytes 524288 | tf_op jit(solution)/shard_map/all_to_all | solution.py:12
  144.4 11.3 %all_gather.25 = bf16[32,512]{1,0:T(8,128)(2,1)S(1)} all-gather(bf16[8,512]{1,0:T(8,128)(2,1)S(1)} %multiply_convert_fusion.2), channel_id=1, replica_groups=mesh['z'=16,'yl'=2,'core'=2,'x'=4,'yh'=4] {'yh'}, dimensions={0}, use_global_device_ids=true | all-gather | bytes 40960 | tf_op jit(solution)/shard_map/all_gather | solution.py:78
  155.6 3.7 %all_gather.26 = bf16[64,512]{1,0:T(8,128)(2,1)S(1)} all-gather(bf16[32,512]{1,0:T(8,128)(2,1)S(1)} %all_gather.25), channel_id=1, replica_groups=mesh['z'=16,'yl'=2,'core'=2,'x'=4,'yh'=4] {'yl'}, dimensions={0}, use_global_device_ids=true | all-gather | bytes 98304 | tf_op jit(solution)/shard_map/all_gather | solution.py:78
  160.0 8.3 %all_to_all.43 = bf16[4,64,512]{2,1,0:T(8,128)(2,1)S(1)} all-to-all(bf16[4,64,512]{2,1,0:T(8,128)(2,1)S(1)} %broadcast_in_dim.20), channel_id=1, replica_groups=mesh['z'=16,'yl'=2,'core'=2,'x'=4,'yh'=4] {'x'}, dimensions={0} | all-to-all | bytes 524288 | tf_op jit(solution)/shard_map/all_to_all | solution.py:12
  168.3 8.2 %all_gather.27 = bf16[512,512]{1,0:T(8,128)(2,1)S(1)} all-gather(bf16[256,512]{1,0:T(8,128)(2,1)S(1)} %bitcast.50), channel_id=1, replica_groups=mesh['z'=16,'yl'=2,'core'=2,'x'=4,'yh'=4] {'core'}, dimensions={0}, use_global_device_ids=true | all-gather | bytes 786432 | tf_op jit(solution)/shard_map/all_gather | solution.py:80
  176.6 1.1 convert_element_type.123
  (35 shorter events, 5.9 us)
Async XLA Ops:
  0.6 83.5 %copy-start = (bf16[512,512]{1,0:T(8,128)(2,1)S(1)}, bf16[512,512]{1,0:T(8,128)(2,1)}, u32[]{:S(2)}) copy-start(bf16[512,512]{1,0:T(8,128)(2,1)} %param.8) | copy-start | bytes 1572868
  2.2 37.1 %all-to-all-start = ((bf16[16,16,512]{2,1,0:T(8,128)(2,1)}), bf16[16,16,512]{2,1,0:T(8,128)(2,1)S(1)}, u32[]{:S(2)}, u32[]{:S(2)}) async-start(bf16[16,16,512]{2,1,0:T(8,128)(2,1)} %broadcast_in_dim.14), calls=%async_computation | async-start | bytes 524288 | tf_op jit(solution)/shard_map/all_to_all | solution.py:12
  23.0 1.2 copy-start.1
  24.2 0.8 copy-start.2
  85.4 19.4 %all-to-all-start.4 = ((bf16[16,8,512]{2,1,0:T(8,128)(2,1)}), bf16[16,8,512]{2,1,0:T(8,128)(2,1)S(1)}, u32[]{:S(2)}, u32[]{:S(2)}) async-start(bf16[16,8,512]{2,1,0:T(8,128)(2,1)} %bitcast.11), calls=%async_computation.4 | async-start | bytes 262144 | tf_op jit(solution)/shard_map/all_to_all | solution.py:12
  106.0 16.7 %collective-permute-start = (bf16[2,16,16,512]{3,2,0,1:T(8,128)(2,1)S(1)}, bf16[2,16,16,512]{3,2,0,1:T(8,128)(2,1)S(1)}, u32[]{:S(2)}, u32[]{:S(2)}) collective-permute-start(bf16[2,16,16,512]{3,2,0,1:T(8,128)(2,1)S(1)} %dynamic-slice_bitcast_fusion), channel_id=1, source_target_pairs={{0,16},{16,0},{1,17},{17,1},{2,18},{18,2},{3,19},{19,3},{4,20},{20... | collective-permute-start | bytes 1572872 | tf_op jit(solution)/shard_map/ppermute | solution.py:23
  111.1 23.4 %all-to-all-start.5 = ((bf16[16,8,512]{2,1,0:T(8,128)(2,1)}), bf16[16,8,512]{2,1,0:T(8,128)(2,1)S(1)}, u32[]{:S(2)}, u32[]{:S(2)}) async-start(bf16[16,8,512]{2,1,0:T(8,128)(2,1)} %broadcast_in_dim.19), calls=%async_computation.5 | async-start | bytes 262144 | tf_op jit(solution)/shard_map/all_to_all | solution.py:12
  122.9 11.6 %collective-permute-start.1 = (bf16[16,16,512]{2,1,0:T(8,128)(2,1)S(1)}, bf16[16,16,512]{2,1,0:T(8,128)(2,1)S(1)}, u32[]{:S(2)}, u32[]{:S(2)}) collective-permute-start(bf16[16,16,512]{2,1,0:T(8,128)(2,1)S(1)} %dynamic-slice_bitcast_fusion.1), channel_id=1, source_target_pairs={{0,32},{32,0},{1,33},{33,1},{2,34},{34,2},{3,35},{35,3},{4,36},{36... | collective-permute-start | bytes 786440 | tf_op jit(solution)/shard_map/ppermute | solution.py:23
  135.3 24.0 %all-to-all-start.6 = ((bf16[16,16,512]{2,1,0:T(8,128)(2,1)}), bf16[16,16,512]{2,1,0:T(8,128)(2,1)S(1)}, u32[]{:S(2)}, u32[]{:S(2)}) async-start(bf16[16,16,512]{2,1,0:T(8,128)(2,1)} %fusion.1), calls=%async_computation.6 | async-start | bytes 524288 | tf_op jit(solution)/shard_map/all_to_all | solution.py:12

commit v10 on v9

--- a/solution.py
+++ b/solution.py
@@ -59,8 +59,6 @@
     w = exchange(w, ("yl", "core", "x")).astype(F32).sum(0).astype(BF16)
     dpre_all = lax.all_gather(dpre_x, "x", axis=0, tiled=True)
     chunk = cols // n_row
-    w, dpre_all, output_x = lax.optimization_barrier((w, dpre_all, output_x))
-    output = lax.dynamic_slice_in_dim(output_x, at["own_row"], own, axis=0)
     w = gather(w, "z").astype(F32).sum(0) * (rows * n_row) ** (-0.5)
     w = w.astype(BF16)
 
@@ -70,6 +68,8 @@
     partial_fg = lax.dot_general(masked, grad_in, (((0,), (0,)), ((), ())), preferred_element_type=F32)
     fg = partial_fg.astype(BF16).reshape(nz, nyl, ncore, chunk, width).transpose(2, 1, 0, 3, 4)
     fg = halve(fg, "core", at)
+    fg, output_x = lax.optimization_barrier((fg, output_x))
+    output = lax.dynamic_slice_in_dim(output_x, at["own_row"], own, axis=0)
     fg = halve(fg, "yl", at)
     fg, w, output = lax.optimization_barrier((fg, w, output))
     feature_grad = exchange(fg, "z").astype(F32).sum(0)

time: 179 us -> 182 us (1.017)
  blocking collectives: 101 us -> 109 us
  starting transfers between devices: 54.3 us -> 50 us
    all_to_all x4 -> x5, blocking collectives: 36.7 us -> 45.2 us  [exchange(): return lax.all_to_all(chunks, axis, split_axis=0, concat_axis=0, tiled=True)]
    all_to_all x4 -> x3, starting transfers between devices: 47 us -> 38.7 us  [exchange(): return lax.all_to_all(chunks, axis, split_axis=0, concat_axis=0, tiled=True)]
    ppermute x2, starting transfers between devices: 7.3 us -> 11.3 us  [halve(): got = lax.ppermute(theirs, axis, [(0, 1), (1, 0)])]
    all_to_all x4 -> x3, waiting for transfers between devices: 8.72 us -> 8.76 us  [exchange(): return lax.all_to_all(chunks, axis, split_axis=0, concat_axis=0, tiled=True)]
  transfers between devices with their start and end apart: 6 -> 5, of which waited for: 1 -> 1; matrix products, arithmetic and copies ran while one was open for 2% -> 2% of each run, Pallas kernels for 0% -> 0%
where the time goes in v10:
time: 182 us; the launch traced here: 181 us
  blocking collectives  109 us (60%)
  starting transfers between devices  50 us (27%)
  waiting for transfers between devices  8.77 us (5%)
  local copies, waits for them, and re-layouts  6.41 us (4%)
  other arithmetic  4.04 us (2%)
  matrix products  2.39 us (1%)
    all_to_all x5, blocking collectives, exchange(): return lax.all_to_all(chunks, axis, split_axis=0, concat_axis=0, tiled=True)  45.2 us
    all_to_all x3, starting transfers between devices, exchange(): return lax.all_to_all(chunks, axis, split_axis=0, concat_axis=0, tiled=True)  38.7 us
    all_gather x1, blocking collectives, shards(): over_yh = lax.all_gather(over_x.astype(F32).sum(0).astype(BF16), 'yh')  15.1 us
    all_gather x2, blocking collectives, shards(): w = lax.all_gather(w, axis, axis=0, tiled=True)  14.8 us
    all_gather x1, blocking collectives, shards(): upstream_x = lax.all_gather(upstream, 'yh', axis=0, tiled=True)  14.3 us
    ppermute x2, starting transfers between devices, halve(): got = lax.ppermute(theirs, axis, [(0, 1), (1, 0)])  11.3 us
    all_gather x1, blocking collectives, shards(): dpre_all = lax.all_gather(dpre_x, 'x', axis=0, tiled=True)  10.6 us
    all_gather x1, blocking collectives, shards(): lax.all_gather(gather(w, 'x').reshape(width // ncore, width), 'core', axi...  8.82 us
  transfers between devices with their start and end apart: 5, of which 1 were waited for; matrix products, arithmetic and copies ran while one was open for 2% of the time, Pallas kernels for 0%

profile of v10, /device:TPU:1, one launch (start us, length us, event | category | flops | bytes accessed | tf_op | source)
XLA Modules:
  0.0 181.3 jit_solution(3111516869730103674)
XLA Ops:
  0.7 1.5 broadcast_in_dim.14
  2.2 19.4 %all-to-all-start = ((bf16[16,16,512]{2,1,0:T(8,128)(2,1)}), bf16[16,16,512]{2,1,0:T(8,128)(2,1)S(1)}, u32[]{:S(2)}, u32[]{:S(2)}) async-start(bf16[16,16,512]{2,1,0:T(8,128)(2,1)} %broadcast_in_dim.14), calls=%async_computation | async-start | bytes 524288 | tf_op jit(solution)/shard_map/all_to_all | solution.py:12
  22.3 0.7 broadcast_in_dim.16
  23.2 1.0 copy-done.1
  25.0 14.3 %all_gather.21 = bf16[128,512]{1,0:T(8,128)(2,1)S(1)} all-gather(bf16[32,512]{1,0:T(8,128)(2,1)S(1)} %copy-done.2), channel_id=1, replica_groups=mesh['z'=16,'yl'=2,'core'=2,'x'=4,'yh'=4] {'yh'}, dimensions={0}, use_global_device_ids=true | all-gather | bytes 163840 | tf_op jit(solution)/shard_map/all_gather | solution.py:39
  39.3 7.8 %all_to_all.40 = bf16[2,16,16,512]{3,2,1,0:T(8,128)(2,1)S(1)} all-to-all(bf16[2,16,16,512]{3,2,1,0:T(8,128)(2,1)S(1)} %broadcast_in_dim.17), channel_id=1, replica_groups=mesh['z'=16,'yl'=2,'core'=2,'x'=4,'yh'=4] {'yl'}, dimensions={0} | all-to-all | bytes 1048576 | tf_op jit(solution)/shard_map/all_to_all | solution.py:12
  47.3 8.1 %all_to_all.41 = bf16[2,2,16,16,512]{4,3,1,2,0:T(8,128)(2,1)S(1)} all-to-all(bf16[2,2,16,16,512]{4,3,1,2,0:T(8,128)(2,1)S(1)} %broadcast_in_dim.18), channel_id=1, replica_groups=mesh['z'=16,'yl'=2,'core'=2,'x'=4,'yh'=4] {'core'}, dimensions={0} | all-to-all | bytes 2097152 | tf_op jit(solution)/shard_map/all_to_all | solution.py:12
  56.3 12.4 %all_to_all.42 = bf16[4,128,512]{2,1,0:T(8,128)(2,1)S(1)} all-to-all(bf16[4,128,512]{2,1,0:T(8,128)(2,1)S(1)} %bitcast.55), channel_id=1, replica_groups=mesh['z'=16,'yl'=2,'core'=2,'x'=4,'yh'=4] {'x'}, dimensions={0} | all-to-all | bytes 1048576 | tf_op jit(solution)/shard_map/all_to_all | solution.py:12
  68.8 15.1 %all-gather = bf16[512,512]{1,0:T(8,128)(2,1)S(1)} all-gather(bf16[128,512]{1,0:T(8,128)(2,1)S(1)} %reduce_sum.54), channel_id=2, replica_groups=mesh['z'=16,'yl'=2,'core'=2,'x'=4,'yh'=4] {'yh'}, dimensions={0}, use_global_device_ids=true | all-gather | bytes 655360 | tf_op jit(solution)/shard_map/all_gather | solution.py:46
  84.5 10.6 %all_gather.24 = bf16[512,512]{1,0:T(8,128)(2,1)S(1)} all-gather(bf16[128,512]{1,0:T(8,128)(2,1)S(1)} %get-tuple-element.38), channel_id=1, replica_groups=mesh['z'=16,'yl'=2,'core'=2,'x'=4,'yh'=4] {'x'}, dimensions={0}, use_global_device_ids=true | all-gather | bytes 655360 | tf_op jit(solution)/shard_map/all_gather | solution.py:60
  95.1 1.1 convolution_convert_fusion
  96.2 0.8 dynamic-slice_bitcast_fusion
  97.0 9.0 %collective-permute-start = (bf16[2,16,16,512]{3,2,0,1:T(8,128)(2,1)}, bf16[2,16,16,512]{3,2,0,1:T(8,128)(2,1)S(1)}, u32[]{:S(2)}, u32[]{:S(2)}) collective-permute-start(bf16[2,16,16,512]{3,2,0,1:T(8,128)(2,1)} %dynamic-slice_bitcast_fusion), channel_id=1, source_target_pairs={{0,16},{16,0},{1,17},{17,1},{2,18},{18,2},{3,19},{19,3},{4,20},{20... | collective-permute-start | bytes 1572872 | tf_op jit(solution)/shard_map/ppermute | solution.py:23
  106.3 8.8 %all_to_all.43 = bf16[16,8,512]{2,1,0:T(8,128)(2,1)S(1)} all-to-all(bf16[16,8,512]{2,1,0:T(8,128)(2,1)S(1)} %bitcast.56), channel_id=1, replica_groups=mesh['z'=16,'yl'=2,'core'=2,'x'=4,'yh'=4] {'yl','core','x'}, dimensions={0} | all-to-all | bytes 262144 | tf_op jit(solution)/shard_map/all_to_all | solution.py:12
  115.8 10.9 %all-to-all-start.5 = ((bf16[16,8,512]{2,1,0:T(8,128)(2,1)}), bf16[16,8,512]{2,1,0:T(8,128)(2,1)S(1)}, u32[]{:S(2)}, u32[]{:S(2)}) async-start(bf16[16,8,512]{2,1,0:T(8,128)(2,1)} %broadcast_in_dim.19), calls=%async_computation.5 | async-start | bytes 262144 | tf_op jit(solution)/shard_map/all_to_all | solution.py:12
  127.0 2.4 %collective-permute-start.1 = (bf16[16,16,512]{2,1,0:T(8,128)(2,1)S(1)}, bf16[16,16,512]{2,1,0:T(8,128)(2,1)S(1)}, u32[]{:S(2)}, u32[]{:S(2)}) collective-permute-start(bf16[16,16,512]{2,1,0:T(8,128)(2,1)S(1)} %dynamic-slice_bitcast_fusion.1), channel_id=1, source_target_pairs={{0,32},{32,0},{1,33},{33,1},{2,34},{34,2},{3,35},{35,3},{4,36},{36... | collective-permute-start | bytes 786440 | tf_op jit(solution)/shard_map/ppermute | solution.py:23
  130.0 8.8 %all-to-all-done.5 = bf16[16,8,512]{2,1,0:T(8,128)(2,1)S(1)} async-done(((bf16[16,8,512]{2,1,0:T(8,128)(2,1)}), bf16[16,8,512]{2,1,0:T(8,128)(2,1)S(1)}, u32[]{:S(2)}, u32[]{:S(2)}) %all-to-all-start.5) | async-done | bytes 131104 | tf_op jit(solution)/shard_map/all_to_all | solution.py:12
  138.8 0.8 fusion.1
  139.6 8.3 %all-to-all-start.6 = ((bf16[16,16,512]{2,1,0:T(8,128)(2,1)}), bf16[16,16,512]{2,1,0:T(8,128)(2,1)S(1)}, u32[]{:S(2)}, u32[]{:S(2)}) async-start(bf16[16,16,512]{2,1,0:T(8,128)(2,1)} %fusion.1), calls=%async_computation.6 | async-start | bytes 524288 | tf_op jit(solution)/shard_map/all_to_all | solution.py:12
  147.9 11.1 %all_gather.25 = bf16[32,512]{1,0:T(8,128)(2,1)S(1)} all-gather(bf16[8,512]{1,0:T(8,128)(2,1)S(1)} %multiply_convert_fusion.2), channel_id=1, replica_groups=mesh['z'=16,'yl'=2,'core'=2,'x'=4,'yh'=4] {'yh'}, dimensions={0}, use_global_device_ids=true | all-gather | bytes 40960 | tf_op jit(solution)/shard_map/all_gather | solution.py:78
  159.0 3.7 %all_gather.26 = bf16[64,512]{1,0:T(8,128)(2,1)S(1)} all-gather(bf16[32,512]{1,0:T(8,128)(2,1)S(1)} %all_gather.25), channel_id=1, replica_groups=mesh['z'=16,'yl'=2,'core'=2,'x'=4,'yh'=4] {'yl'}, dimensions={0}, use_global_device_ids=true | all-gather | bytes 98304 | tf_op jit(solution)/shard_map/all_gather | solution.py:78
  163.4 7.9 %all_to_all.44 = bf16[4,64,512]{2,1,0:T(8,128)(2,1)S(1)} all-to-all(bf16[4,64,512]{2,1,0:T(8,128)(2,1)S(1)} %broadcast_in_dim.20), channel_id=1, replica_groups=mesh['z'=16,'yl'=2,'core'=2,'x'=4,'yh'=4] {'x'}, dimensions={0} | all-to-all | bytes 524288 | tf_op jit(solution)/shard_map/all_to_all | solution.py:12
  171.3 8.8 %all_gather.27 = bf16[512,512]{1,0:T(8,128)(2,1)S(1)} all-gather(bf16[256,512]{1,0:T(8,128)(2,1)S(1)} %bitcast.50), channel_id=1, replica_groups=mesh['z'=16,'yl'=2,'core'=2,'x'=4,'yh'=4] {'core'}, dimensions={0}, use_global_device_ids=true | all-gather | bytes 786432 | tf_op jit(solution)/shard_map/all_gather | solution.py:80
  180.2 1.1 convert_element_type.123
  (34 shorter events, 5.8 us)
Async XLA Ops:
  0.6 83.5 %copy-start = (bf16[512,512]{1,0:T(8,128)(2,1)S(1)}, bf16[512,512]{1,0:T(8,128)(2,1)}, u32[]{:S(2)}) copy-start(bf16[512,512]{1,0:T(8,128)(2,1)} %param.8) | copy-start | bytes 1572868
  2.2 37.1 %all-to-all-start = ((bf16[16,16,512]{2,1,0:T(8,128)(2,1)}), bf16[16,16,512]{2,1,0:T(8,128)(2,1)S(1)}, u32[]{:S(2)}, u32[]{:S(2)}) async-start(bf16[16,16,512]{2,1,0:T(8,128)(2,1)} %broadcast_in_dim.14), calls=%async_computation | async-start | bytes 524288 | tf_op jit(solution)/shard_map/all_to_all | solution.py:12
  23.0 1.2 copy-start.1
  24.2 0.8 copy-start.2
  97.0 29.8 %collective-permute-start = (bf16[2,16,16,512]{3,2,0,1:T(8,128)(2,1)}, bf16[2,16,16,512]{3,2,0,1:T(8,128)(2,1)S(1)}, u32[]{:S(2)}, u32[]{:S(2)}) collective-permute-start(bf16[2,16,16,512]{3,2,0,1:T(8,128)(2,1)} %dynamic-slice_bitcast_fusion), channel_id=1, source_target_pairs={{0,16},{16,0},{1,17},{17,1},{2,18},{18,2},{3,19},{19,3},{4,20},{20... | collective-permute-start | bytes 1572872 | tf_op jit(solution)/shard_map/ppermute | solution.py:23
  115.8 23.0 %all-to-all-start.5 = ((bf16[16,8,512]{2,1,0:T(8,128)(2,1)}), bf16[16,8,512]{2,1,0:T(8,128)(2,1)S(1)}, u32[]{:S(2)}, u32[]{:S(2)}) async-start(bf16[16,8,512]{2,1,0:T(8,128)(2,1)} %broadcast_in_dim.19), calls=%async_computation.5 | async-start | bytes 262144 | tf_op jit(solution)/shard_map/all_to_all | solution.py:12
  127.0 11.8 %collective-permute-start.1 = (bf16[16,16,512]{2,1,0:T(8,128)(2,1)S(1)}, bf16[16,16,512]{2,1,0:T(8,128)(2,1)S(1)}, u32[]{:S(2)}, u32[]{:S(2)}) collective-permute-start(bf16[16,16,512]{2,1,0:T(8,128)(2,1)S(1)} %dynamic-slice_bitcast_fusion.1), channel_id=1, source_target_pairs={{0,32},{32,0},{1,33},{33,1},{2,34},{34,2},{3,35},{35,3},{4,36},{36... | collective-permute-start | bytes 786440 | tf_op jit(solution)/shard_map/ppermute | solution.py:23
  139.6 23.1 %all-to-all-start.6 = ((bf16[16,16,512]{2,1,0:T(8,128)(2,1)}), bf16[16,16,512]{2,1,0:T(8,128)(2,1)S(1)}, u32[]{:S(2)}, u32[]{:S(2)}) async-start(bf16[16,16,512]{2,1,0:T(8,128)(2,1)} %fusion.1), calls=%async_computation.6 | async-start | bytes 524288 | tf_op jit(solution)/shard_map/all_to_all | solution.py:12

commit v11 on v9

--- a/solution.py
+++ b/solution.py
@@ -55,11 +55,15 @@
     piece = slab // (ncore * nyl)
     w = w.reshape(ncore, nx, nyl, nyh, piece, width)
     w = lax.dynamic_index_in_dim(w, at["yh"], axis=3, keepdims=False)
-    w = w.transpose(2, 0, 1, 3, 4).reshape(nyl * ncore * nx, piece, width).astype(BF16)
-    w = exchange(w, ("yl", "core", "x")).astype(F32).sum(0).astype(BF16)
-    dpre_all = lax.all_gather(dpre_x, "x", axis=0, tiled=True)
+    w = w.transpose(1, 2, 0, 3, 4).reshape(nx, slab, width)
+    dpre_x = jnp.broadcast_to(dpre_x[None], (nx,) + dpre_x.shape)
+    both = exchange(jnp.concatenate([dpre_x, w.astype(BF16)], axis=1), "x")
+    dpre_all = jnp.concatenate([both[i, : rows // nx] for i in range(nx)], axis=0)
+    w = both[:, rows // nx :].astype(F32).sum(0).astype(BF16)
+
     chunk = cols // n_row
-    w, dpre_all, output_x = lax.optimization_barrier((w, dpre_all, output_x))
+    w = exchange(w.reshape(nyl * ncore, piece, width), ("yl", "core")).astype(F32).sum(0).astype(BF16)
+    w, output_x = lax.optimization_barrier((w, output_x))
     output = lax.dynamic_slice_in_dim(output_x, at["own_row"], own, axis=0)
     w = gather(w, "z").astype(F32).sum(0) * (rows * n_row) ** (-0.5)
     w = w.astype(BF16)

time: 179 us -> 180 us (level)
  starting transfers between devices: 54.3 us -> 49 us
  blocking collectives: 101 us -> 105 us
    all_to_all x4 -> x6, blocking collectives: 36.7 us -> 51.9 us  [exchange(): return lax.all_to_all(chunks, axis, split_axis=0, concat_axis=0, tiled=True)]
    all_gather x1 -> x0, blocking collectives: 11.8 us -> none  [shards(): dpre_all = lax.all_gather(dpre_x, 'x', axis=0, tiled=True)]
    all_to_all x4 -> x3, starting transfers between devices: 47 us -> 39.7 us  [exchange(): return lax.all_to_all(chunks, axis, split_axis=0, concat_axis=0, tiled=True)]
    ppermute x2, starting transfers between devices: 7.3 us -> 9.31 us  [halve(): got = lax.ppermute(theirs, axis, [(0, 1), (1, 0)])]
    all_to_all x4 -> x3, waiting for transfers between devices: 8.72 us -> 8.42 us  [exchange(): return lax.all_to_all(chunks, axis, split_axis=0, concat_axis=0, tiled=True)]
  transfers between devices with their start and end apart: 6 -> 5, of which waited for: 1 -> 1; matrix products, arithmetic and copies ran while one was open for 2% -> 2% of each run, Pallas kernels for 0% -> 0%
where the time goes in v11:
time: 180 us; the launch traced here: 179 us
  blocking collectives  105 us (58%)
  starting transfers between devices  49 us (27%)
  waiting for transfers between devices  8.42 us (5%)
  local copies, waits for them, and re-layouts  7.17 us (4%)
  other arithmetic  4.09 us (2%)
  matrix products  4.01 us (2%)
    all_to_all x6, blocking collectives, exchange(): return lax.all_to_all(chunks, axis, split_axis=0, concat_axis=0, tiled=True)  51.9 us
    all_to_all x3, starting transfers between devices, exchange(): return lax.all_to_all(chunks, axis, split_axis=0, concat_axis=0, tiled=True)  39.7 us
    all_gather x1, blocking collectives, shards(): over_yh = lax.all_gather(over_x.astype(F32).sum(0).astype(BF16), 'yh')  15.1 us
    all_gather x2, blocking collectives, shards(): w = lax.all_gather(w, axis, axis=0, tiled=True)  15.1 us
    all_gather x1, blocking collectives, shards(): upstream_x = lax.all_gather(upstream, 'yh', axis=0, tiled=True)  14.3 us
    ppermute x2, starting transfers between devices, halve(): got = lax.ppermute(theirs, axis, [(0, 1), (1, 0)])  9.31 us
    all_gather x1, blocking collectives, shards(): lax.all_gather(gather(w, 'x').reshape(width // ncore, width), 'core', axi...  8.69 us
    all_to_all x3, waiting for transfers between devices, exchange(): return lax.all_to_all(chunks, axis, split_axis=0, concat_axis=0, tiled=True)  8.42 us
  transfers between devices with their start and end apart: 5, of which 1 were waited for; matrix products, arithmetic and copies ran while one was open for 2% of the time, Pallas kernels for 0%

profile of v11, /device:TPU:1, one launch (start us, length us, event | category | flops | bytes accessed | tf_op | source)
XLA Modules:
  0.0 178.7 jit_solution(10171999314971132820)
XLA Ops:
  0.7 1.5 broadcast_in_dim.16
  2.2 19.4 %all-to-all-start = ((bf16[16,16,512]{2,1,0:T(8,128)(2,1)}), bf16[16,16,512]{2,1,0:T(8,128)(2,1)S(1)}, u32[]{:S(2)}, u32[]{:S(2)}) async-start(bf16[16,16,512]{2,1,0:T(8,128)(2,1)} %broadcast_in_dim.16), calls=%async_computation | async-start | bytes 524288 | tf_op jit(solution)/shard_map/all_to_all | solution.py:12
  23.2 1.0 copy-done.1
  25.0 14.3 %all_gather.18 = bf16[128,512]{1,0:T(8,128)(2,1)S(1)} all-gather(bf16[32,512]{1,0:T(8,128)(2,1)S(1)} %copy-done.2), channel_id=1, replica_groups=mesh['z'=16,'yl'=2,'core'=2,'x'=4,'yh'=4] {'yh'}, dimensions={0}, use_global_device_ids=true | all-gather | bytes 163840 | tf_op jit(solution)/shard_map/all_gather | solution.py:39
  39.3 7.8 %all_to_all.45 = bf16[2,16,16,512]{3,2,1,0:T(8,128)(2,1)S(1)} all-to-all(bf16[2,16,16,512]{3,2,1,0:T(8,128)(2,1)S(1)} %broadcast_in_dim.19), channel_id=1, replica_groups=mesh['z'=16,'yl'=2,'core'=2,'x'=4,'yh'=4] {'yl'}, dimensions={0} | all-to-all | bytes 1048576 | tf_op jit(solution)/shard_map/all_to_all | solution.py:12
  47.3 8.1 %all_to_all.46 = bf16[2,2,16,16,512]{4,3,1,2,0:T(8,128)(2,1)S(1)} all-to-all(bf16[2,2,16,16,512]{4,3,1,2,0:T(8,128)(2,1)S(1)} %broadcast_in_dim.20), channel_id=1, replica_groups=mesh['z'=16,'yl'=2,'core'=2,'x'=4,'yh'=4] {'core'}, dimensions={0} | all-to-all | bytes 2097152 | tf_op jit(solution)/shard_map/all_to_all | solution.py:12
  56.3 12.4 %all_to_all.47 = bf16[4,128,512]{2,1,0:T(8,128)(2,1)S(1)} all-to-all(bf16[4,128,512]{2,1,0:T(8,128)(2,1)S(1)} %bitcast.64), channel_id=1, replica_groups=mesh['z'=16,'yl'=2,'core'=2,'x'=4,'yh'=4] {'x'}, dimensions={0} | all-to-all | bytes 1048576 | tf_op jit(solution)/shard_map/all_to_all | solution.py:12
  68.8 15.1 %all-gather = bf16[512,512]{1,0:T(8,128)(2,1)S(1)} all-gather(bf16[128,512]{1,0:T(8,128)(2,1)S(1)} %reduce_sum.66), channel_id=2, replica_groups=mesh['z'=16,'yl'=2,'core'=2,'x'=4,'yh'=4] {'yh'}, dimensions={0}, use_global_device_ids=true | all-gather | bytes 655360 | tf_op jit(solution)/shard_map/all_gather | solution.py:46
  84.1 1.0 multiply_convert_fusion
  85.5 10.0 %all_to_all.48 = bf16[4,160,512]{2,1,0:T(8,128)(2,1)S(1)} all-to-all(bf16[4,160,512]{2,1,0:T(8,128)(2,1)S(1)} %pad_maximum_fusion), channel_id=1, replica_groups=mesh['z'=16,'yl'=2,'core'=2,'x'=4,'yh'=4] {'x'}, dimensions={0} | all-to-all | bytes 1310720 | tf_op jit(solution)/shard_map/all_to_all | solution.py:12
  96.3 2.0 %convolution_convert_fusion = bf16[1024,512]{1,0:T(8,128)(2,1)S(1)} fusion(bf16[512,1024]{1,0:T(8,128)(2,1)S(1)} %mul.25, bf16[512,512]{1,0:T(8,128)(2,1)S(1)} %copy-done, bf16[128,512]{1,0:T(8,128)(2,1)S(1)} %get-tuple-element.38, bf16[128,512]{1,0:T(8,128)(2,1)} %get-tuple-element.39, bf16[128,512]{1,0:T(8,128)(2,1)} %get-tuple-element.40, ...), kind=kOutput, calls=%fused_computation | convolution fusion | flops 808189952 | bytes 3145728 | tf_op jit(solution)/shard_map/dot_general | solution.py:74
  98.4 7.4 %collective-permute-start = (bf16[2,16,16,512]{3,2,0,1:T(8,128)(2,1)S(1)}, bf16[2,16,16,512]{3,2,0,1:T(8,128)(2,1)S(1)}, u32[]{:S(2)}, u32[]{:S(2)}) collective-permute-start(bf16[2,16,16,512]{3,2,0,1:T(8,128)(2,1)S(1)} %dynamic-slice_bitcast_fusion), channel_id=1, source_target_pairs={{0,16},{16,0},{1,17},{17,1},{2,18},{18,2},{3,19},{19,3},{4,20},{20... | collective-permute-start | bytes 1572872 | tf_op jit(solution)/shard_map/ppermute | solution.py:23
  105.8 5.5 %all_to_all.49 = bf16[4,8,512]{2,1,0:T(8,128)(2,1)S(1)} all-to-all(bf16[4,8,512]{2,1,0:T(8,128)(2,1)S(1)} %bitcast.67), channel_id=1, replica_groups=mesh['z'=16,'yl'=2,'core'=2,'x'=4,'yh'=4] {'yl','core'}, dimensions={0} | all-to-all | bytes 65536 | tf_op jit(solution)/shard_map/all_to_all | solution.py:12
  112.0 10.9 %all-to-all-start.6 = ((bf16[16,8,512]{2,1,0:T(8,128)(2,1)}), bf16[16,8,512]{2,1,0:T(8,128)(2,1)S(1)}, u32[]{:S(2)}, u32[]{:S(2)}) async-start(bf16[16,8,512]{2,1,0:T(8,128)(2,1)} %broadcast_in_dim.22), calls=%async_computation.6 | async-start | bytes 262144 | tf_op jit(solution)/shard_map/all_to_all | solution.py:12
  123.0 1.4 constant_dynamic-slice_fusion
  124.6 1.9 %collective-permute-start.1 = (bf16[16,16,512]{2,1,0:T(8,128)(2,1)S(1)}, bf16[16,16,512]{2,1,0:T(8,128)(2,1)S(1)}, u32[]{:S(2)}, u32[]{:S(2)}) collective-permute-start(bf16[16,16,512]{2,1,0:T(8,128)(2,1)S(1)} %dynamic-slice_bitcast_fusion.1), channel_id=1, source_target_pairs={{0,32},{32,0},{1,33},{33,1},{2,34},{34,2},{3,35},{35,3},{4,36},{36... | collective-permute-start | bytes 786440 | tf_op jit(solution)/shard_map/ppermute | solution.py:23
  126.5 8.4 %all-to-all-done.6 = bf16[16,8,512]{2,1,0:T(8,128)(2,1)S(1)} async-done(((bf16[16,8,512]{2,1,0:T(8,128)(2,1)}), bf16[16,8,512]{2,1,0:T(8,128)(2,1)S(1)}, u32[]{:S(2)}, u32[]{:S(2)}) %all-to-all-start.6) | async-done | bytes 131104 | tf_op jit(solution)/shard_map/all_to_all | solution.py:12
  135.0 0.8 fusion.15
  135.8 9.4 %all-to-all-start.7 = ((bf16[16,16,512]{2,1,0:T(8,128)(2,1)}), bf16[16,16,512]{2,1,0:T(8,128)(2,1)S(1)}, u32[]{:S(2)}, u32[]{:S(2)}) async-start(bf16[16,16,512]{2,1,0:T(8,128)(2,1)} %fusion.15), calls=%async_computation.7 | async-start | bytes 524288 | tf_op jit(solution)/shard_map/all_to_all | solution.py:12
  145.2 11.4 %all_gather.21 = bf16[32,512]{1,0:T(8,128)(2,1)S(1)} all-gather(bf16[8,512]{1,0:T(8,128)(2,1)S(1)} %multiply_convert_fusion.2), channel_id=1, replica_groups=mesh['z'=16,'yl'=2,'core'=2,'x'=4,'yh'=4] {'yh'}, dimensions={0}, use_global_device_ids=true | all-gather | bytes 40960 | tf_op jit(solution)/shard_map/all_gather | solution.py:82
  156.6 3.7 %all_gather.22 = bf16[64,512]{1,0:T(8,128)(2,1)S(1)} all-gather(bf16[32,512]{1,0:T(8,128)(2,1)S(1)} %all_gather.21), channel_id=1, replica_groups=mesh['z'=16,'yl'=2,'core'=2,'x'=4,'yh'=4] {'yl'}, dimensions={0}, use_global_device_ids=true | all-gather | bytes 98304 | tf_op jit(solution)/shard_map/all_gather | solution.py:82
  161.0 7.9 %all_to_all.50 = bf16[4,64,512]{2,1,0:T(8,128)(2,1)S(1)} all-to-all(bf16[4,64,512]{2,1,0:T(8,128)(2,1)S(1)} %broadcast_in_dim.23), channel_id=1, replica_groups=mesh['z'=16,'yl'=2,'core'=2,'x'=4,'yh'=4] {'x'}, dimensions={0} | all-to-all | bytes 524288 | tf_op jit(solution)/shard_map/all_to_all | solution.py:12
  168.9 8.7 %all_gather.23 = bf16[512,512]{1,0:T(8,128)(2,1)S(1)} all-gather(bf16[256,512]{1,0:T(8,128)(2,1)S(1)} %bitcast.58), channel_id=1, replica_groups=mesh['z'=16,'yl'=2,'core'=2,'x'=4,'yh'=4] {'core'}, dimensions={0}, use_global_device_ids=true | all-gather | bytes 786432 | tf_op jit(solution)/shard_map/all_gather | solution.py:84
  177.6 1.1 convert_element_type.125
  (38 shorter events, 6.5 us)
Async XLA Ops:
  0.6 83.5 %copy-start = (bf16[512,512]{1,0:T(8,128)(2,1)S(1)}, bf16[512,512]{1,0:T(8,128)(2,1)}, u32[]{:S(2)}) copy-start(bf16[512,512]{1,0:T(8,128)(2,1)} %param.8) | copy-start | bytes 1572868
  2.2 37.1 %all-to-all-start = ((bf16[16,16,512]{2,1,0:T(8,128)(2,1)}), bf16[16,16,512]{2,1,0:T(8,128)(2,1)S(1)}, u32[]{:S(2)}, u32[]{:S(2)}) async-start(bf16[16,16,512]{2,1,0:T(8,128)(2,1)} %broadcast_in_dim.16), calls=%async_computation | async-start | bytes 524288 | tf_op jit(solution)/shard_map/all_to_all | solution.py:12
  23.0 1.2 copy-start.1
  24.2 0.8 copy-start.2
  98.4 26.0 %collective-permute-start = (bf16[2,16,16,512]{3,2,0,1:T(8,128)(2,1)S(1)}, bf16[2,16,16,512]{3,2,0,1:T(8,128)(2,1)S(1)}, u32[]{:S(2)}, u32[]{:S(2)}) collective-permute-start(bf16[2,16,16,512]{3,2,0,1:T(8,128)(2,1)S(1)} %dynamic-slice_bitcast_fusion), channel_id=1, source_target_pairs={{0,16},{16,0},{1,17},{17,1},{2,18},{18,2},{3,19},{19,3},{4,20},{20... | collective-permute-start | bytes 1572872 | tf_op jit(solution)/shard_map/ppermute | solution.py:23
  112.0 22.9 %all-to-all-start.6 = ((bf16[16,8,512]{2,1,0:T(8,128)(2,1)}), bf16[16,8,512]{2,1,0:T(8,128)(2,1)S(1)}, u32[]{:S(2)}, u32[]{:S(2)}) async-start(bf16[16,8,512]{2,1,0:T(8,128)(2,1)} %broadcast_in_dim.22), calls=%async_computation.6 | async-start | bytes 262144 | tf_op jit(solution)/shard_map/all_to_all | solution.py:12
  124.6 10.4 %collective-permute-start.1 = (bf16[16,16,512]{2,1,0:T(8,128)(2,1)S(1)}, bf16[16,16,512]{2,1,0:T(8,128)(2,1)S(1)}, u32[]{:S(2)}, u32[]{:S(2)}) collective-permute-start(bf16[16,16,512]{2,1,0:T(8,128)(2,1)S(1)} %dynamic-slice_bitcast_fusion.1), channel_id=1, source_target_pairs={{0,32},{32,0},{1,33},{33,1},{2,34},{34,2},{3,35},{35,3},{4,36},{36... | collective-permute-start | bytes 786440 | tf_op jit(solution)/shard_map/ppermute | solution.py:23
  135.8 24.5 %all-to-all-start.7 = ((bf16[16,16,512]{2,1,0:T(8,128)(2,1)}), bf16[16,16,512]{2,1,0:T(8,128)(2,1)S(1)}, u32[]{:S(2)}, u32[]{:S(2)}) async-start(bf16[16,16,512]{2,1,0:T(8,128)(2,1)} %fusion.15), calls=%async_computation.7 | async-start | bytes 524288 | tf_op jit(solution)/shard_map/all_to_all | solution.py:12

commit v12 on v9

--- a/solution.py
+++ b/solution.py
@@ -1,6 +1,8 @@
 import jax
 import jax.numpy as jnp
 from jax import lax
+from jax.experimental import pallas as pl
+from jax.experimental.pallas import tpu as pltpu
 from jax.sharding import Mesh, PartitionSpec as P
 
 TILE = 256
@@ -24,6 +26,30 @@
     return (mine.astype(F32) + got.astype(F32)).astype(BF16)
 
 
+def mask_rows(mask, adjacency, masked):
+    i = pl.program_id(0)
+    for j in range(adjacency.shape[1] // TILE):
+        tile = pl.ds(j * TILE, TILE)
+        scale = mask[i, j].astype(F32)
+        masked[:, tile] = (adjacency[:, tile].astype(F32) * scale).astype(BF16)
+
+
+def mask_tiles(adjacency, block_mask):
+    rows, cols = adjacency.shape
+    return pl.pallas_call(
+        mask_rows,
+        grid=(rows // TILE,),
+        in_specs=[
+            pl.BlockSpec(memory_space=pltpu.SMEM),
+            pl.BlockSpec((TILE, cols), lambda i: (i, 0)),
+        ],
+        out_specs=pl.BlockSpec((TILE, cols), lambda i: (i, 0)),
+        out_shape=jax.ShapeDtypeStruct((rows, cols), BF16),
+        compiler_params=pltpu.CompilerParams(vmem_limit_bytes=60 * 2**20),
+        cost_estimate=pl.CostEstimate(flops=rows * cols, bytes_accessed=4 * rows * cols, transcendentals=0),
+    )(block_mask, adjacency)
+
+
 def shards(adjacency, block_mask, features, weight, upstream):
     rows, cols = adjacency.shape
     width = features.shape[1]
@@ -35,7 +61,7 @@
     features, at = lax.optimization_barrier((features, at))
 
     by_z = gather(features, "z")
-    masked = adjacency * jnp.repeat(jnp.repeat(block_mask, TILE, 0), TILE, 1).astype(BF16)
+    masked = mask_tiles(adjacency, block_mask)
     upstream_x = lax.all_gather(upstream, "yh", axis=0, tiled=True)
     by_z, masked, upstream_x = lax.optimization_barrier((by_z, masked, upstream_x))
     panel = gather(gather(by_z, "yl"), "core")

time: 179 us -> 178 us (level)
  Pallas kernels: 0 us -> 2.12 us
    pallas_call x0 -> x1, Pallas kernels: none -> 2.12 us  [mask_tiles(): pl.pallas_call(mask_rows, grid=(rows // TILE,), in_specs=[pl.BlockSpec(me...]
  transfers between devices with their start and end apart: 6 -> 6, of which waited for: 1 -> 1; matrix products, arithmetic and copies ran while one was open for 2% -> 1% of each run, Pallas kernels for 0% -> 1%
where the time goes in v12:
time: 178 us; the launch traced here: 177 us
  blocking collectives  102 us (57%)
  starting transfers between devices  53 us (30%)
  waiting for transfers between devices  8.72 us (5%)
  local copies, waits for them, and re-layouts  5.13 us (3%)
  other arithmetic  2.95 us (2%)
  matrix products  2.4 us (1%)
  Pallas kernels  2.12 us (1%)
    all_to_all x4, starting transfers between devices, exchange(): return lax.all_to_all(chunks, axis, split_axis=0, concat_axis=0, tiled=True)  45.7 us
    all_to_all x4, blocking collectives, exchange(): return lax.all_to_all(chunks, axis, split_axis=0, concat_axis=0, tiled=True)  37.1 us
    all_gather x1, blocking collectives, shards(): over_yh = lax.all_gather(over_x.astype(F32).sum(0).astype(BF16), 'yh')  16 us
    all_gather x2, blocking collectives, shards(): w = lax.all_gather(w, axis, axis=0, tiled=True)  15 us
    all_gather x1, blocking collectives, shards(): upstream_x = lax.all_gather(upstream, 'yh', axis=0, tiled=True)  14.2 us
    all_gather x1, blocking collectives, shards(): dpre_all = lax.all_gather(dpre_x, 'x', axis=0, tiled=True)  11.8 us
    all_to_all x4, waiting for transfers between devices, exchange(): return lax.all_to_all(chunks, axis, split_axis=0, concat_axis=0, tiled=True)  8.72 us
    all_gather x1, blocking collectives, shards(): lax.all_gather(gather(w, 'x').reshape(width // ncore, width), 'core', axi...  8.24 us
  transfers between devices with their start and end apart: 6, of which 1 were waited for; matrix products, arithmetic and copies ran while one was open for 1% of the time, Pallas kernels for 1%

profile of v12, /device:TPU:1, one launch (start us, length us, event | category | flops | bytes accessed | tf_op | source)
XLA Modules:
  0.0 177.5 jit_solution(11469718062216352012)
XLA Ops:
  0.7 1.5 broadcast_in_dim.10
  2.1 19.4 %all-to-all-start = ((bf16[16,16,512]{2,1,0:T(8,128)(2,1)}), bf16[16,16,512]{2,1,0:T(8,128)(2,1)S(1)}, u32[]{:S(2)}, u32[]{:S(2)}) async-start(bf16[16,16,512]{2,1,0:T(8,128)(2,1)} %broadcast_in_dim.10), calls=%async_computation | async-start | bytes 524288 | tf_op jit(solution)/shard_map/all_to_all | solution.py:14
  21.6 2.1 %shard_map.76 = bf16[512,1024]{1,0:T(8,128)(2,1)} custom-call(s32[2,4]{1,0:T(2,128)} %mask.1, bf16[512,1024]{1,0:T(8,128)(2,1)} %adjacency.1), custom_call_target="tpu_custom_call" | custom-call | flops 524288 | bytes 2097152 | tf_op jit(solution)/shard_map/pallas_call | solution.py:39
  23.7 14.2 %all_gather.21 = bf16[128,512]{1,0:T(8,128)(2,1)S(1)} all-gather(bf16[32,512]{1,0:T(8,128)(2,1)S(1)} %copy-done.2), channel_id=1, replica_groups=mesh['z'=16,'yl'=2,'core'=2,'x'=4,'yh'=4] {'yh'}, dimensions={0}, use_global_device_ids=true | all-gather | bytes 163840 | tf_op jit(solution)/shard_map/all_gather | solution.py:65
  38.0 7.8 %all_to_all.40 = bf16[2,16,16,512]{3,2,1,0:T(8,128)(2,1)S(1)} all-to-all(bf16[2,16,16,512]{3,2,1,0:T(8,128)(2,1)S(1)} %broadcast_in_dim.11), channel_id=1, replica_groups=mesh['z'=16,'yl'=2,'core'=2,'x'=4,'yh'=4] {'yl'}, dimensions={0} | all-to-all | bytes 1048576 | tf_op jit(solution)/shard_map/all_to_all | solution.py:14
  46.0 8.6 %all_to_all.41 = bf16[2,2,16,16,512]{4,3,1,2,0:T(8,128)(2,1)S(1)} all-to-all(bf16[2,2,16,16,512]{4,3,1,2,0:T(8,128)(2,1)S(1)} %broadcast_in_dim.12), channel_id=1, replica_groups=mesh['z'=16,'yl'=2,'core'=2,'x'=4,'yh'=4] {'core'}, dimensions={0} | all-to-all | bytes 2097152 | tf_op jit(solution)/shard_map/all_to_all | solution.py:14
  54.6 1.1 copy-done.1
  55.8 0.7 convolution_convert_fusion.2
  56.5 12.4 %all_to_all.42 = bf16[4,128,512]{2,1,0:T(8,128)(2,1)S(1)} all-to-all(bf16[4,128,512]{2,1,0:T(8,128)(2,1)S(1)} %bitcast.49), channel_id=1, replica_groups=mesh['z'=16,'yl'=2,'core'=2,'x'=4,'yh'=4] {'x'}, dimensions={0} | all-to-all | bytes 1048576 | tf_op jit(solution)/shard_map/all_to_all | solution.py:14
  69.0 16.0 %all-gather = bf16[512,512]{1,0:T(8,128)(2,1)S(1)} all-gather(bf16[128,512]{1,0:T(8,128)(2,1)S(1)} %reduce_sum.54), channel_id=2, replica_groups=mesh['z'=16,'yl'=2,'core'=2,'x'=4,'yh'=4] {'yh'}, dimensions={0}, use_global_device_ids=true | all-gather | bytes 655360 | tf_op jit(solution)/shard_map/all_gather | solution.py:72
  86.5 7.6 %all-to-all-start.4 = ((bf16[16,8,512]{2,1,0:T(8,128)(2,1)}), bf16[16,8,512]{2,1,0:T(8,128)(2,1)S(1)}, u32[]{:S(2)}, u32[]{:S(2)}) async-start(bf16[16,8,512]{2,1,0:T(8,128)(2,1)} %bitcast.10), calls=%async_computation.4 | async-start | bytes 262144 | tf_op jit(solution)/shard_map/all_to_all | solution.py:14
  94.2 11.8 %all_gather.24 = bf16[512,512]{1,0:T(8,128)(2,1)S(1)} all-gather(bf16[128,512]{1,0:T(8,128)(2,1)S(1)} %get-tuple-element.40), channel_id=1, replica_groups=mesh['z'=16,'yl'=2,'core'=2,'x'=4,'yh'=4] {'x'}, dimensions={0}, use_global_device_ids=true | all-gather | bytes 655360 | tf_op jit(solution)/shard_map/all_gather | solution.py:86
  106.0 1.1 convolution_convert_fusion
  107.1 4.4 %collective-permute-start = (bf16[2,16,16,512]{3,2,0,1:T(8,128)(2,1)S(1)}, bf16[2,16,16,512]{3,2,0,1:T(8,128)(2,1)S(1)}, u32[]{:S(2)}, u32[]{:S(2)}) collective-permute-start(bf16[2,16,16,512]{3,2,0,1:T(8,128)(2,1)S(1)} %dynamic-slice_bitcast_fusion), channel_id=1, source_target_pairs={{0,16},{16,0},{1,17},{17,1},{2,18},{18,2},{3,19},{19,3},{4,20},{20... | collective-permute-start | bytes 1572872 | tf_op jit(solution)/shard_map/ppermute | solution.py:25
  112.2 9.6 %all-to-all-start.5 = ((bf16[16,8,512]{2,1,0:T(8,128)(2,1)}), bf16[16,8,512]{2,1,0:T(8,128)(2,1)S(1)}, u32[]{:S(2)}, u32[]{:S(2)}) async-start(bf16[16,8,512]{2,1,0:T(8,128)(2,1)} %broadcast_in_dim.13), calls=%async_computation.5 | async-start | bytes 262144 | tf_op jit(solution)/shard_map/all_to_all | solution.py:14
  122.8 2.9 %collective-permute-start.1 = (bf16[16,16,512]{2,1,0:T(8,128)(2,1)S(1)}, bf16[16,16,512]{2,1,0:T(8,128)(2,1)S(1)}, u32[]{:S(2)}, u32[]{:S(2)}) collective-permute-start(bf16[16,16,512]{2,1,0:T(8,128)(2,1)S(1)} %dynamic-slice_bitcast_fusion.1), channel_id=1, source_target_pairs={{0,32},{32,0},{1,33},{33,1},{2,34},{34,2},{3,35},{35,3},{4,36},{36... | collective-permute-start | bytes 786440 | tf_op jit(solution)/shard_map/ppermute | solution.py:25
  125.6 8.7 %all-to-all-done.5 = bf16[16,8,512]{2,1,0:T(8,128)(2,1)S(1)} async-done(((bf16[16,8,512]{2,1,0:T(8,128)(2,1)}), bf16[16,8,512]{2,1,0:T(8,128)(2,1)S(1)}, u32[]{:S(2)}, u32[]{:S(2)}) %all-to-all-start.5) | async-done | bytes 131104 | tf_op jit(solution)/shard_map/all_to_all | solution.py:14
  134.4 0.8 fusion.1
  135.2 9.0 %all-to-all-start.6 = ((bf16[16,16,512]{2,1,0:T(8,128)(2,1)}), bf16[16,16,512]{2,1,0:T(8,128)(2,1)S(1)}, u32[]{:S(2)}, u32[]{:S(2)}) async-start(bf16[16,16,512]{2,1,0:T(8,128)(2,1)} %fusion.1), calls=%async_computation.6 | async-start | bytes 524288 | tf_op jit(solution)/shard_map/all_to_all | solution.py:14
  144.2 11.3 %all_gather.25 = bf16[32,512]{1,0:T(8,128)(2,1)S(1)} all-gather(bf16[8,512]{1,0:T(8,128)(2,1)S(1)} %multiply_convert_fusion.2), channel_id=1, replica_groups=mesh['z'=16,'yl'=2,'core'=2,'x'=4,'yh'=4] {'yh'}, dimensions={0}, use_global_device_ids=true | all-gather | bytes 40960 | tf_op jit(solution)/shard_map/all_gather | solution.py:104
  155.4 3.7 %all_gather.26 = bf16[64,512]{1,0:T(8,128)(2,1)S(1)} all-gather(bf16[32,512]{1,0:T(8,128)(2,1)S(1)} %all_gather.25), channel_id=1, replica_groups=mesh['z'=16,'yl'=2,'core'=2,'x'=4,'yh'=4] {'yl'}, dimensions={0}, use_global_device_ids=true | all-gather | bytes 98304 | tf_op jit(solution)/shard_map/all_gather | solution.py:104
  159.9 8.3 %all_to_all.43 = bf16[4,64,512]{2,1,0:T(8,128)(2,1)S(1)} all-to-all(bf16[4,64,512]{2,1,0:T(8,128)(2,1)S(1)} %broadcast_in_dim.14), channel_id=1, replica_groups=mesh['z'=16,'yl'=2,'core'=2,'x'=4,'yh'=4] {'x'}, dimensions={0} | all-to-all | bytes 524288 | tf_op jit(solution)/shard_map/all_to_all | solution.py:14
  168.2 8.2 %all_gather.27 = bf16[512,512]{1,0:T(8,128)(2,1)S(1)} all-gather(bf16[256,512]{1,0:T(8,128)(2,1)S(1)} %bitcast.45), channel_id=1, replica_groups=mesh['z'=16,'yl'=2,'core'=2,'x'=4,'yh'=4] {'core'}, dimensions={0}, use_global_device_ids=true | all-gather | bytes 786432 | tf_op jit(solution)/shard_map/all_gather | solution.py:106
  176.4 1.1 convert_element_type.109
  (31 shorter events, 4.2 us)
Async XLA Ops:
  0.6 84.6 %copy-start = (bf16[512,512]{1,0:T(8,128)(2,1)S(1)}, bf16[512,512]{1,0:T(8,128)(2,1)}, u32[]{:S(2)}) copy-start(bf16[512,512]{1,0:T(8,128)(2,1)} %param.8) | copy-start | bytes 1572868
  2.1 35.8 %all-to-all-start = ((bf16[16,16,512]{2,1,0:T(8,128)(2,1)}), bf16[16,16,512]{2,1,0:T(8,128)(2,1)S(1)}, u32[]{:S(2)}, u32[]{:S(2)}) async-start(bf16[16,16,512]{2,1,0:T(8,128)(2,1)} %broadcast_in_dim.10), calls=%async_computation | async-start | bytes 524288 | tf_op jit(solution)/shard_map/all_to_all | solution.py:14
  21.6 2.1 %copy-start.2 = (bf16[32,512]{1,0:T(8,128)(2,1)S(1)}, bf16[32,512]{1,0:T(8,128)(2,1)}, u32[]{:S(2)}) copy-start(bf16[32,512]{1,0:T(8,128)(2,1)} %param.9) | copy-start | bytes 98308
  54.5 1.2 copy-start.1
  86.5 19.4 %all-to-all-start.4 = ((bf16[16,8,512]{2,1,0:T(8,128)(2,1)}), bf16[16,8,512]{2,1,0:T(8,128)(2,1)S(1)}, u32[]{:S(2)}, u32[]{:S(2)}) async-start(bf16[16,8,512]{2,1,0:T(8,128)(2,1)} %bitcast.10), calls=%async_computation.4 | async-start | bytes 262144 | tf_op jit(solution)/shard_map/all_to_all | solution.py:14
  107.1 15.4 %collective-permute-start = (bf16[2,16,16,512]{3,2,0,1:T(8,128)(2,1)S(1)}, bf16[2,16,16,512]{3,2,0,1:T(8,128)(2,1)S(1)}, u32[]{:S(2)}, u32[]{:S(2)}) collective-permute-start(bf16[2,16,16,512]{3,2,0,1:T(8,128)(2,1)S(1)} %dynamic-slice_bitcast_fusion), channel_id=1, source_target_pairs={{0,16},{16,0},{1,17},{17,1},{2,18},{18,2},{3,19},{19,3},{4,20},{20... | collective-permute-start | bytes 1572872 | tf_op jit(solution)/shard_map/ppermute | solution.py:25
  112.2 22.1 %all-to-all-start.5 = ((bf16[16,8,512]{2,1,0:T(8,128)(2,1)}), bf16[16,8,512]{2,1,0:T(8,128)(2,1)S(1)}, u32[]{:S(2)}, u32[]{:S(2)}) async-start(bf16[16,8,512]{2,1,0:T(8,128)(2,1)} %broadcast_in_dim.13), calls=%async_computation.5 | async-start | bytes 262144 | tf_op jit(solution)/shard_map/all_to_all | solution.py:14
  122.8 11.6 %collective-permute-start.1 = (bf16[16,16,512]{2,1,0:T(8,128)(2,1)S(1)}, bf16[16,16,512]{2,1,0:T(8,128)(2,1)S(1)}, u32[]{:S(2)}, u32[]{:S(2)}) collective-permute-start(bf16[16,16,512]{2,1,0:T(8,128)(2,1)S(1)} %dynamic-slice_bitcast_fusion.1), channel_id=1, source_target_pairs={{0,32},{32,0},{1,33},{33,1},{2,34},{34,2},{3,35},{35,3},{4,36},{36... | collective-permute-start | bytes 786440 | tf_op jit(solution)/shard_map/ppermute | solution.py:25
  135.2 24.0 %all-to-all-start.6 = ((bf16[16,16,512]{2,1,0:T(8,128)(2,1)}), bf16[16,16,512]{2,1,0:T(8,128)(2,1)S(1)}, u32[]{:S(2)}, u32[]{:S(2)}) async-start(bf16[16,16,512]{2,1,0:T(8,128)(2,1)} %fusion.1), calls=%async_computation.6 | async-start | bytes 524288 | tf_op jit(solution)/shard_map/all_to_all | solution.py:14

commit v13 on v11

--- a/solution.py
+++ b/solution.py
@@ -58,21 +58,22 @@
     w = w.transpose(1, 2, 0, 3, 4).reshape(nx, slab, width)
     dpre_x = jnp.broadcast_to(dpre_x[None], (nx,) + dpre_x.shape)
     both = exchange(jnp.concatenate([dpre_x, w.astype(BF16)], axis=1), "x")
-    dpre_all = jnp.concatenate([both[i, : rows // nx] for i in range(nx)], axis=0)
+    dpre_all = both[:, : rows // nx].reshape(rows, width)
     w = both[:, rows // nx :].astype(F32).sum(0).astype(BF16)
 
     chunk = cols // n_row
     w = exchange(w.reshape(nyl * ncore, piece, width), ("yl", "core")).astype(F32).sum(0).astype(BF16)
-    w, output_x = lax.optimization_barrier((w, output_x))
+    w_sum, output_x = lax.optimization_barrier((w, output_x))
     output = lax.dynamic_slice_in_dim(output_x, at["own_row"], own, axis=0)
-    w = gather(w, "z").astype(F32).sum(0) * (rows * n_row) ** (-0.5)
-    w = w.astype(BF16)
 
     grad_in = lax.dot_general(
         dpre_all, weight, (((1,), (1,)), ((), ())), preferred_element_type=F32
     ).astype(BF16)
     partial_fg = lax.dot_general(masked, grad_in, (((0,), (0,)), ((), ())), preferred_element_type=F32)
     fg = partial_fg.astype(BF16).reshape(nz, nyl, ncore, chunk, width).transpose(2, 1, 0, 3, 4)
+    fg, w_sum = lax.optimization_barrier((fg, w_sum))
+    w = gather(w_sum, "z").astype(F32).sum(0) * (rows * n_row) ** (-0.5)
+    w = w.astype(BF16)
     fg = halve(fg, "core", at)
     fg = halve(fg, "yl", at)
     fg, w, output = lax.optimization_barrier((fg, w, output))

time: 180 us -> 178 us (0.989)
  blocking collectives: 105 us -> 98.7 us
  starting transfers between devices: 49 us -> 52.7 us
  waiting for transfers between devices: 8.42 us -> 11.7 us
    all_to_all x3 -> x4, starting transfers between devices: 39.7 us -> 48.1 us  [exchange(): return lax.all_to_all(chunks, axis, split_axis=0, concat_axis=0, tiled=True)]
    all_to_all x6 -> x5, blocking collectives: 51.9 us -> 46.4 us  [exchange(): return lax.all_to_all(chunks, axis, split_axis=0, concat_axis=0, tiled=True)]
    ppermute x2, starting transfers between devices: 9.31 us -> 4.6 us  [halve(): got = lax.ppermute(theirs, axis, [(0, 1), (1, 0)])]
    all_to_all x3 -> x4, waiting for transfers between devices: 8.42 us -> 11.7 us  [exchange(): return lax.all_to_all(chunks, axis, split_axis=0, concat_axis=0, tiled=True)]
  transfers between devices with their start and end apart: 5 -> 6, of which waited for: 1 -> 2; matrix products, arithmetic and copies ran while one was open for 2% -> 3% of each run, Pallas kernels for 0% -> 0%
where the time goes in v13:
time: 178 us; the launch traced here: 177 us
  blocking collectives  98.7 us (55%)
  starting transfers between devices  52.7 us (30%)
  waiting for transfers between devices  11.7 us (7%)
  local copies, waits for them, and re-layouts  5.71 us (3%)
  other arithmetic  4.7 us (3%)
  matrix products  2.4 us (1%)
    all_to_all x4, starting transfers between devices, exchange(): return lax.all_to_all(chunks, axis, split_axis=0, concat_axis=0, tiled=True)  48.1 us
    all_to_all x5, blocking collectives, exchange(): return lax.all_to_all(chunks, axis, split_axis=0, concat_axis=0, tiled=True)  46.4 us
    all_gather x1, blocking collectives, shards(): over_yh = lax.all_gather(over_x.astype(F32).sum(0).astype(BF16), 'yh')  15.1 us
    all_gather x2, blocking collectives, shards(): w = lax.all_gather(w, axis, axis=0, tiled=True)  15 us
    all_gather x1, blocking collectives, shards(): upstream_x = lax.all_gather(upstream, 'yh', axis=0, tiled=True)  14.3 us
    all_to_all x4, waiting for transfers between devices, exchange(): return lax.all_to_all(chunks, axis, split_axis=0, concat_axis=0, tiled=True)  11.7 us
    all_gather x1, blocking collectives, shards(): lax.all_gather(gather(w, 'x').reshape(width // ncore, width), 'core', axi...  7.96 us
    ppermute x2, starting transfers between devices, halve(): got = lax.ppermute(theirs, axis, [(0, 1), (1, 0)])  4.6 us
  transfers between devices with their start and end apart: 6, of which 2 were waited for; matrix products, arithmetic and copies ran while one was open for 3% of the time, Pallas kernels for 0%

profile of v13, /device:TPU:1, one launch (start us, length us, event | category | flops | bytes accessed | tf_op | source)
XLA Modules:
  0.0 176.7 jit_solution(17339960480408606084)
XLA Ops:
  0.7 1.5 broadcast_in_dim.16
  2.2 19.4 %all-to-all-start = ((bf16[16,16,512]{2,1,0:T(8,128)(2,1)}), bf16[16,16,512]{2,1,0:T(8,128)(2,1)S(1)}, u32[]{:S(2)}, u32[]{:S(2)}) async-start(bf16[16,16,512]{2,1,0:T(8,128)(2,1)} %broadcast_in_dim.16), calls=%async_computation | async-start | bytes 524288 | tf_op jit(solution)/shard_map/all_to_all | solution.py:12
  22.3 0.7 broadcast_in_dim.18
  23.2 1.0 copy-done.1
  25.0 14.3 %all_gather.18 = bf16[128,512]{1,0:T(8,128)(2,1)S(1)} all-gather(bf16[32,512]{1,0:T(8,128)(2,1)S(1)} %copy-done.2), channel_id=1, replica_groups=mesh['z'=16,'yl'=2,'core'=2,'x'=4,'yh'=4] {'yh'}, dimensions={0}, use_global_device_ids=true | all-gather | bytes 163840 | tf_op jit(solution)/shard_map/all_gather | solution.py:39
  39.3 7.8 %all_to_all.45 = bf16[2,16,16,512]{3,2,1,0:T(8,128)(2,1)S(1)} all-to-all(bf16[2,16,16,512]{3,2,1,0:T(8,128)(2,1)S(1)} %broadcast_in_dim.19), channel_id=1, replica_groups=mesh['z'=16,'yl'=2,'core'=2,'x'=4,'yh'=4] {'yl'}, dimensions={0} | all-to-all | bytes 1048576 | tf_op jit(solution)/shard_map/all_to_all | solution.py:12
  47.3 8.1 %all_to_all.46 = bf16[2,2,16,16,512]{4,3,1,2,0:T(8,128)(2,1)S(1)} all-to-all(bf16[2,2,16,16,512]{4,3,1,2,0:T(8,128)(2,1)S(1)} %broadcast_in_dim.20), channel_id=1, replica_groups=mesh['z'=16,'yl'=2,'core'=2,'x'=4,'yh'=4] {'core'}, dimensions={0} | all-to-all | bytes 2097152 | tf_op jit(solution)/shard_map/all_to_all | solution.py:12
  56.3 12.4 %all_to_all.47 = bf16[4,128,512]{2,1,0:T(8,128)(2,1)S(1)} all-to-all(bf16[4,128,512]{2,1,0:T(8,128)(2,1)S(1)} %bitcast.54), channel_id=1, replica_groups=mesh['z'=16,'yl'=2,'core'=2,'x'=4,'yh'=4] {'x'}, dimensions={0} | all-to-all | bytes 1048576 | tf_op jit(solution)/shard_map/all_to_all | solution.py:12
  68.8 15.1 %all-gather = bf16[512,512]{1,0:T(8,128)(2,1)S(1)} all-gather(bf16[128,512]{1,0:T(8,128)(2,1)S(1)} %reduce_sum.66), channel_id=2, replica_groups=mesh['z'=16,'yl'=2,'core'=2,'x'=4,'yh'=4] {'yh'}, dimensions={0}, use_global_device_ids=true | all-gather | bytes 655360 | tf_op jit(solution)/shard_map/all_gather | solution.py:46
  84.9 10.0 %all_to_all.48 = bf16[4,160,512]{2,1,0:T(8,128)(2,1)S(1)} all-to-all(bf16[4,160,512]{2,1,0:T(8,128)(2,1)S(1)} %pad_maximum_fusion), channel_id=1, replica_groups=mesh['z'=16,'yl'=2,'core'=2,'x'=4,'yh'=4] {'x'}, dimensions={0} | all-to-all | bytes 1310720 | tf_op jit(solution)/shard_map/all_to_all | solution.py:12
  95.5 8.7 %all-to-all-start.5 = ((bf16[4,8,512]{2,1,0:T(8,128)(2,1)}), bf16[4,8,512]{2,1,0:T(8,128)(2,1)S(1)}, u32[]{:S(2)}, u32[]{:S(2)}) async-start(bf16[4,8,512]{2,1,0:T(8,128)(2,1)} %bitcast.15), calls=%async_computation.5 | async-start | bytes 65536 | tf_op jit(solution)/shard_map/all_to_all | solution.py:12
  104.3 1.1 convolution_convert_fusion
  105.4 2.0 %all-to-all-done.5 = bf16[4,8,512]{2,1,0:T(8,128)(2,1)S(1)} async-done(((bf16[4,8,512]{2,1,0:T(8,128)(2,1)}), bf16[4,8,512]{2,1,0:T(8,128)(2,1)S(1)}, u32[]{:S(2)}, u32[]{:S(2)}) %all-to-all-start.5) | async-done | bytes 32800 | tf_op jit(solution)/shard_map/all_to_all | solution.py:12
  107.5 2.7 %collective-permute-start = (bf16[2,16,16,512]{3,2,0,1:T(8,128)(2,1)S(1)}, bf16[2,16,16,512]{3,2,0,1:T(8,128)(2,1)S(1)}, u32[]{:S(2)}, u32[]{:S(2)}) collective-permute-start(bf16[2,16,16,512]{3,2,0,1:T(8,128)(2,1)S(1)} %dynamic-slice_bitcast_fusion), channel_id=1, source_target_pairs={{0,16},{16,0},{1,17},{17,1},{2,18},{18,2},{3,19},{19,3},{4,20},{20... | collective-permute-start | bytes 1572872 | tf_op jit(solution)/shard_map/ppermute | solution.py:23
  110.9 10.9 %all-to-all-start.6 = ((bf16[16,8,512]{2,1,0:T(8,128)(2,1)}), bf16[16,8,512]{2,1,0:T(8,128)(2,1)S(1)}, u32[]{:S(2)}, u32[]{:S(2)}) async-start(bf16[16,8,512]{2,1,0:T(8,128)(2,1)} %broadcast_in_dim.22), calls=%async_computation.6 | async-start | bytes 262144 | tf_op jit(solution)/shard_map/all_to_all | solution.py:12
  122.6 1.9 %collective-permute-start.1 = (bf16[16,16,512]{2,1,0:T(8,128)(2,1)S(1)}, bf16[16,16,512]{2,1,0:T(8,128)(2,1)S(1)}, u32[]{:S(2)}, u32[]{:S(2)}) collective-permute-start(bf16[16,16,512]{2,1,0:T(8,128)(2,1)S(1)} %dynamic-slice_bitcast_fusion.1), channel_id=1, source_target_pairs={{0,32},{32,0},{1,33},{33,1},{2,34},{34,2},{3,35},{35,3},{4,36},{36... | collective-permute-start | bytes 786440 | tf_op jit(solution)/shard_map/ppermute | solution.py:23
  124.6 9.6 %all-to-all-done.6 = bf16[16,8,512]{2,1,0:T(8,128)(2,1)S(1)} async-done(((bf16[16,8,512]{2,1,0:T(8,128)(2,1)}), bf16[16,8,512]{2,1,0:T(8,128)(2,1)S(1)}, u32[]{:S(2)}, u32[]{:S(2)}) %all-to-all-start.6) | async-done | bytes 131104 | tf_op jit(solution)/shard_map/all_to_all | solution.py:12
  134.3 0.8 fusion.1
  135.1 9.0 %all-to-all-start.7 = ((bf16[16,16,512]{2,1,0:T(8,128)(2,1)}), bf16[16,16,512]{2,1,0:T(8,128)(2,1)S(1)}, u32[]{:S(2)}, u32[]{:S(2)}) async-start(bf16[16,16,512]{2,1,0:T(8,128)(2,1)} %fusion.1), calls=%async_computation.7 | async-start | bytes 524288 | tf_op jit(solution)/shard_map/all_to_all | solution.py:12
  144.1 11.3 %all_gather.21 = bf16[32,512]{1,0:T(8,128)(2,1)S(1)} all-gather(bf16[8,512]{1,0:T(8,128)(2,1)S(1)} %multiply_convert_fusion.2), channel_id=1, replica_groups=mesh['z'=16,'yl'=2,'core'=2,'x'=4,'yh'=4] {'yh'}, dimensions={0}, use_global_device_ids=true | all-gather | bytes 40960 | tf_op jit(solution)/shard_map/all_gather | solution.py:83
  155.3 3.7 %all_gather.22 = bf16[64,512]{1,0:T(8,128)(2,1)S(1)} all-gather(bf16[32,512]{1,0:T(8,128)(2,1)S(1)} %all_gather.21), channel_id=1, replica_groups=mesh['z'=16,'yl'=2,'core'=2,'x'=4,'yh'=4] {'yl'}, dimensions={0}, use_global_device_ids=true | all-gather | bytes 98304 | tf_op jit(solution)/shard_map/all_gather | solution.py:83
  159.7 7.9 %all_to_all.49 = bf16[4,64,512]{2,1,0:T(8,128)(2,1)S(1)} all-to-all(bf16[4,64,512]{2,1,0:T(8,128)(2,1)S(1)} %broadcast_in_dim.23), channel_id=1, replica_groups=mesh['z'=16,'yl'=2,'core'=2,'x'=4,'yh'=4] {'x'}, dimensions={0} | all-to-all | bytes 524288 | tf_op jit(solution)/shard_map/all_to_all | solution.py:12
  167.7 8.0 %all_gather.23 = bf16[512,512]{1,0:T(8,128)(2,1)S(1)} all-gather(bf16[256,512]{1,0:T(8,128)(2,1)S(1)} %bitcast.47), channel_id=1, replica_groups=mesh['z'=16,'yl'=2,'core'=2,'x'=4,'yh'=4] {'core'}, dimensions={0}, use_global_device_ids=true | all-gather | bytes 786432 | tf_op jit(solution)/shard_map/all_gather | solution.py:85
  175.6 1.1 convert_element_type.121
  (39 shorter events, 6.6 us)
Async XLA Ops:
  0.6 83.5 %copy-start = (bf16[512,512]{1,0:T(8,128)(2,1)S(1)}, bf16[512,512]{1,0:T(8,128)(2,1)}, u32[]{:S(2)}) copy-start(bf16[512,512]{1,0:T(8,128)(2,1)} %param.8) | copy-start | bytes 1572868
  2.2 37.1 %all-to-all-start = ((bf16[16,16,512]{2,1,0:T(8,128)(2,1)}), bf16[16,16,512]{2,1,0:T(8,128)(2,1)S(1)}, u32[]{:S(2)}, u32[]{:S(2)}) async-start(bf16[16,16,512]{2,1,0:T(8,128)(2,1)} %broadcast_in_dim.16), calls=%async_computation | async-start | bytes 524288 | tf_op jit(solution)/shard_map/all_to_all | solution.py:12
  23.0 1.2 copy-start.1
  24.2 0.8 copy-start.2
  95.5 11.9 %all-to-all-start.5 = ((bf16[4,8,512]{2,1,0:T(8,128)(2,1)}), bf16[4,8,512]{2,1,0:T(8,128)(2,1)S(1)}, u32[]{:S(2)}, u32[]{:S(2)}) async-start(bf16[4,8,512]{2,1,0:T(8,128)(2,1)} %bitcast.15), calls=%async_computation.5 | async-start | bytes 65536 | tf_op jit(solution)/shard_map/all_to_all | solution.py:12
  107.5 14.9 %collective-permute-start = (bf16[2,16,16,512]{3,2,0,1:T(8,128)(2,1)S(1)}, bf16[2,16,16,512]{3,2,0,1:T(8,128)(2,1)S(1)}, u32[]{:S(2)}, u32[]{:S(2)}) collective-permute-start(bf16[2,16,16,512]{3,2,0,1:T(8,128)(2,1)S(1)} %dynamic-slice_bitcast_fusion), channel_id=1, source_target_pairs={{0,16},{16,0},{1,17},{17,1},{2,18},{18,2},{3,19},{19,3},{4,20},{20... | collective-permute-start | bytes 1572872 | tf_op jit(solution)/shard_map/ppermute | solution.py:23
  110.9 23.4 %all-to-all-start.6 = ((bf16[16,8,512]{2,1,0:T(8,128)(2,1)}), bf16[16,8,512]{2,1,0:T(8,128)(2,1)S(1)}, u32[]{:S(2)}, u32[]{:S(2)}) async-start(bf16[16,8,512]{2,1,0:T(8,128)(2,1)} %broadcast_in_dim.22), calls=%async_computation.6 | async-start | bytes 262144 | tf_op jit(solution)/shard_map/all_to_all | solution.py:12
  122.6 11.6 %collective-permute-start.1 = (bf16[16,16,512]{2,1,0:T(8,128)(2,1)S(1)}, bf16[16,16,512]{2,1,0:T(8,128)(2,1)S(1)}, u32[]{:S(2)}, u32[]{:S(2)}) collective-permute-start(bf16[16,16,512]{2,1,0:T(8,128)(2,1)S(1)} %dynamic-slice_bitcast_fusion.1), channel_id=1, source_target_pairs={{0,32},{32,0},{1,33},{33,1},{2,34},{34,2},{3,35},{35,3},{4,36},{36... | collective-permute-start | bytes 786440 | tf_op jit(solution)/shard_map/ppermute | solution.py:23
  135.1 24.0 %all-to-all-start.7 = ((bf16[16,16,512]{2,1,0:T(8,128)(2,1)}), bf16[16,16,512]{2,1,0:T(8,128)(2,1)S(1)}, u32[]{:S(2)}, u32[]{:S(2)}) async-start(bf16[16,16,512]{2,1,0:T(8,128)(2,1)} %fusion.1), calls=%async_computation.7 | async-start | bytes 524288 | tf_op jit(solution)/shard_map/all_to_all | solution.py:12

commit v14 on v13

--- a/solution.py
+++ b/solution.py
@@ -37,7 +37,7 @@
     by_z = gather(features, "z")
     masked = adjacency * jnp.repeat(jnp.repeat(block_mask, TILE, 0), TILE, 1).astype(BF16)
     upstream_x = lax.all_gather(upstream, "yh", axis=0, tiled=True)
-    by_z, masked, upstream_x = lax.optimization_barrier((by_z, masked, upstream_x))
+    by_z, upstream_x = lax.optimization_barrier((by_z, upstream_x))
     panel = gather(gather(by_z, "yl"), "core")
     panel = panel.transpose(2, 1, 0, 3, 4).reshape(cols, width)
 

time: 178 us -> 176 us (0.989)
  blocking collectives: 98.7 us -> 94.3 us
  waiting for transfers between devices: 11.7 us -> 14.7 us
    all_to_all x5 -> x4, blocking collectives: 46.4 us -> 40.8 us  [exchange(): return lax.all_to_all(chunks, axis, split_axis=0, concat_axis=0, tiled=True)]
    all_to_all x4 -> x5, waiting for transfers between devices: 11.7 us -> 14.7 us  [exchange(): return lax.all_to_all(chunks, axis, split_axis=0, concat_axis=0, tiled=True)]
    all_to_all x4 -> x5, starting transfers between devices: 48.1 us -> 48.3 us  [exchange(): return lax.all_to_all(chunks, axis, split_axis=0, concat_axis=0, tiled=True)]
  transfers between devices with their start and end apart: 6 -> 7, of which waited for: 2 -> 3; matrix products, arithmetic and copies ran while one was open for 3% -> 2% of each run, Pallas kernels for 0% -> 0%
where the time goes in v14:
time: 176 us; the launch traced here: 175 us
  blocking collectives  94.3 us (54%)
  starting transfers between devices  52.9 us (30%)
  waiting for transfers between devices  14.7 us (8%)
  local copies, waits for them, and re-layouts  6.16 us (4%)
  other arithmetic  4.02 us (2%)
  matrix products  2.39 us (1%)
    all_to_all x5, starting transfers between devices, exchange(): return lax.all_to_all(chunks, axis, split_axis=0, concat_axis=0, tiled=True)  48.3 us
    all_to_all x4, blocking collectives, exchange(): return lax.all_to_all(chunks, axis, split_axis=0, concat_axis=0, tiled=True)  40.8 us
    all_gather x1, blocking collectives, shards(): over_yh = lax.all_gather(over_x.astype(F32).sum(0).astype(BF16), 'yh')  16.3 us
    all_gather x2, blocking collectives, shards(): w = lax.all_gather(w, axis, axis=0, tiled=True)  14.8 us
    all_to_all x5, waiting for transfers between devices, exchange(): return lax.all_to_all(chunks, axis, split_axis=0, concat_axis=0, tiled=True)  14.7 us
    all_gather x1, blocking collectives, shards(): upstream_x = lax.all_gather(upstream, 'yh', axis=0, tiled=True)  14.2 us
    all_gather x1, blocking collectives, shards(): lax.all_gather(gather(w, 'x').reshape(width // ncore, width), 'core', axi...  8.13 us
    ppermute x2, starting transfers between devices, halve(): got = lax.ppermute(theirs, axis, [(0, 1), (1, 0)])  4.6 us
  transfers between devices with their start and end apart: 7, of which 3 were waited for; matrix products, arithmetic and copies ran while one was open for 2% of the time, Pallas kernels for 0%

profile of v14, /device:TPU:1, one launch (start us, length us, event | category | flops | bytes accessed | tf_op | source)
XLA Modules:
  0.0 175.4 jit_solution(2152338976216403384)
XLA Ops:
  0.7 1.5 broadcast_in_dim.18
  2.2 19.4 %all-to-all-start = ((bf16[16,16,512]{2,1,0:T(8,128)(2,1)}), bf16[16,16,512]{2,1,0:T(8,128)(2,1)S(1)}, u32[]{:S(2)}, u32[]{:S(2)}) async-start(bf16[16,16,512]{2,1,0:T(8,128)(2,1)} %broadcast_in_dim.18), calls=%async_computation | async-start | bytes 524288 | tf_op jit(solution)/shard_map/all_to_all | solution.py:12
  21.6 14.2 %all_gather.18 = bf16[128,512]{1,0:T(8,128)(2,1)S(1)} all-gather(bf16[32,512]{1,0:T(8,128)(2,1)} %param.9), channel_id=1, replica_groups=mesh['z'=16,'yl'=2,'core'=2,'x'=4,'yh'=4] {'yh'}, dimensions={0}, use_global_device_ids=true | all-gather | bytes 163840 | tf_op jit(solution)/shard_map/all_gather | solution.py:39
  35.8 0.9 broadcast_in_dim.19
  36.6 3.5 %all-to-all-start.1 = ((bf16[2,16,16,512]{3,2,1,0:T(8,128)(2,1)}), bf16[2,16,16,512]{3,2,1,0:T(8,128)(2,1)S(1)}, u32[]{:S(2)}, u32[]{:S(2)}) async-start(bf16[2,16,16,512]{3,2,1,0:T(8,128)(2,1)} %broadcast_in_dim.19), calls=%async_computation.1 | async-start | bytes 1048576 | tf_op jit(solution)/shard_map/all_to_all | solution.py:12
  41.1 1.0 copy-done.1
  42.5 3.0 %all-to-all-done.1 = bf16[2,16,16,512]{3,2,1,0:T(8,128)(2,1)S(1)} async-done(((bf16[2,16,16,512]{3,2,1,0:T(8,128)(2,1)}), bf16[2,16,16,512]{3,2,1,0:T(8,128)(2,1)S(1)}, u32[]{:S(2)}, u32[]{:S(2)}) %all-to-all-start.1) | async-done | bytes 524320 | tf_op jit(solution)/shard_map/all_to_all | solution.py:12
  45.7 10.5 %all_to_all.45 = bf16[2,2,16,16,512]{4,3,1,2,0:T(8,128)(2,1)S(1)} all-to-all(bf16[2,2,16,16,512]{4,3,1,2,0:T(8,128)(2,1)S(1)} %broadcast_in_dim.20), channel_id=1, replica_groups=mesh['z'=16,'yl'=2,'core'=2,'x'=4,'yh'=4] {'core'}, dimensions={0} | all-to-all | bytes 2097152 | tf_op jit(solution)/shard_map/all_to_all | solution.py:12
  57.0 12.4 %all_to_all.46 = bf16[4,128,512]{2,1,0:T(8,128)(2,1)S(1)} all-to-all(bf16[4,128,512]{2,1,0:T(8,128)(2,1)S(1)} %bitcast.54), channel_id=1, replica_groups=mesh['z'=16,'yl'=2,'core'=2,'x'=4,'yh'=4] {'x'}, dimensions={0} | all-to-all | bytes 1048576 | tf_op jit(solution)/shard_map/all_to_all | solution.py:12
  69.5 16.3 %all-gather = bf16[512,512]{1,0:T(8,128)(2,1)S(1)} all-gather(bf16[128,512]{1,0:T(8,128)(2,1)S(1)} %reduce_sum.66), channel_id=2, replica_groups=mesh['z'=16,'yl'=2,'core'=2,'x'=4,'yh'=4] {'yh'}, dimensions={0}, use_global_device_ids=true | all-gather | bytes 655360 | tf_op jit(solution)/shard_map/all_gather | solution.py:46
  86.8 10.0 %all_to_all.47 = bf16[4,160,512]{2,1,0:T(8,128)(2,1)S(1)} all-to-all(bf16[4,160,512]{2,1,0:T(8,128)(2,1)S(1)} %pad_maximum_fusion), channel_id=1, replica_groups=mesh['z'=16,'yl'=2,'core'=2,'x'=4,'yh'=4] {'x'}, dimensions={0} | all-to-all | bytes 1310720 | tf_op jit(solution)/shard_map/all_to_all | solution.py:12
  97.5 8.7 %all-to-all-start.5 = ((bf16[4,8,512]{2,1,0:T(8,128)(2,1)}), bf16[4,8,512]{2,1,0:T(8,128)(2,1)S(1)}, u32[]{:S(2)}, u32[]{:S(2)}) async-start(bf16[4,8,512]{2,1,0:T(8,128)(2,1)} %bitcast.15), calls=%async_computation.5 | async-start | bytes 65536 | tf_op jit(solution)/shard_map/all_to_all | solution.py:12
  106.2 1.1 convolution_convert_fusion
  107.3 2.0 %all-to-all-done.5 = bf16[4,8,512]{2,1,0:T(8,128)(2,1)S(1)} async-done(((bf16[4,8,512]{2,1,0:T(8,128)(2,1)}), bf16[4,8,512]{2,1,0:T(8,128)(2,1)S(1)}, u32[]{:S(2)}, u32[]{:S(2)}) %all-to-all-start.5) | async-done | bytes 32800 | tf_op jit(solution)/shard_map/all_to_all | solution.py:12
  109.4 2.7 %collective-permute-start = (bf16[2,16,16,512]{3,2,0,1:T(8,128)(2,1)S(1)}, bf16[2,16,16,512]{3,2,0,1:T(8,128)(2,1)S(1)}, u32[]{:S(2)}, u32[]{:S(2)}) collective-permute-start(bf16[2,16,16,512]{3,2,0,1:T(8,128)(2,1)S(1)} %dynamic-slice_bitcast_fusion), channel_id=1, source_target_pairs={{0,16},{16,0},{1,17},{17,1},{2,18},{18,2},{3,19},{19,3},{4,20},{20... | collective-permute-start | bytes 1572872 | tf_op jit(solution)/shard_map/ppermute | solution.py:23
  112.7 7.7 %all-to-all-start.6 = ((bf16[16,8,512]{2,1,0:T(8,128)(2,1)}), bf16[16,8,512]{2,1,0:T(8,128)(2,1)S(1)}, u32[]{:S(2)}, u32[]{:S(2)}) async-start(bf16[16,8,512]{2,1,0:T(8,128)(2,1)} %broadcast_in_dim.22), calls=%async_computation.6 | async-start | bytes 262144 | tf_op jit(solution)/shard_map/all_to_all | solution.py:12
  121.3 1.9 %collective-permute-start.1 = (bf16[16,16,512]{2,1,0:T(8,128)(2,1)S(1)}, bf16[16,16,512]{2,1,0:T(8,128)(2,1)S(1)}, u32[]{:S(2)}, u32[]{:S(2)}) collective-permute-start(bf16[16,16,512]{2,1,0:T(8,128)(2,1)S(1)} %dynamic-slice_bitcast_fusion.1), channel_id=1, source_target_pairs={{0,32},{32,0},{1,33},{33,1},{2,34},{34,2},{3,35},{35,3},{4,36},{36... | collective-permute-start | bytes 786440 | tf_op jit(solution)/shard_map/ppermute | solution.py:23
  123.3 9.6 %all-to-all-done.6 = bf16[16,8,512]{2,1,0:T(8,128)(2,1)S(1)} async-done(((bf16[16,8,512]{2,1,0:T(8,128)(2,1)}), bf16[16,8,512]{2,1,0:T(8,128)(2,1)S(1)}, u32[]{:S(2)}, u32[]{:S(2)}) %all-to-all-start.6) | async-done | bytes 131104 | tf_op jit(solution)/shard_map/all_to_all | solution.py:12
  133.8 9.0 %all-to-all-start.7 = ((bf16[16,16,512]{2,1,0:T(8,128)(2,1)}), bf16[16,16,512]{2,1,0:T(8,128)(2,1)S(1)}, u32[]{:S(2)}, u32[]{:S(2)}) async-start(bf16[16,16,512]{2,1,0:T(8,128)(2,1)} %fusion.1), calls=%async_computation.7 | async-start | bytes 524288 | tf_op jit(solution)/shard_map/all_to_all | solution.py:12
  142.8 11.1 %all_gather.21 = bf16[32,512]{1,0:T(8,128)(2,1)S(1)} all-gather(bf16[8,512]{1,0:T(8,128)(2,1)S(1)} %multiply_convert_fusion.2), channel_id=1, replica_groups=mesh['z'=16,'yl'=2,'core'=2,'x'=4,'yh'=4] {'yh'}, dimensions={0}, use_global_device_ids=true | all-gather | bytes 40960 | tf_op jit(solution)/shard_map/all_gather | solution.py:83
  153.9 3.7 %all_gather.22 = bf16[64,512]{1,0:T(8,128)(2,1)S(1)} all-gather(bf16[32,512]{1,0:T(8,128)(2,1)S(1)} %all_gather.21), channel_id=1, replica_groups=mesh['z'=16,'yl'=2,'core'=2,'x'=4,'yh'=4] {'yl'}, dimensions={0}, use_global_device_ids=true | all-gather | bytes 98304 | tf_op jit(solution)/shard_map/all_gather | solution.py:83
  158.3 7.9 %all_to_all.48 = bf16[4,64,512]{2,1,0:T(8,128)(2,1)S(1)} all-to-all(bf16[4,64,512]{2,1,0:T(8,128)(2,1)S(1)} %broadcast_in_dim.23), channel_id=1, replica_groups=mesh['z'=16,'yl'=2,'core'=2,'x'=4,'yh'=4] {'x'}, dimensions={0} | all-to-all | bytes 524288 | tf_op jit(solution)/shard_map/all_to_all | solution.py:12
  166.2 8.1 %all_gather.23 = bf16[512,512]{1,0:T(8,128)(2,1)S(1)} all-gather(bf16[256,512]{1,0:T(8,128)(2,1)S(1)} %bitcast.47), channel_id=1, replica_groups=mesh['z'=16,'yl'=2,'core'=2,'x'=4,'yh'=4] {'core'}, dimensions={0}, use_global_device_ids=true | all-gather | bytes 786432 | tf_op jit(solution)/shard_map/all_gather | solution.py:85
  174.3 1.1 convert_element_type.121
  (40 shorter events, 7.1 us)
Async XLA Ops:
  0.6 85.4 %copy-start = (bf16[512,512]{1,0:T(8,128)(2,1)S(1)}, bf16[512,512]{1,0:T(8,128)(2,1)}, u32[]{:S(2)}) copy-start(bf16[512,512]{1,0:T(8,128)(2,1)} %param.8) | copy-start | bytes 1572868
  2.2 33.6 %all-to-all-start = ((bf16[16,16,512]{2,1,0:T(8,128)(2,1)}), bf16[16,16,512]{2,1,0:T(8,128)(2,1)S(1)}, u32[]{:S(2)}, u32[]{:S(2)}) async-start(bf16[16,16,512]{2,1,0:T(8,128)(2,1)} %broadcast_in_dim.18), calls=%async_computation | async-start | bytes 524288 | tf_op jit(solution)/shard_map/all_to_all | solution.py:12
  21.6 18.6 %copy-start.2 = (s32[2,4]{1,0:T(2,128)S(1)}, s32[2,4]{1,0:T(2,128)}, u32[]{:S(2)}) copy-start(s32[2,4]{1,0:T(2,128)} %param.6) | copy-start | bytes 100
  36.6 8.9 %all-to-all-start.1 = ((bf16[2,16,16,512]{3,2,1,0:T(8,128)(2,1)}), bf16[2,16,16,512]{3,2,1,0:T(8,128)(2,1)S(1)}, u32[]{:S(2)}, u32[]{:S(2)}) async-start(bf16[2,16,16,512]{3,2,1,0:T(8,128)(2,1)} %broadcast_in_dim.19), calls=%async_computation.1 | async-start | bytes 1048576 | tf_op jit(solution)/shard_map/all_to_all | solution.py:12
  40.9 1.2 copy-start.1
  97.5 11.8 %all-to-all-start.5 = ((bf16[4,8,512]{2,1,0:T(8,128)(2,1)}), bf16[4,8,512]{2,1,0:T(8,128)(2,1)S(1)}, u32[]{:S(2)}, u32[]{:S(2)}) async-start(bf16[4,8,512]{2,1,0:T(8,128)(2,1)} %bitcast.15), calls=%async_computation.5 | async-start | bytes 65536 | tf_op jit(solution)/shard_map/all_to_all | solution.py:12
  109.4 11.7 %collective-permute-start = (bf16[2,16,16,512]{3,2,0,1:T(8,128)(2,1)S(1)}, bf16[2,16,16,512]{3,2,0,1:T(8,128)(2,1)S(1)}, u32[]{:S(2)}, u32[]{:S(2)}) collective-permute-start(bf16[2,16,16,512]{3,2,0,1:T(8,128)(2,1)S(1)} %dynamic-slice_bitcast_fusion), channel_id=1, source_target_pairs={{0,16},{16,0},{1,17},{17,1},{2,18},{18,2},{3,19},{19,3},{4,20},{20... | collective-permute-start | bytes 1572872 | tf_op jit(solution)/shard_map/ppermute | solution.py:23
  112.7 20.2 %all-to-all-start.6 = ((bf16[16,8,512]{2,1,0:T(8,128)(2,1)}), bf16[16,8,512]{2,1,0:T(8,128)(2,1)S(1)}, u32[]{:S(2)}, u32[]{:S(2)}) async-start(bf16[16,8,512]{2,1,0:T(8,128)(2,1)} %broadcast_in_dim.22), calls=%async_computation.6 | async-start | bytes 262144 | tf_op jit(solution)/shard_map/all_to_all | solution.py:12
  121.3 11.6 %collective-permute-start.1 = (bf16[16,16,512]{2,1,0:T(8,128)(2,1)S(1)}, bf16[16,16,512]{2,1,0:T(8,128)(2,1)S(1)}, u32[]{:S(2)}, u32[]{:S(2)}) collective-permute-start(bf16[16,16,512]{2,1,0:T(8,128)(2,1)S(1)} %dynamic-slice_bitcast_fusion.1), channel_id=1, source_target_pairs={{0,32},{32,0},{1,33},{33,1},{2,34},{34,2},{3,35},{35,3},{4,36},{36... | collective-permute-start | bytes 786440 | tf_op jit(solution)/shard_map/ppermute | solution.py:23
  133.8 23.8 %all-to-all-start.7 = ((bf16[16,16,512]{2,1,0:T(8,128)(2,1)}), bf16[16,16,512]{2,1,0:T(8,128)(2,1)S(1)}, u32[]{:S(2)}, u32[]{:S(2)}) async-start(bf16[16,16,512]{2,1,0:T(8,128)(2,1)} %fusion.1), calls=%async_computation.7 | async-start | bytes 524288 | tf_op jit(solution)/shard_map/all_to_all | solution.py:12
